TPU v7x, 256 devices: a whole 4x4x8 slice. The times are simulated.
256 devices in a mesh: grp: 8 (over y, core), brick: 32 (over x, z).
Axes of the slice: x: 4, y: 4, z: 8, core: 2. Of those that a mesh axis runs over, the one named last changes fastest.
Arguments:
- right_side: float32 [3, 128, 512, 128], P(None, 'grp', 'brick'), may hold values from -24 to 24
- stiffness: float32 [128, 512, 128], P('grp', 'brick'), may hold values from 1 to 10
- reaction: float32 [128, 512, 128], P('grp', 'brick'), may hold values from 0.1 to 1
Outputs:
- correction: float32 [3, 128, 512, 128], P(None, 'grp', 'brick')
All inputs are finite; a program needn't handle non-finite values.
Results may differ from a plain program's by a relative error of at most 0.00025.
Values sent between devices are 32-bit elements; how exact they have to be, the bound alone decides.
No kernel may reach another device: no remote copies, remote signals or barrier semaphores. Data moves between devices by JAX's collectives and lax.ppermute only.
A program may use at most 128 MiB of HBM per device.

v0:
```python
import jax
import jax.numpy as jnp
from jax import lax
from jax.sharding import PartitionSpec as P

LEVELS = 4


BETA = 1.0
THETA = 1.5
DELTA = 1.0
SIGMA = 1.5


def with_halo(cells, sides, width):
    for axis, dim in sides:
        count = lax.axis_size(axis)
        ends = count - 1
        head = lax.slice_in_dim(cells, 0, width, axis=dim)
        tail = lax.slice_in_dim(cells, cells.shape[dim] - width, cells.shape[dim], axis=dim)
        cells = jnp.concatenate(
            [
                lax.ppermute(tail, axis, [(i, (i + 1) % count) for i in range(ends)]),
                cells,
                lax.ppermute(head, axis, [((i + 1) % count, i) for i in range(ends)]),
            ],
            axis=dim,
        )
    return cells


def rate_list():
    rates = [1.0 / SIGMA]
    for number in range(3):
        rates.append(1.0 / (2.0 * SIGMA - rates[-1]))
    return rates


def advance(step, old, resid, inverse):
    rates = rate_list()
    return rates[step] * rates[step - 1] * old + 2.0 * rates[step] / DELTA * (inverse * resid)


def offset_of(axis, sign):
    return tuple((sign if index == axis else 0 for index in range(3)))


def view(array, shift, rows, cols, depth):
    return array[
        ...,
        1 + shift[0] : 1 + shift[0] + rows,
        1 + shift[1] : 1 + shift[1] + cols,
        1 + shift[2] : 1 + shift[2] + depth,
    ]


def face_total(stiff, rows, cols, depth):
    centre = view(stiff, (0, 0, 0), rows, cols, depth)
    total = jnp.zeros_like(centre)
    for axis in range(3):
        total = total + 0.5 * (centre + view(stiff, offset_of(axis, 1), rows, cols, depth))
        total = total + 0.5 * (centre + view(stiff, offset_of(axis, -1), rows, cols, depth))
    return total


def inverse_diagonal(coeff, scale):
    rows = coeff.shape[1] - 2
    cols = coeff.shape[2] - 2
    depth = coeff.shape[3]
    stiff = jnp.pad(coeff[0], ((0, 0), (0, 0), (1, 1)))
    react = coeff[1, 1:-1, 1:-1, :]
    faces = face_total(stiff, rows, cols, depth)
    return (1.0 / (scale * (faces + 2.0 * BETA) + react))[None]


def operate(field, coeff, scale):
    rows = field.shape[1] - 2
    cols = field.shape[2] - 2
    depth = field.shape[3]
    padded = jnp.pad(field, ((0, 0), (0, 0), (0, 0), (1, 1)))
    stiff = jnp.pad(coeff[0], ((0, 0), (0, 0), (1, 1)))
    react = coeff[1, 1:-1, 1:-1, :]
    centre = view(stiff, (0, 0, 0), rows, cols, depth)
    middle = view(padded, (0, 0, 0), rows, cols, depth)
    laplace = jnp.zeros_like(middle)
    for axis in range(3):
        ahead = offset_of(axis, 1)
        behind = offset_of(axis, -1)
        upper = 0.5 * (centre + view(stiff, ahead, rows, cols, depth))
        lower = 0.5 * (centre + view(stiff, behind, rows, cols, depth))
        laplace = laplace + upper * (middle - view(padded, ahead, rows, cols, depth))
        laplace = laplace + lower * (middle - view(padded, behind, rows, cols, depth))

    def divergence(anchor):
        total = jnp.zeros_like(centre)
        for axis in range(3):
            moved = tuple((anchor[index] + offset_of(axis, 1)[index] for index in range(3)))
            total = (
                total
                + view(padded[axis], moved, rows, cols, depth)
                - view(padded[axis], anchor, rows, cols, depth)
            )
        return total

    centre_div = divergence((0, 0, 0))
    parts = []
    for axis in range(3):
        graddiv = divergence(offset_of(axis, -1)) - centre_div
        parts.append(scale * (laplace[axis] + BETA * graddiv) + react * middle[axis])
    return jnp.stack(parts)


def shrink(array):
    comps, rows, cols, depth = array.shape
    blocks = array.reshape(comps, rows // 2, 2, cols // 2, 2, depth // 2, 2)
    return blocks.mean(axis=(2, 4, 6))


def grow(array):
    return jnp.repeat(jnp.repeat(jnp.repeat(array, 2, axis=1), 2, axis=2), 2, axis=3)


def crop(array, have, want):
    margin = have - want
    return array[:, margin:-margin, margin:-margin, :]


def spread(array, width):
    return with_halo(array, (("grp", 1), ("brick", 2)), width)


def relax_plain(source, start, context):
    padded, inverse, scale, group = context
    near_coeff = crop(padded, 2, 1)
    inner_inverse = crop(inverse, 1, 0)
    if start is None:
        resid = source
        state = jnp.zeros_like(source)
    else:
        resid = source - operate(spread(start, 1), near_coeff, scale)
        state = start
    step_dir = inner_inverse * resid / THETA
    for step in range(1, 4):
        state = state + step_dir
        resid = source - operate(spread(state, 1), near_coeff, scale)
        step_dir = advance(step, step_dir, resid, inner_inverse)
    return state + step_dir


def relax(source, start, context):
    return relax_plain(source, start, context)


def on_device(right_side, stiffness, reaction):
    coeff = jnp.stack([stiffness, reaction])
    contexts = []
    group = 1
    for level in range(LEVELS):
        scale = 0.25**level
        if level > 0:
            coeff = shrink(coeff)
        padded = spread(coeff, 2)
        contexts.append((padded, inverse_diagonal(padded, scale), scale, group))
    sources = [right_side]
    saved = []
    source_rims = []
    answer = right_side
    for level in range(LEVELS):
        source = sources[level]
        padded, inverse, scale, group = contexts[level]
        source_rims.append(source)
        smooth = relax(source, None, contexts[level])
        if level < LEVELS - 1:
            saved.append(smooth)
            resid = source - operate(spread(smooth, 1), crop(padded, 2, 1), scale)
            coarse = shrink(resid)
            sources.append(coarse)
        else:
            answer = smooth
    for level in reversed(range(LEVELS - 1)):
        answer = relax(sources[level], saved[level] + grow(answer), contexts[level])
    return answer


def solution(mesh):
    in_specs = (P(None, "grp", "brick", None), P("grp", "brick", None), P("grp", "brick", None))
    out_specs = P(None, "grp", "brick", None)
    return jax.shard_map(
        on_device, mesh=mesh, in_specs=in_specs, out_specs=out_specs, check_vma=False
    )
```

profile of v0, /device:TPU:22, one launch (start us, length us, event | category | flops | bytes accessed | tf_op | source)
XLA Modules:
  0.0 628.7 jit_solution(916062821650698863)
XLA Ops:
  0.0 10.5 %stack.359 = f32[1,8,2,8,2,64,2]{6,5,4,3,2,1,0:T(8,128)} reshape(f32[16,16,128]{2,1,0:T(8,128)} %param.5) | data formatting | bytes 262144 | tf_op jit(solution)/shard_map/stack | solution.py:155
  10.5 9.7 %stack.358 = f32[1,8,2,8,2,64,2]{6,5,4,3,2,1,0:T(8,128)} reshape(f32[16,16,128]{2,1,0:T(8,128)S(1)} %copy-done.2) | data formatting | bytes 262144 | tf_op jit(solution)/shard_map/stack | solution.py:155
  20.3 7.5 %maximum_reduce_fusion = f32[2,8,8,64]{3,2,1,0:T(8,128)S(1)} fusion(f32[1,8,2,8,2,64,2]{6,5,4,3,2,1,0:T(8,128)} %stack.359, f32[1,8,2,8,2,64,2]{6,5,4,3,2,1,0:T(8,128)} %stack.358), kind=kLoop, calls=%fused_computation | loop fusion | flops 122880 | bytes 294912 | tf_op jit(solution)/shard_map/reduce_sum | solution.py:116
  51.0 8.0 %collective-permute-start.3 = (f32[2,20,2,128]{3,2,1,0:T(2,128)S(1)}, f32[2,20,2,128]{3,2,1,0:T(2,128)S(1)}, u32[]{:S(2)}, u32[]{:S(2)}) collective-permute-start(f32[2,20,2,128]{3,2,1,0:T(2,128)S(1)} %get-tuple-element.156), channel_id=1, source_target_pairs={{1,0},{2,1},{3,2},{4,3},{5,4},{6,5},{7,6},{8,7},{9,8},{10,9},{11,1... | collective-permute-start | bytes 122888 | tf_op jit(solution)/shard_map/ppermute | solution.py:25
  61.0 6.3 %collective-permute-done.2 = f32[2,20,2,128]{3,2,1,0:T(2,128)S(1)} collective-permute-done((f32[2,20,2,128]{3,2,1,0:T(2,128)S(1)}, f32[2,20,2,128]{3,2,1,0:T(2,128)S(1)}, u32[]{:S(2)}, u32[]{:S(2)}) %collective-permute-start.2) | collective-permute-done | bytes 40992 | tf_op jit(solution)/shard_map/ppermute | solution.py:23
  77.7 3.9 collective-permute-start.7
  98.0 5.5 collective-permute-start.10
  105.8 5.7 collective-permute-done.11
  123.0 3.9 collective-permute-start.15
  142.2 3.9 collective-permute-start.19
  146.2 3.9 collective-permute-done.19
  152.1 26.5 %reshape.145 = f32[3,8,2,8,2,64,2]{6,5,4,3,2,1,0:T(8,128)} reshape(f32[3,16,16,128]{3,2,1,0:T(8,128)S(1)} %maximum_subtract_fusion.4) | data formatting | bytes 786432 | tf_op jit(solution)/shard_map/reshape | solution.py:115
  178.6 9.4 %reduce_sum.54 = f32[3,8,8,64]{3,2,1,0:T(8,128)S(1)} reduce(f32[3,8,2,8,2,64,2]{6,5,4,3,2,1,0:T(8,128)} %reshape.145, f32[]{:T(128)} %constant.22.clone.1), dimensions={2,4,6}, to_apply=%region_0.1 | reduce | flops 86016 | bytes 442372 | tf_op jit(solution)/shard_map/reduce_sum | solution.py:116
  197.0 3.9 collective-permute-start.27
  211.8 3.9 collective-permute-start.42
  215.8 4.0 collective-permute-start.30
  221.8 5.7 collective-permute-done.31
  237.2 3.9 collective-permute-start.35
  254.7 3.9 collective-permute-start.39
  258.7 4.9 div.102
  282.3 4.0 collective-permute-start.46
  289.0 5.0 collective-permute-done.47
  301.5 3.9 collective-permute-start.62
  305.5 4.0 collective-permute-start.50
  312.2 5.0 collective-permute-done.51
  326.5 3.9 collective-permute-start.55
  343.5 3.9 collective-permute-start.59
  361.0 3.9 collective-permute-start.67
  377.8 3.9 collective-permute-start.71
  394.7 3.9 collective-permute-start.75
  412.0 3.9 collective-permute-start.79
  429.0 3.9 collective-permute-start.83
  446.1 3.9 collective-permute-start.87
  463.1 4.3 collective-permute-start.91
  483.5 3.9 collective-permute-start.95
  487.4 3.8 collective-permute-done.95
  500.8 3.9 collective-permute-start.99
  504.8 3.8 collective-permute-done.99
  518.2 3.9 collective-permute-start.103
  522.1 3.8 collective-permute-done.103
  535.6 3.9 collective-permute-start.107
  560.4 3.9 collective-permute-start.111
  564.4 3.9 collective-permute-done.111
  579.4 3.9 collective-permute-start.115
  583.4 3.9 collective-permute-done.115
  598.5 4.1 collective-permute-start.119
  617.6 3.9 collective-permute-start.123
  621.6 3.9 collective-permute-done.123
  (572 shorter events, 377.2 us)
Async XLA Ops:
  33.5 265.4 %collective-permute-start.61 = (f32[2,2,2,16]{3,2,1,0:T(2,128)S(1)}, f32[2,2,2,16]{3,2,1,0:T(2,128)S(1)}, u32[]{:S(2)}, u32[]{:S(2)}) collective-permute-start(f32[2,2,2,16]{3,2,1,0:T(2,128)S(1)} %broadcast_multiply_fusion.6), channel_id=1, source_target_pairs={{32,0},{64,32},{96,64},{128,96},{160,128},{192,160},{224,192},{33,... | collective-permute-start | bytes 1544 | tf_op jit(solution)/shard_map/ppermute | solution.py:25
  35.4 263.5 %collective-permute-start.60 = (f32[2,2,2,16]{3,2,1,0:T(2,128)S(1)}, f32[2,2,2,16]{3,2,1,0:T(2,128)}, u32[]{:S(2)}, u32[]{:S(2)}) collective-permute-start(f32[2,2,2,16]{3,2,1,0:T(2,128)S(1)} %broadcast_multiply_fusion.6), channel_id=1, source_target_pairs={{0,32},{32,64},{64,96},{96,128},{128,160},{160,192},{192,224},{1,3... | collective-permute-start | bytes 1544 | tf_op jit(solution)/shard_map/ppermute | solution.py:23
  37.8 8.8 %collective-permute-start.1 = (f32[2,2,16,128]{3,2,1,0:T(8,128)S(1)}, f32[2,2,16,128]{3,2,1,0:T(8,128)S(1)}, u32[]{:S(2)}, u32[]{:S(2)}) collective-permute-start(f32[2,2,16,128]{3,2,1,0:T(8,128)S(1)} %get-tuple-element.158), channel_id=1, source_target_pairs={{32,0},{64,32},{96,64},{128,96},{160,128},{192,160},{224,192},{33,... | collective-permute-start | bytes 98312 | tf_op jit(solution)/shard_map/ppermute | solution.py:25
  42.9 46.7 %collective-permute-start.21 = (f32[2,2,8,64]{3,2,1,0:T(8,128)S(1)}, f32[2,2,8,64]{3,2,1,0:T(8,128)S(1)}, u32[]{:S(2)}, u32[]{:S(2)}) collective-permute-start(f32[2,2,8,64]{3,2,1,0:T(8,128)S(1)} %get-tuple-element.272), channel_id=1, source_target_pairs={{32,0},{64,32},{96,64},{128,96},{160,128},{192,160},{224,192},{33,... | collective-permute-start | bytes 24584 | tf_op jit(solution)/shard_map/ppermute | solution.py:25
  48.5 10.5 %collective-permute-start.40 = (f32[2,2,4,32]{3,2,1,0:T(4,128)S(1)}, f32[2,2,4,32]{3,2,1,0:T(4,128)S(1)}, u32[]{:S(2)}, u32[]{:S(2)}) collective-permute-start(f32[2,2,4,32]{3,2,1,0:T(4,128)S(1)} %get-tuple-element.329), channel_id=1, source_target_pairs={{0,32},{32,64},{64,96},{96,128},{128,160},{160,192},{192,224},{1,3... | collective-permute-start | bytes 6152 | tf_op jit(solution)/shard_map/ppermute | solution.py:23
  51.0 10.0 %collective-permute-start.3 = (f32[2,20,2,128]{3,2,1,0:T(2,128)S(1)}, f32[2,20,2,128]{3,2,1,0:T(2,128)S(1)}, u32[]{:S(2)}, u32[]{:S(2)}) collective-permute-start(f32[2,20,2,128]{3,2,1,0:T(2,128)S(1)} %get-tuple-element.156), channel_id=1, source_target_pairs={{1,0},{2,1},{3,2},{4,3},{5,4},{6,5},{7,6},{8,7},{9,8},{10,9},{11,1... | collective-permute-start | bytes 122888 | tf_op jit(solution)/shard_map/ppermute | solution.py:25
  59.1 8.3 %collective-permute-start.2 = (f32[2,20,2,128]{3,2,1,0:T(2,128)S(1)}, f32[2,20,2,128]{3,2,1,0:T(2,128)S(1)}, u32[]{:S(2)}, u32[]{:S(2)}) collective-permute-start(f32[2,20,2,128]{3,2,1,0:T(2,128)S(1)} %get-tuple-element.155), channel_id=1, source_target_pairs={{0,1},{1,2},{2,3},{3,4},{4,5},{5,6},{6,7},{7,8},{8,9},{9,10},{10,1... | collective-permute-start | bytes 122888 | tf_op jit(solution)/shard_map/ppermute | solution.py:23
  77.7 7.9 %collective-permute-start.7 = (f32[3,18,1,128]{3,2,1,0:T(1,128)S(1)}, f32[3,18,1,128]{3,2,1,0:T(1,128)S(1)}, u32[]{:S(2)}, u32[]{:S(2)}) collective-permute-start(f32[3,18,1,128]{3,2,1,0:T(1,128)S(1)} %get-tuple-element.137), channel_id=1, source_target_pairs={{0,1},{1,2},{2,3},{3,4},{4,5},{5,6},{6,7},{7,8},{8,9},{9,10},{10,1... | collective-permute-start | bytes 82952 | tf_op jit(solution)/shard_map/ppermute | solution.py:23
  81.8 10.2 %collective-permute-start.20 = (f32[2,2,8,64]{3,2,1,0:T(8,128)S(1)}, f32[2,2,8,64]{3,2,1,0:T(8,128)S(1)}, u32[]{:S(2)}, u32[]{:S(2)}) collective-permute-start(f32[2,2,8,64]{3,2,1,0:T(8,128)S(1)} %get-tuple-element.271), channel_id=1, source_target_pairs={{0,32},{32,64},{64,96},{96,128},{128,160},{160,192},{192,224},{1,3... | collective-permute-start | bytes 24584 | tf_op jit(solution)/shard_map/ppermute | solution.py:23
  87.7 7.8 %collective-permute-start.8 = (f32[3,1,16,128]{3,2,1,0:T(8,128)S(1)}, f32[3,1,16,128]{3,2,1,0:T(8,128)S(1)}, u32[]{:S(2)}, u32[]{:S(2)}) collective-permute-start(f32[3,1,16,128]{3,2,1,0:T(8,128)S(1)} %get-tuple-element.152), channel_id=1, source_target_pairs={{32,0},{64,32},{96,64},{128,96},{160,128},{192,160},{224,192},{33,... | collective-permute-start | bytes 73736 | tf_op jit(solution)/shard_map/ppermute | solution.py:25
  89.6 8.3 %collective-permute-start.9 = (f32[3,1,16,128]{3,2,1,0:T(8,128)S(1)}, f32[3,1,16,128]{3,2,1,0:T(8,128)S(1)}, u32[]{:S(2)}, u32[]{:S(2)}) collective-permute-start(f32[3,1,16,128]{3,2,1,0:T(8,128)S(1)} %get-tuple-element.151), channel_id=1, source_target_pairs={{0,32},{32,64},{64,96},{96,128},{128,160},{160,192},{192,224},{1,3... | collective-permute-start | bytes 73736 | tf_op jit(solution)/shard_map/ppermute | solution.py:23
  92.1 11.5 %collective-permute-start.23 = (f32[2,12,2,64]{3,2,1,0:T(2,128)S(1)}, f32[2,12,2,64]{3,2,1,0:T(2,128)S(1)}, u32[]{:S(2)}, u32[]{:S(2)}) collective-permute-start(f32[2,12,2,64]{3,2,1,0:T(2,128)S(1)} %get-tuple-element.240), channel_id=1, source_target_pairs={{1,0},{2,1},{3,2},{4,3},{5,4},{6,5},{7,6},{8,7},{9,8},{10,9},{11,1... | collective-permute-start | bytes 36872 | tf_op jit(solution)/shard_map/ppermute | solution.py:25
  95.6 10.1 %collective-permute-start.22 = (f32[2,12,2,64]{3,2,1,0:T(2,128)S(1)}, f32[2,12,2,64]{3,2,1,0:T(2,128)S(1)}, u32[]{:S(2)}, u32[]{:S(2)}) collective-permute-start(f32[2,12,2,64]{3,2,1,0:T(2,128)S(1)} %get-tuple-element.239), channel_id=1, source_target_pairs={{0,1},{1,2},{2,3},{3,4},{4,5},{5,6},{6,7},{7,8},{8,9},{9,10},{10,1... | collective-permute-start | bytes 36872 | tf_op jit(solution)/shard_map/ppermute | solution.py:23
  98.0 7.7 %collective-permute-start.10 = (f32[3,18,1,128]{3,2,1,0:T(1,128)S(1)}, f32[3,18,1,128]{3,2,1,0:T(1,128)S(1)}, u32[]{:S(2)}, u32[]{:S(2)}) collective-permute-start(f32[3,18,1,128]{3,2,1,0:T(1,128)S(1)} %get-tuple-element.136), channel_id=1, source_target_pairs={{1,0},{2,1},{3,2},{4,3},{5,4},{6,5},{7,6},{8,7},{9,8},{10,9},{11,1... | collective-permute-start | bytes 82952 | tf_op jit(solution)/shard_map/ppermute | solution.py:25
  103.6 7.9 %collective-permute-start.11 = (f32[3,18,1,128]{3,2,1,0:T(1,128)S(1)}, f32[3,18,1,128]{3,2,1,0:T(1,128)S(1)}, u32[]{:S(2)}, u32[]{:S(2)}) collective-permute-start(f32[3,18,1,128]{3,2,1,0:T(1,128)S(1)} %get-tuple-element.135), channel_id=1, source_target_pairs={{0,1},{1,2},{2,3},{3,4},{4,5},{5,6},{6,7},{7,8},{8,9},{9,10},{10,1... | collective-permute-start | bytes 82952 | tf_op jit(solution)/shard_map/ppermute | solution.py:23
  123.0 7.9 %collective-permute-start.15 = (f32[3,18,1,128]{3,2,1,0:T(1,128)S(1)}, f32[3,18,1,128]{3,2,1,0:T(1,128)S(1)}, u32[]{:S(2)}, u32[]{:S(2)}) collective-permute-start(f32[3,18,1,128]{3,2,1,0:T(1,128)S(1)} %get-tuple-element.133), channel_id=1, source_target_pairs={{0,1},{1,2},{2,3},{3,4},{4,5},{5,6},{6,7},{7,8},{8,9},{9,10},{10,1... | collective-permute-start | bytes 82952 | tf_op jit(solution)/shard_map/ppermute | solution.py:23
  142.2 7.9 %collective-permute-start.19 = (f32[3,18,1,128]{3,2,1,0:T(1,128)S(1)}, f32[3,18,1,128]{3,2,1,0:T(1,128)S(1)}, u32[]{:S(2)}, u32[]{:S(2)}) collective-permute-start(f32[3,18,1,128]{3,2,1,0:T(1,128)S(1)} %get-tuple-element.131), channel_id=1, source_target_pairs={{0,1},{1,2},{2,3},{3,4},{4,5},{5,6},{6,7},{7,8},{8,9},{9,10},{10,1... | collective-permute-start | bytes 82952 | tf_op jit(solution)/shard_map/ppermute | solution.py:23
  197.0 7.7 %collective-permute-start.27 = (f32[3,10,1,64]{3,2,1,0:T(1,128)S(1)}, f32[3,10,1,64]{3,2,1,0:T(1,128)S(1)}, u32[]{:S(2)}, u32[]{:S(2)}) collective-permute-start(f32[3,10,1,64]{3,2,1,0:T(1,128)S(1)} %get-tuple-element.219), channel_id=1, source_target_pairs={{0,1},{1,2},{2,3},{3,4},{4,5},{5,6},{6,7},{7,8},{8,9},{9,10},{10,1... | collective-permute-start | bytes 23048 | tf_op jit(solution)/shard_map/ppermute | solution.py:23
  207.4 8.3 %collective-permute-start.29 = (f32[3,1,8,64]{3,2,1,0:T(8,128)S(1)}, f32[3,1,8,64]{3,2,1,0:T(8,128)S(1)}, u32[]{:S(2)}, u32[]{:S(2)}) collective-permute-start(f32[3,1,8,64]{3,2,1,0:T(8,128)S(1)} %get-tuple-element.235), channel_id=1, source_target_pairs={{0,32},{32,64},{64,96},{96,128},{128,160},{160,192},{192,224},{1,3... | collective-permute-start | bytes 18440 | tf_op jit(solution)/shard_map/ppermute | solution.py:23
  209.9 10.0 %collective-permute-start.43 = (f32[2,8,2,32]{3,2,1,0:T(2,128)S(1)}, f32[2,8,2,32]{3,2,1,0:T(2,128)S(1)}, u32[]{:S(2)}, u32[]{:S(2)}) collective-permute-start(f32[2,8,2,32]{3,2,1,0:T(2,128)S(1)} %get-tuple-element.296), channel_id=1, source_target_pairs={{1,0},{2,1},{3,2},{4,3},{5,4},{6,5},{7,6},{8,7},{9,8},{10,9},{11,1... | collective-permute-start | bytes 12296 | tf_op jit(solution)/shard_map/ppermute | solution.py:25
  211.8 10.0 %collective-permute-start.42 = (f32[2,8,2,32]{3,2,1,0:T(2,128)S(1)}, f32[2,8,2,32]{3,2,1,0:T(2,128)S(1)}, u32[]{:S(2)}, u32[]{:S(2)}) collective-permute-start(f32[2,8,2,32]{3,2,1,0:T(2,128)S(1)} %get-tuple-element.295), channel_id=1, source_target_pairs={{0,1},{1,2},{2,3},{3,4},{4,5},{5,6},{6,7},{7,8},{8,9},{9,10},{10,1... | collective-permute-start | bytes 12296 | tf_op jit(solution)/shard_map/ppermute | solution.py:23
  219.8 7.7 %collective-permute-start.31 = (f32[3,10,1,64]{3,2,1,0:T(1,128)S(1)}, f32[3,10,1,64]{3,2,1,0:T(1,128)S(1)}, u32[]{:S(2)}, u32[]{:S(2)}) collective-permute-start(f32[3,10,1,64]{3,2,1,0:T(1,128)S(1)} %get-tuple-element.217), channel_id=1, source_target_pairs={{0,1},{1,2},{2,3},{3,4},{4,5},{5,6},{6,7},{7,8},{8,9},{9,10},{10,1... | collective-permute-start | bytes 23048 | tf_op jit(solution)/shard_map/ppermute | solution.py:23
  237.2 7.7 %collective-permute-start.35 = (f32[3,10,1,64]{3,2,1,0:T(1,128)S(1)}, f32[3,10,1,64]{3,2,1,0:T(1,128)S(1)}, u32[]{:S(2)}, u32[]{:S(2)}) collective-permute-start(f32[3,10,1,64]{3,2,1,0:T(1,128)S(1)} %get-tuple-element.215), channel_id=1, source_target_pairs={{0,1},{1,2},{2,3},{3,4},{4,5},{5,6},{6,7},{7,8},{8,9},{9,10},{10,1... | collective-permute-start | bytes 23048 | tf_op jit(solution)/shard_map/ppermute | solution.py:23
  252.8 10.8 %collective-permute-start.38 = (f32[3,10,1,64]{3,2,1,0:T(1,128)S(1)}, f32[3,10,1,64]{3,2,1,0:T(1,128)S(1)}, u32[]{:S(2)}, u32[]{:S(2)}) collective-permute-start(f32[3,10,1,64]{3,2,1,0:T(1,128)S(1)} %get-tuple-element.214), channel_id=1, source_target_pairs={{1,0},{2,1},{3,2},{4,3},{5,4},{6,5},{7,6},{8,7},{9,8},{10,9},{11,1... | collective-permute-start | bytes 23048 | tf_op jit(solution)/shard_map/ppermute | solution.py:25
  254.7 8.9 %collective-permute-start.39 = (f32[3,10,1,64]{3,2,1,0:T(1,128)S(1)}, f32[3,10,1,64]{3,2,1,0:T(1,128)S(1)}, u32[]{:S(2)}, u32[]{:S(2)}) collective-permute-start(f32[3,10,1,64]{3,2,1,0:T(1,128)S(1)} %get-tuple-element.213), channel_id=1, source_target_pairs={{0,1},{1,2},{2,3},{3,4},{4,5},{5,6},{6,7},{7,8},{8,9},{9,10},{10,1... | collective-permute-start | bytes 23048 | tf_op jit(solution)/shard_map/ppermute | solution.py:23
  286.3 7.7 %collective-permute-start.47 = (f32[3,6,1,32]{3,2,1,0:T(1,128)S(1)}, f32[3,6,1,32]{3,2,1,0:T(1,128)S(1)}, u32[]{:S(2)}, u32[]{:S(2)}) collective-permute-start(f32[3,6,1,32]{3,2,1,0:T(1,128)S(1)} %get-tuple-element.293), channel_id=1, source_target_pairs={{0,1},{1,2},{2,3},{3,4},{4,5},{5,6},{6,7},{7,8},{8,9},{9,10},{10,1... | collective-permute-start | bytes 6920 | tf_op jit(solution)/shard_map/ppermute | solution.py:23
  294.5 10.9 %collective-permute-start.48 = (f32[3,1,4,32]{3,2,1,0:T(4,128)S(1)}, f32[3,1,4,32]{3,2,1,0:T(4,128)S(1)}, u32[]{:S(2)}, u32[]{:S(2)}) collective-permute-start(f32[3,1,4,32]{3,2,1,0:T(4,128)S(1)} %get-tuple-element.320), channel_id=1, source_target_pairs={{32,0},{64,32},{96,64},{128,96},{160,128},{192,160},{224,192},{33,... | collective-permute-start | bytes 4616 | tf_op jit(solution)/shard_map/ppermute | solution.py:25
  296.4 9.0 %collective-permute-start.49 = (f32[3,1,4,32]{3,2,1,0:T(4,128)S(1)}, f32[3,1,4,32]{3,2,1,0:T(4,128)S(1)}, u32[]{:S(2)}, u32[]{:S(2)}) collective-permute-start(f32[3,1,4,32]{3,2,1,0:T(4,128)S(1)} %get-tuple-element.319), channel_id=1, source_target_pairs={{0,32},{32,64},{64,96},{96,128},{128,160},{160,192},{192,224},{1,3... | collective-permute-start | bytes 4616 | tf_op jit(solution)/shard_map/ppermute | solution.py:23
  299.6 11.9 %collective-permute-start.63 = (f32[2,6,2,16]{3,2,1,0:T(2,128)S(1)}, f32[2,6,2,16]{3,2,1,0:T(2,128)S(1)}, u32[]{:S(2)}, u32[]{:S(2)}) collective-permute-start(f32[2,6,2,16]{3,2,1,0:T(2,128)S(1)} %pad_maximum_fusion.254), channel_id=1, source_target_pairs={{1,0},{2,1},{3,2},{4,3},{5,4},{6,5},{7,6},{8,7},{9,8},{10,9},{11,1... | collective-permute-start | bytes 4616 | tf_op jit(solution)/shard_map/ppermute | solution.py:25
  301.5 10.0 %collective-permute-start.62 = (f32[2,6,2,16]{3,2,1,0:T(2,128)S(1)}, f32[2,6,2,16]{3,2,1,0:T(2,128)S(1)}, u32[]{:S(2)}, u32[]{:S(2)}) collective-permute-start(f32[2,6,2,16]{3,2,1,0:T(2,128)S(1)} %pad_maximum_fusion.254), channel_id=1, source_target_pairs={{0,1},{1,2},{2,3},{3,4},{4,5},{5,6},{6,7},{7,8},{8,9},{9,10},{10,1... | collective-permute-start | bytes 4616 | tf_op jit(solution)/shard_map/ppermute | solution.py:23
  309.5 7.7 %collective-permute-start.51 = (f32[3,6,1,32]{3,2,1,0:T(1,128)S(1)}, f32[3,6,1,32]{3,2,1,0:T(1,128)S(1)}, u32[]{:S(2)}, u32[]{:S(2)}) collective-permute-start(f32[3,6,1,32]{3,2,1,0:T(1,128)S(1)} %get-tuple-element.291), channel_id=1, source_target_pairs={{0,1},{1,2},{2,3},{3,4},{4,5},{5,6},{6,7},{7,8},{8,9},{9,10},{10,1... | collective-permute-start | bytes 6920 | tf_op jit(solution)/shard_map/ppermute | solution.py:23
  326.5 7.7 %collective-permute-start.55 = (f32[3,6,1,32]{3,2,1,0:T(1,128)S(1)}, f32[3,6,1,32]{3,2,1,0:T(1,128)S(1)}, u32[]{:S(2)}, u32[]{:S(2)}) collective-permute-start(f32[3,6,1,32]{3,2,1,0:T(1,128)S(1)} %get-tuple-element.289), channel_id=1, source_target_pairs={{0,1},{1,2},{2,3},{3,4},{4,5},{5,6},{6,7},{7,8},{8,9},{9,10},{10,1... | collective-permute-start | bytes 6920 | tf_op jit(solution)/shard_map/ppermute | solution.py:23
  343.5 7.7 %collective-permute-start.59 = (f32[3,6,1,32]{3,2,1,0:T(1,128)S(1)}, f32[3,6,1,32]{3,2,1,0:T(1,128)S(1)}, u32[]{:S(2)}, u32[]{:S(2)}) collective-permute-start(f32[3,6,1,32]{3,2,1,0:T(1,128)S(1)} %get-tuple-element.287), channel_id=1, source_target_pairs={{0,1},{1,2},{2,3},{3,4},{4,5},{5,6},{6,7},{7,8},{8,9},{9,10},{10,1... | collective-permute-start | bytes 6920 | tf_op jit(solution)/shard_map/ppermute | solution.py:23
  361.0 7.6 %collective-permute-start.67 = (f32[3,4,1,16]{3,2,1,0:T(1,128)S(1)}, f32[3,4,1,16]{3,2,1,0:T(1,128)S(1)}, u32[]{:S(2)}, u32[]{:S(2)}) collective-permute-start(f32[3,4,1,16]{3,2,1,0:T(1,128)S(1)} %get-tuple-element.335), channel_id=1, source_target_pairs={{0,1},{1,2},{2,3},{3,4},{4,5},{5,6},{6,7},{7,8},{8,9},{9,10},{10,1... | collective-permute-start | bytes 2312 | tf_op jit(solution)/shard_map/ppermute | solution.py:23
  377.8 7.6 %collective-permute-start.71 = (f32[3,4,1,16]{3,2,1,0:T(1,128)S(1)}, f32[3,4,1,16]{3,2,1,0:T(1,128)S(1)}, u32[]{:S(2)}, u32[]{:S(2)}) collective-permute-start(f32[3,4,1,16]{3,2,1,0:T(1,128)S(1)} %get-tuple-element.333), channel_id=1, source_target_pairs={{0,1},{1,2},{2,3},{3,4},{4,5},{5,6},{6,7},{7,8},{8,9},{9,10},{10,1... | collective-permute-start | bytes 2312 | tf_op jit(solution)/shard_map/ppermute | solution.py:23
  394.7 7.6 %collective-permute-start.75 = (f32[3,4,1,16]{3,2,1,0:T(1,128)S(1)}, f32[3,4,1,16]{3,2,1,0:T(1,128)S(1)}, u32[]{:S(2)}, u32[]{:S(2)}) collective-permute-start(f32[3,4,1,16]{3,2,1,0:T(1,128)S(1)} %get-tuple-element.331), channel_id=1, source_target_pairs={{0,1},{1,2},{2,3},{3,4},{4,5},{5,6},{6,7},{7,8},{8,9},{9,10},{10,1... | collective-permute-start | bytes 2312 | tf_op jit(solution)/shard_map/ppermute | solution.py:23
  412.0 7.7 %collective-permute-start.79 = (f32[3,6,1,32]{3,2,1,0:T(1,128)S(1)}, f32[3,6,1,32]{3,2,1,0:T(1,128)S(1)}, u32[]{:S(2)}, u32[]{:S(2)}) collective-permute-start(f32[3,6,1,32]{3,2,1,0:T(1,128)S(1)} %get-tuple-element.285), channel_id=1, source_target_pairs={{0,1},{1,2},{2,3},{3,4},{4,5},{5,6},{6,7},{7,8},{8,9},{9,10},{10,1... | collective-permute-start | bytes 6920 | tf_op jit(solution)/shard_map/ppermute | solution.py:23
  429.0 7.7 %collective-permute-start.83 = (f32[3,6,1,32]{3,2,1,0:T(1,128)S(1)}, f32[3,6,1,32]{3,2,1,0:T(1,128)S(1)}, u32[]{:S(2)}, u32[]{:S(2)}) collective-permute-start(f32[3,6,1,32]{3,2,1,0:T(1,128)S(1)} %get-tuple-element.283), channel_id=1, source_target_pairs={{0,1},{1,2},{2,3},{3,4},{4,5},{5,6},{6,7},{7,8},{8,9},{9,10},{10,1... | collective-permute-start | bytes 6920 | tf_op jit(solution)/shard_map/ppermute | solution.py:23
  446.1 7.7 %collective-permute-start.87 = (f32[3,6,1,32]{3,2,1,0:T(1,128)S(1)}, f32[3,6,1,32]{3,2,1,0:T(1,128)S(1)}, u32[]{:S(2)}, u32[]{:S(2)}) collective-permute-start(f32[3,6,1,32]{3,2,1,0:T(1,128)S(1)} %get-tuple-element.281), channel_id=1, source_target_pairs={{0,1},{1,2},{2,3},{3,4},{4,5},{5,6},{6,7},{7,8},{8,9},{9,10},{10,1... | collective-permute-start | bytes 6920 | tf_op jit(solution)/shard_map/ppermute | solution.py:23
  463.1 7.7 %collective-permute-start.91 = (f32[3,6,1,32]{3,2,1,0:T(1,128)S(1)}, f32[3,6,1,32]{3,2,1,0:T(1,128)S(1)}, u32[]{:S(2)}, u32[]{:S(2)}) collective-permute-start(f32[3,6,1,32]{3,2,1,0:T(1,128)S(1)} %get-tuple-element.279), channel_id=1, source_target_pairs={{0,1},{1,2},{2,3},{3,4},{4,5},{5,6},{6,7},{7,8},{8,9},{9,10},{10,1... | collective-permute-start | bytes 6920 | tf_op jit(solution)/shard_map/ppermute | solution.py:23
  483.5 7.7 %collective-permute-start.95 = (f32[3,10,1,64]{3,2,1,0:T(1,128)S(1)}, f32[3,10,1,64]{3,2,1,0:T(1,128)S(1)}, u32[]{:S(2)}, u32[]{:S(2)}) collective-permute-start(f32[3,10,1,64]{3,2,1,0:T(1,128)S(1)} %get-tuple-element.211), channel_id=1, source_target_pairs={{0,1},{1,2},{2,3},{3,4},{4,5},{5,6},{6,7},{7,8},{8,9},{9,10},{10,1... | collective-permute-start | bytes 23048 | tf_op jit(solution)/shard_map/ppermute | solution.py:23
  500.8 7.7 %collective-permute-start.99 = (f32[3,10,1,64]{3,2,1,0:T(1,128)S(1)}, f32[3,10,1,64]{3,2,1,0:T(1,128)S(1)}, u32[]{:S(2)}, u32[]{:S(2)}) collective-permute-start(f32[3,10,1,64]{3,2,1,0:T(1,128)S(1)} %get-tuple-element.209), channel_id=1, source_target_pairs={{0,1},{1,2},{2,3},{3,4},{4,5},{5,6},{6,7},{7,8},{8,9},{9,10},{10,1... | collective-permute-start | bytes 23048 | tf_op jit(solution)/shard_map/ppermute | solution.py:23
  518.2 7.7 %collective-permute-start.103 = (f32[3,10,1,64]{3,2,1,0:T(1,128)S(1)}, f32[3,10,1,64]{3,2,1,0:T(1,128)S(1)}, u32[]{:S(2)}, u32[]{:S(2)}) collective-permute-start(f32[3,10,1,64]{3,2,1,0:T(1,128)S(1)} %get-tuple-element.207), channel_id=1, source_target_pairs={{0,1},{1,2},{2,3},{3,4},{4,5},{5,6},{6,7},{7,8},{8,9},{9,10},{10,1... | collective-permute-start | bytes 23048 | tf_op jit(solution)/shard_map/ppermute | solution.py:23
  535.6 7.7 %collective-permute-start.107 = (f32[3,10,1,64]{3,2,1,0:T(1,128)S(1)}, f32[3,10,1,64]{3,2,1,0:T(1,128)S(1)}, u32[]{:S(2)}, u32[]{:S(2)}) collective-permute-start(f32[3,10,1,64]{3,2,1,0:T(1,128)S(1)} %get-tuple-element.205), channel_id=1, source_target_pairs={{0,1},{1,2},{2,3},{3,4},{4,5},{5,6},{6,7},{7,8},{8,9},{9,10},{10,1... | collective-permute-start | bytes 23048 | tf_op jit(solution)/shard_map/ppermute | solution.py:23
  560.4 7.9 %collective-permute-start.111 = (f32[3,18,1,128]{3,2,1,0:T(1,128)S(1)}, f32[3,18,1,128]{3,2,1,0:T(1,128)S(1)}, u32[]{:S(2)}, u32[]{:S(2)}) collective-permute-start(f32[3,18,1,128]{3,2,1,0:T(1,128)S(1)} %get-tuple-element.129), channel_id=1, source_target_pairs={{0,1},{1,2},{2,3},{3,4},{4,5},{5,6},{6,7},{7,8},{8,9},{9,10},{10,1... | collective-permute-start | bytes 82952 | tf_op jit(solution)/shard_map/ppermute | solution.py:23
  579.4 7.9 %collective-permute-start.115 = (f32[3,18,1,128]{3,2,1,0:T(1,128)S(1)}, f32[3,18,1,128]{3,2,1,0:T(1,128)S(1)}, u32[]{:S(2)}, u32[]{:S(2)}) collective-permute-start(f32[3,18,1,128]{3,2,1,0:T(1,128)S(1)} %get-tuple-element.127), channel_id=1, source_target_pairs={{0,1},{1,2},{2,3},{3,4},{4,5},{5,6},{6,7},{7,8},{8,9},{9,10},{10,1... | collective-permute-start | bytes 82952 | tf_op jit(solution)/shard_map/ppermute | solution.py:23
  598.5 7.9 %collective-permute-start.119 = (f32[3,18,1,128]{3,2,1,0:T(1,128)S(1)}, f32[3,18,1,128]{3,2,1,0:T(1,128)S(1)}, u32[]{:S(2)}, u32[]{:S(2)}) collective-permute-start(f32[3,18,1,128]{3,2,1,0:T(1,128)S(1)} %get-tuple-element.125), channel_id=1, source_target_pairs={{0,1},{1,2},{2,3},{3,4},{4,5},{5,6},{6,7},{7,8},{8,9},{9,10},{10,1... | collective-permute-start | bytes 82952 | tf_op jit(solution)/shard_map/ppermute | solution.py:23
  617.6 7.9 %collective-permute-start.123 = (f32[3,18,1,128]{3,2,1,0:T(1,128)S(1)}, f32[3,18,1,128]{3,2,1,0:T(1,128)S(1)}, u32[]{:S(2)}, u32[]{:S(2)}) collective-permute-start(f32[3,18,1,128]{3,2,1,0:T(1,128)S(1)} %get-tuple-element.123), channel_id=1, source_target_pairs={{0,1},{1,2},{2,3},{3,4},{4,5},{5,6},{6,7},{7,8},{8,9},{9,10},{10,1... | collective-permute-start | bytes 82952 | tf_op jit(solution)/shard_map/ppermute | solution.py:23
  (113 other events, 900.4 us)
where the time goes:
time: 640 us; the launch traced here: 629 us
  starting transfers between devices  324 us (51%)
  waiting for transfers between devices  168 us (26%)
  local copies, waits for them, and re-layouts  76.7 us (12%)
  other arithmetic  56.3 us (9%)
    ppermute x62, starting transfers between devices, with_halo(): lax.ppermute(tail, axis, [(i, (i + 1) % count) for i in range(ends)])  184 us
    ppermute x62, waiting for transfers between devices, with_halo(): lax.ppermute(tail, axis, [(i, (i + 1) % count) for i in range(ends)])  168 us
    ppermute x62, starting transfers between devices, with_halo(): lax.ppermute(head, axis, [((i + 1) % count, i) for i in range(ends)])  140 us
    reshape x1, local copies, waits for them, and re-layouts, shrink(): blocks = array.reshape(comps, rows // 2, 2, cols // 2, 2, depth // 2, 2)  26.5 us
    reduce_sum x6, other arithmetic, shrink(): return blocks.mean(axis=(2, 4, 6))  22 us
    another operation x2, local copies, waits for them, and re-layouts, on_device(): coeff = jnp.stack([stiffness, reaction])  20.2 us
  transfers between devices with their start and end apart: 124, of which 51 were waited for; matrix products, arithmetic and copies ran while one was open for 11% of the time, Pallas kernels for 0%

commit v1 on v0

v1 whole, which is shorter than its diff:
```python
import jax
import jax.numpy as jnp
from jax import lax
from jax.experimental import pallas as pl
from jax.experimental.pallas import tpu as pltpu
from jax.sharding import PartitionSpec as P

BETA = 1.0
THETA = 1.5
DELTA = 1.0
SIGMA = 1.5
LANES = 128
HALO = 8
NEAR = 10
SKIRT = 12
REACH = 5
F32 = jnp.float32


def rate_list():
    rates = [1.0 / SIGMA]
    for number in range(3):
        rates.append(1.0 / (2.0 * SIGMA - rates[-1]))
    return rates


RATES = rate_list()
STEPS = [(0.0, 1.0 / THETA)] + [
    (RATES[k] * RATES[k - 1], 2.0 * RATES[k] / DELTA) for k in (1, 2, 3)
]


def lane_of(shape):
    return lax.broadcasted_iota(jnp.int32, shape, len(shape) - 1)


def row_of(shape):
    return lax.broadcasted_iota(jnp.int32, shape, len(shape) - 2)


def ahead_y(v):
    return pltpu.roll(v, v.shape[0] - 1, 0)


def behind_y(v):
    return pltpu.roll(v, 1, 0)


def ahead_z(v):
    return pltpu.roll(v, LANES - 1, 1)


def behind_z(v):
    return pltpu.roll(v, 1, 1)


class Level:
    def __init__(self, scale, depth, rows, height):
        self.scale = scale
        self.depth = depth
        self.groups = LANES // depth
        self.rows = rows
        self.height = height

    def shape(self, *lead):
        return (*lead, self.rows + 2, self.height, LANES)

    def lanes(self):
        z = lane_of((self.height, LANES)) % self.depth
        return z == 0, z == self.depth - 1


def ghosts(level, ref, index=()):
    if level.groups == 1:
        return
    lane = lane_of((level.height, LANES))
    first = ref[(*index, 1)]
    last = ref[(*index, level.rows)]
    ref[(*index, 0)] = jnp.where(lane < level.depth, 0.0, pltpu.roll(last, level.depth, 1))
    ref[(*index, level.rows + 1)] = jnp.where(
        lane >= LANES - level.depth, 0.0, pltpu.roll(first, LANES - level.depth, 1)
    )


def setup(level, stiff, react, coef, inside, lo, hi):
    kx, ky, kym, kz, kzm, diag, inv = coef
    half = 0.5 * level.scale
    front, back = level.lanes()
    kx[lo - 1] = half * (stiff(lo - 1) + stiff(lo))

    def body(i, _):
        centre = stiff(i)
        xp = half * (centre + stiff(i + 1))
        xm = kx[i - 1]
        yp = half * (centre + ahead_y(centre))
        ym = behind_y(yp)
        zp = half * (centre + jnp.where(back, 0.0, ahead_z(centre)))
        zm = half * (centre + jnp.where(front, 0.0, behind_z(centre)))
        total = ((xp + xm) + (yp + ym)) + (zp + zm) + react(i)
        kx[i] = xp
        ky[i] = yp
        kym[i] = ym
        kz[i] = jnp.where(back, 0.0, zp)
        kzm[i] = jnp.where(front, 0.0, zm)
        diag[i] = total
        inv[i] = jnp.where(inside(i), 1.0 / (total + 2.0 * BETA * level.scale), 0.0)
        return 0

    lax.fori_loop(lo, hi, body, 0)


def begin(level, src, coef, state, direction, lo, hi):
    inv = coef[6]

    def body(i, _):
        scaled = inv[i] * (1.0 / THETA)
        for c in range(3):
            value = scaled * src[c, i]
            state[c, i] = value
            direction[c, i] = value
        return 0

    lax.fori_loop(lo, hi, body, 0)
    for c in range(3):
        ghosts(level, state, (c,))


def sweep(level, src, coef, state, lo, hi, emit):
    kx, ky, kym, kz, kzm, diag, inv = coef
    front, back = level.lanes()
    bulk = BETA * level.scale

    def spread(i):
        ux, uy, uz = state[0, i], state[1, i], state[2, i]
        return (
            (state[0, i + 1] - ux)
            + (ahead_y(uy) - uy)
            + (jnp.where(back, 0.0, ahead_z(uz)) - uz)
        ) * bulk

    def body(i, before):
        here = spread(i)
        for c in range(3):
            u = state[c, i]
            flux = kx[i] * state[c, i + 1] + kx[i - 1] * state[c, i - 1]
            flux = flux + (ky[i] * ahead_y(u) + kym[i] * behind_y(u))
            flux = flux + (kz[i] * ahead_z(u) + kzm[i] * behind_z(u))
            if c == 0:
                other = before
            elif c == 1:
                other = behind_y(here)
            else:
                other = jnp.where(front, bulk * u, behind_z(here))
            resid = src[c, i] - diag[i] * u + flux + (here - other)
            emit(i, c, u, resid)
        return here

    lax.fori_loop(lo, hi, body, spread(lo - 1))


def step(level, number, src, coef, state, fresh, direction, lo, hi):
    keep, gain = STEPS[number]
    inv = coef[6]

    def emit(i, c, u, resid):
        move = (gain * inv[i]) * resid
        if number > 0:
            move = move + keep * direction[c, i]
        direction[c, i] = move
        fresh[c, i] = u + move

    sweep(level, src, coef, state, lo, hi, emit)
    for c in range(3):
        ghosts(level, fresh, (c,))


def residual(level, src, coef, state, out, lo, hi):
    def emit(i, c, u, resid):
        out[c, i] = resid

    sweep(level, src, coef, state, lo, hi, emit)


def pick(rows, cols, rule, value):
    shape = (rows, cols)
    return jnp.where(rule(row_of(shape), lane_of(shape)), value, 0.0).astype(F32)


def mix(values, matrix):
    return jnp.dot(values, matrix, precision=lax.Precision.HIGHEST, preferred_element_type=F32)


def pairs(ref, index, start, count):
    return ref[(*index, pl.ds(start, count, 2))] + ref[(*index, pl.ds(start + 1, count, 2))]


def vmem(count):
    return [pl.BlockSpec(memory_space=pltpu.VMEM)] * count


def call(kernel, outs, scratch, *args, name):
    smem = pl.BlockSpec(memory_space=pltpu.SMEM)
    return pl.pallas_call(
        kernel,
        out_shape=[jax.ShapeDtypeStruct(s, F32) for s in outs],
        in_specs=[smem] + vmem(len(args) - 1),
        out_specs=vmem(len(outs)),
        scratch_shapes=[pltpu.VMEM(s, F32) for s in scratch],
        compiler_params=pltpu.CompilerParams(vmem_limit_bytes=50 * 2**20),
        name=name,
    )(*args)


def cut_kernel(place, f, k, r, lo, hi):
    for q in range(5):
        part = (lambda s: f[q, :, s]) if q < 3 else (lambda s: (k, r)[q - 3][:, s])
        lo[q] = part(slice(0, HALO))
        hi[q] = part(slice(HALO, 2 * HALO))


def join_kernel(place, f, k, r, lo, hi, first, second):
    for q in range(5):
        for half, out in enumerate((first, second)):
            rows = slice(8 * half, 8 * half + 8)
            part = f[q, rows] if q < 3 else (k, r)[q - 3][rows]
            out[q, :, 0:8] = lo[q, rows]
            out[q, :, 8:24] = part
            out[q, :, 24:32] = hi[q, rows]


FINE = Level(1.0, 128, 30, 32)
MIDDLE = Level(0.25, 64, 14, 32)
COARSE = Level(0.0625, 32, 8, 48)
LAST = Level(0.015625, 16, 2, 24)


def coef_shapes(level):
    return [level.shape()] * 7


def fine_inside(place):
    y = place[1] * 16 - HALO + row_of((32, LANES))
    fits = (y >= 0) & (y < place[3] * 16)

    def inside(i):
        x = place[0] * 16 + i - HALO
        return fits & (x >= 0) & (x < place[2] * 16)

    return inside


def fine_down(place, first, second, lo, hi, data, saved, packed, s0, d0, t0, sums, *coef):
    for q in range(5):
        data[q, 0:8] = lo[q]
        data[q, 8:16] = first[q]
        data[q, 16:24] = second[q]
        data[q, 24:32] = hi[q]
    inside = fine_inside(place)
    setup(FINE, lambda i: data[3, i], lambda i: data[4, i], coef, inside, 1, 31)
    begin(FINE, data, coef, s0, d0, 1, 31)
    step(FINE, 1, data, coef, s0, t0, d0, 2, 30)
    step(FINE, 2, data, coef, t0, s0, d0, 3, 29)
    step(FINE, 3, data, coef, s0, t0, d0, 4, 28)
    saved[...] = t0[:, 4:28]
    residual(FINE, data, coef, t0, d0, 6, 26)
    pair = s0.at[0]
    wide = sums
    for q in range(5):
        for t in range(16):
            half, i = divmod(t, 8)
            where = (q, i, slice(None), slice(half * LANES, half * LANES + LANES))
            if q >= 3:
                pair[t] = data[q, 2 * t] + data[q, 2 * t + 1]
            elif 3 <= t <= 12:
                pair[t] = d0[q, 2 * t] + d0[q, 2 * t + 1]
            else:
                wide[where] = jnp.zeros((16, LANES), F32)
                continue
            wide[where] = pairs(pair, (t,), 0, 16)
    matrix = pick(
        2 * LANES, LANES, lambda a, b: (a % LANES) // 2 + 64 * (a // LANES) == b, 0.125
    )
    packed[...] = mix(wide[...].reshape(5 * 8 * 16, 2 * LANES), matrix).reshape(5, 8, 16, LANES)


def middle_cut(place, own, left, right, up, down, centre):
    lane = lane_of((32, LANES))

    for q in range(5):
        for i in range(8):
            centre[q, i, 0:12] = left[q, i, 0:12]
            centre[q, i, 12:20] = own[q, i, 4:12]
            centre[q, i, 20:32] = right[q, i, 4:16]
        for t in range(5):
            tail = pltpu.roll(centre[q, 7], 64, 1) if t == 0 else centre[q, t - 1]
            up[q, t] = jnp.where(lane < 64, centre[q, 2 + t], tail)
            head = pltpu.roll(centre[q, 0], 64, 1) if t == 4 else centre[q, 4 + t]
            down[q, t] = jnp.where(lane < 64, head, centre[q, 1 + t])


def middle_inside(place):
    y = place[1] * 8 - SKIRT + row_of((32, LANES))
    fits = (y >= 0) & (y < place[3] * 8)
    x0 = place[0] * 8 - NEAR + 14 * (lane_of((32, LANES)) // 64)

    def inside(i):
        x = x0 + (i - 1)
        return fits & (x >= 0) & (x < place[2] * 8)

    return inside


def middle_down(place, centre, lo, hi, data, saved, packed, s1, d1, t1, pair, sums, *coef):
    lane = lane_of((32, LANES))
    low = lane < 64
    for q in range(5):
        for i in range(14):
            if i < 5:
                a = lo[q, i]
            elif i < 10:
                a = pltpu.roll(lo[q, i - 5], 64, 1)
            else:
                a = centre[q, i - 6]
            if i < 4:
                b = centre[q, i]
            elif i < 9:
                b = pltpu.roll(hi[q, i - 4], 64, 1)
            else:
                b = hi[q, i - 9]
            data[q, i + 1] = jnp.where(low, a, b)
        ghosts(MIDDLE, data, (q,))
    setup(MIDDLE, lambda i: data[3, i], lambda i: data[4, i], coef, middle_inside(place), 1, 15)
    begin(MIDDLE, data, coef, s1, d1, 1, 15)
    step(MIDDLE, 1, data, coef, s1, t1, d1, 1, 15)
    step(MIDDLE, 2, data, coef, t1, s1, d1, 1, 15)
    step(MIDDLE, 3, data, coef, s1, saved, d1, 1, 15)
    residual(MIDDLE, data, coef, saved, d1, 11, 15)
    residual(MIDDLE, data, coef, saved, d1, 1, 5)
    for q in range(5):
        from_, at = (d1, q) if q < 3 else (data, q)
        for m in range(2):
            a = from_[at, 11 + 2 * m] + from_[at, 12 + 2 * m]
            b = from_[at, 1 + 2 * m] + from_[at, 2 + 2 * m]
            pair[q, m] = jnp.where(low, a, b)
            sums[q, :, m * LANES : m * LANES + LANES] = pairs(pair, (q, m), 0, 16)
    matrix = pick(
        2 * LANES,
        LANES,
        lambda a, b: (a // LANES) * 32 + ((a % LANES) // 64) * 64 + (a % 64) // 2 == b,
        0.125,
    )
    packed[...] = mix(sums[...].reshape(5 * 16, 2 * LANES), matrix).reshape(5, 16, LANES)


def column_kernel(place, parts, out):
    zero = jnp.zeros((4, LANES), F32)
    for q in range(5):
        out[q, 0:2] = zero[0:2]
        out[q, 46:48] = zero[0:2]
    for d in range(2 * REACH + 1):
        at = place[1] + (d - REACH)
        valid = (at >= 0) & (at < place[3])
        safe = jnp.clip(at, 0, place[3] - 1)
        for q in range(5):
            block = parts[safe, 4 * q : 4 * q + 4]
            out[q, 2 + 4 * d : 6 + 4 * d] = jnp.where(valid, block, zero)


def coarse_inside(place):
    sub = row_of((48, LANES))
    y = place[1] * 4 - 22 + sub
    fits = (y >= 0) & (y < place[3] * 4)
    return lambda i: fits


def last_inside(place):
    y = place[1] * 2 - 11 + row_of((24, LANES))
    fits = (y >= 0) & (y < place[3] * 2)
    return lambda i: fits


def climb(place, parts, data1, saved1, data0, saved0, out, *scratch):
    scratch = list(scratch)

    def take(count):
        got, scratch[:] = scratch[:count], scratch[count:]
        return got

    data2, s2, t2, d2, keep2 = take(5)
    coef2 = take(7)
    sums3 = take(1)[0]
    data3, s3, t3, d3 = take(4)
    coef3 = take(7)
    grown3, grown2, grown1 = take(3)
    s1, t1, d1 = take(3)
    coef1 = take(7)
    s0, t0, d0 = take(3)
    coef0 = take(7)

    lane = lane_of((48, LANES))
    group = lane // 32
    for q in range(5):
        for i in range(8):
            row = None
            for g in range(4):
                block = parts[2 * g + i // 4, q]
                shift = ((g - i % 4) * 32) % LANES
                block = pltpu.roll(block, shift, 1) if shift else block
                row = block if row is None else jnp.where(group == g, block, row)
            data2[q, i + 1] = row
        ghosts(COARSE, data2, (q,))
    setup(COARSE, lambda i: data2[3, i], lambda i: data2[4, i], coef2, coarse_inside(place), 1, 9)
    begin(COARSE, data2, coef2, s2, d2, 1, 9)
    step(COARSE, 1, data2, coef2, s2, t2, d2, 1, 9)
    step(COARSE, 2, data2, coef2, t2, s2, d2, 1, 9)
    step(COARSE, 3, data2, coef2, s2, keep2, d2, 1, 9)
    residual(COARSE, data2, coef2, keep2, d2, 1, 9)

    pair = s2.at[0]
    for q in range(5):
        from_ = d2 if q < 3 else data2
        for t in range(4):
            half, i = divmod(t, 2)
            pair[t] = from_[q, 1 + 2 * t] + from_[q, 2 + 2 * t]
            sums3[q, i, :, half * LANES : half * LANES + LANES] = pairs(pair, (t,), 0, 24)
    matrix = pick(
        2 * LANES,
        LANES,
        lambda a, b: (2 * ((a % LANES) // 32) + a // LANES) * 16 + (a % 32) // 2 == b,
        0.125,
    )
    shrunk = mix(sums3[...].reshape(5 * 2 * 24, 2 * LANES), matrix).reshape(5, 2, 24, LANES)
    for q in range(5):
        for i in range(2):
            data3[q, i + 1] = shrunk[q, i]
        ghosts(LAST, data3, (q,))
    setup(LAST, lambda i: data3[3, i], lambda i: data3[4, i], coef3, last_inside(place), 1, 3)
    begin(LAST, data3, coef3, s3, d3, 1, 3)
    step(LAST, 1, data3, coef3, s3, t3, d3, 1, 3)
    step(LAST, 2, data3, coef3, t3, s3, d3, 1, 3)
    step(LAST, 3, data3, coef3, s3, t3, d3, 1, 3)

    matrix = pick(
        LANES,
        2 * LANES,
        lambda a, b: (2 * ((b % LANES) // 32) + b // LANES == a // 16) & ((b % 32) // 2 == a % 16),
        1.0,
    )
    flat = jnp.concatenate([t3[c, i + 1] for c in range(3) for i in range(2)], axis=0)
    wide = mix(flat, matrix)
    for c in range(3):
        for t in range(4):
            half, i = divmod(t, 2)
            at = (c * 2 + i) * 24
            piece = wide[at : at + 24, half * LANES : half * LANES + LANES]
            grown3[c, t, pl.ds(0, 24, 2)] = piece
            grown3[c, t, pl.ds(1, 24, 2)] = piece
            more = grown3[c, t]
            s2[c, 1 + 2 * t] = keep2[c, 1 + 2 * t] + more
            s2[c, 2 + 2 * t] = keep2[c, 2 + 2 * t] + more
        ghosts(COARSE, s2, (c,))
    step(COARSE, 0, data2, coef2, s2, t2, d2, 1, 9)
    step(COARSE, 1, data2, coef2, t2, s2, d2, 1, 9)
    step(COARSE, 2, data2, coef2, s2, t2, d2, 1, 9)
    step(COARSE, 3, data2, coef2, t2, s2, d2, 1, 9)

    setup(MIDDLE, lambda i: data1[3, i], lambda i: data1[4, i], coef1, middle_inside(place), 1, 15)
    matrix = pick(
        LANES,
        LANES,
        lambda a, b: (a < 64) & (b // 64 == a // 32) & ((b % 64) // 2 == a % 32),
        1.0,
    )
    small = lane_of((16, LANES)) < 32

    def window(c, x, slot):
        valid = (x >= 0) & (x < place[2] * 4)
        safe = jnp.clip(x, 0, place[2] * 4 - 1)
        value = s2[c, 1 + safe % 8, 16:32]
        value = pltpu.roll(value, (slot * 32 + LANES - (safe // 8) * 32) % LANES, 1)
        return jnp.where(valid, value, 0.0)

    pieces = []
    for c in range(3):
        for m in range(7):
            x = place[0] * 4 - 5 + m
            pieces.append(jnp.where(small, window(c, x, 0), window(c, x + 7, 1)))
    wide = mix(jnp.concatenate(pieces, axis=0), matrix)
    for c in range(3):
        for m in range(7):
            at = (c * 7 + m) * 16
            piece = wide[at : at + 16]
            grown2[c, m, pl.ds(0, 16, 2)] = piece
            grown2[c, m, pl.ds(1, 16, 2)] = piece
            more = grown2[c, m]
            s1[c, 1 + 2 * m] = saved1[c, 1 + 2 * m] + more
            s1[c, 2 + 2 * m] = saved1[c, 2 + 2 * m] + more
        ghosts(MIDDLE, s1, (c,))
    step(MIDDLE, 0, data1, coef1, s1, t1, d1, 1, 15)
    step(MIDDLE, 1, data1, coef1, t1, s1, d1, 1, 15)
    step(MIDDLE, 2, data1, coef1, s1, t1, d1, 1, 15)
    step(MIDDLE, 3, data1, coef1, t1, s1, d1, 1, 15)

    setup(FINE, lambda i: data0[3, i], lambda i: data0[4, i], coef0, fine_inside(place), 5, 27)
    for half in range(2):
        matrix = pick(LANES, LANES, lambda a, b: a == 64 * half + b // 2, 1.0)
        rows = [9 + t for t in range(6)] if half == 0 else [1 + t for t in range(6)]
        flat = jnp.concatenate([s1[c, i, 8:24] for c in range(3) for i in rows], axis=0)
        wide = mix(flat, matrix)
        for c in range(3):
            for t in range(6):
                at = (c * 6 + t) * 16
                piece = wide[at : at + 16]
                grown1[c, t, pl.ds(0, 16, 2)] = piece
                grown1[c, t, pl.ds(1, 16, 2)] = piece
                more = grown1[c, t]
                row = 2 * (t + 6 * half)
                s0[c, 4 + row] = saved0[c, row] + more
                s0[c, 5 + row] = saved0[c, row + 1] + more
    step(FINE, 0, data0, coef0, s0, t0, d0, 5, 27)
    step(FINE, 1, data0, coef0, t0, s0, d0, 6, 26)
    step(FINE, 2, data0, coef0, s0, t0, d0, 7, 25)
    keep, gain = STEPS[3]

    def emit(i, c, u, resid):
        move = (gain * coef0[6][i]) * resid + keep * d0[c, i]
        out[c, i - 8] = (u + move)[8:24]

    sweep(FINE, data0, coef0, t0, 8, 24, emit)


def shift(value, axis, by):
    count = lax.axis_size(axis)
    return lax.ppermute(
        value, axis, [(i, i + by) for i in range(count) if 0 <= i + by < count]
    )


def on_device(right_side, stiffness, reaction):
    place = jnp.stack(
        [
            lax.axis_index("grp"),
            lax.axis_index("brick"),
            jnp.int32(lax.axis_size("grp")),
            jnp.int32(lax.axis_size("brick")),
        ]
    ).astype(jnp.int32)
    local = (right_side, stiffness, reaction)
    low, high = call(cut_kernel, [(5, 16, 8, 128)] * 2, [], place, *local, name="cut0")
    left = shift(high, "brick", 1)
    right = shift(low, "brick", -1)
    first, second = call(
        join_kernel, [(5, 8, 32, 128)] * 2, [], place, *local, left, right, name="join0"
    )
    below = shift(second, "grp", 1)
    above = shift(first, "grp", -1)
    fine = [FINE.shape(3)] * 3
    data0, saved0, packed1 = call(
        fine_down,
        [FINE.shape(5), (3, 24, 32, 128), (5, 8, 16, 128)],
        fine + [(5, 8, 16, 256)] + coef_shapes(FINE),
        place,
        first,
        second,
        below,
        above,
        name="down0",
    )
    left = shift(packed1, "brick", 1)
    right = shift(packed1, "brick", -1)
    up, down, centre = call(
        middle_cut,
        [(5, 5, 32, 128)] * 2 + [(5, 8, 32, 128)],
        [],
        place,
        packed1,
        left,
        right,
        name="cut1",
    )
    below = shift(up, "grp", 1)
    above = shift(down, "grp", -1)
    middle = [MIDDLE.shape(3)] * 3
    data1, saved1, packed2 = call(
        middle_down,
        [MIDDLE.shape(5), MIDDLE.shape(3), (5, 16, 128)],
        middle + [(5, 2, 32, 128), (5, 16, 256)] + coef_shapes(MIDDLE),
        place,
        centre,
        below,
        above,
        name="down1",
    )
    block = packed2[:, 6:10].reshape(1, 20, 128)
    parts = lax.all_to_all(
        jnp.broadcast_to(block, (lax.axis_size("brick"), 20, 128)), "brick", 0, 0
    )
    (column,) = call(column_kernel, [(5, 48, 128)], [], place, parts, name="column")
    parts = lax.all_to_all(
        jnp.broadcast_to(column[None], (lax.axis_size("grp"), 5, 48, 128)), "grp", 0, 0
    )
    coarse = [COARSE.shape(5)] + [COARSE.shape(3)] * 4 + coef_shapes(COARSE)
    last = [(5, 2, 24, 256), LAST.shape(5)] + [LAST.shape(3)] * 3 + coef_shapes(LAST)
    grown = [(3, 4, 48, 128), (3, 7, 32, 128), (3, 6, 32, 128)]
    (answer,) = call(
        climb,
        [(3, 16, 16, 128)],
        coarse + last + grown + middle + coef_shapes(MIDDLE) + fine + coef_shapes(FINE),
        place,
        parts,
        data1,
        saved1,
        data0,
        saved0,
        name="climb",
    )
    return answer


def solution(mesh):
    in_specs = (P(None, "grp", "brick", None), P("grp", "brick", None), P("grp", "brick", None))
    out_specs = P(None, "grp", "brick", None)
    return jax.shard_map(
        on_device, mesh=mesh, in_specs=in_specs, out_specs=out_specs, check_vma=False
    )
```

time: 640 us -> 184 us (0.29)
  the two profiles are of different devices: /device:TPU:22 before, /device:TPU:33 now
where the time goes in v1:
time: 184 us; the launch traced here: 183 us
  Pallas kernels  77.7 us (42%)
  blocking collectives  46.3 us (25%)
  starting transfers between devices  27.7 us (15%)
  waiting for transfers between devices  27.5 us (15%)
  local copies, waits for them, and re-layouts  3.97 us (2%)
    pallas_call x7, Pallas kernels, call(): pl.pallas_call(kernel, out_shape=[jax.ShapeDtypeStruct(s, F32) for s in o...  77.7 us
    ppermute x8, starting transfers between devices, shift(): lax.ppermute(value, axis, [(i, i + by) for i in range(count) if 0 <= i +...  27.7 us
    ppermute x8, waiting for transfers between devices, shift(): lax.ppermute(value, axis, [(i, i + by) for i in range(count) if 0 <= i +...  27.5 us
    all_to_all x1, blocking collectives, on_device(): lax.all_to_all(jnp.broadcast_to(block, (lax.axis_size('brick'), 20, 128))...  24.8 us
    all_to_all x1, blocking collectives, on_device(): lax.all_to_all(jnp.broadcast_to(column[None], (lax.axis_size('grp'), 5, 4...  21.5 us
    unnamed x10, local copies, waits for them, and re-layouts  3.86 us
  transfers between devices with their start and end apart: 8, of which 8 were waited for; matrix products, arithmetic and copies ran while one was open for 0% of the time, Pallas kernels for 0%

profile of v1, /device:TPU:33, one launch (start us, length us, event | category | flops | bytes accessed | tf_op | source)
XLA Modules:
  0.0 183.4 jit_solution(16871255927387298926)
XLA Ops:
  0.0 0.1 pad_add_fusion.place
  0.1 0.0 copy-start
  0.1 1.0 copy-done
  1.1 0.0 copy-start.3
  1.1 0.9 copy-done.3
  2.0 0.0 copy-start.4
  2.0 0.9 copy-done.4
  2.9 0.6 cut0.1
  3.5 3.5 %collective-permute-start = (f32[5,16,8,128]{3,2,1,0:T(8,128)S(1)}, f32[5,16,8,128]{3,2,1,0:T(8,128)S(1)}, u32[]{:S(2)}, u32[]{:S(2)}) collective-permute-start(f32[5,16,8,128]{3,2,1,0:T(8,128)S(1)} %get-tuple-element.18), channel_id=1, source_target_pairs={{0,1},{1,2},{2,3},{3,4},{4,5},{5,6},{6,7},{7,8},{8,9},{9,10},{10,1... | collective-permute-start | bytes 983048 | tf_op jit(solution)/shard_map/ppermute | solution.py:534
  7.0 1.9 %collective-permute-start.1 = (f32[5,16,8,128]{3,2,1,0:T(8,128)S(1)}, f32[5,16,8,128]{3,2,1,0:T(8,128)S(1)}, u32[]{:S(2)}, u32[]{:S(2)}) collective-permute-start(f32[5,16,8,128]{3,2,1,0:T(8,128)S(1)} %get-tuple-element.19), channel_id=1, source_target_pairs={{1,0},{2,1},{3,2},{4,3},{5,4},{6,5},{7,6},{8,7},{9,8},{10,9},{11,1... | collective-permute-start | bytes 983048 | tf_op jit(solution)/shard_map/ppermute | solution.py:534
  9.0 5.0 %collective-permute-done.lo = f32[5,16,8,128]{3,2,1,0:T(8,128)S(1)} collective-permute-done((f32[5,16,8,128]{3,2,1,0:T(8,128)S(1)}, f32[5,16,8,128]{3,2,1,0:T(8,128)S(1)}, u32[]{:S(2)}, u32[]{:S(2)}) %collective-permute-start) | collective-permute-done | bytes 327712 | tf_op jit(solution)/shard_map/ppermute | solution.py:534
  13.9 3.6 %collective-permute-done.1.hi = f32[5,16,8,128]{3,2,1,0:T(8,128)S(1)} collective-permute-done((f32[5,16,8,128]{3,2,1,0:T(8,128)S(1)}, f32[5,16,8,128]{3,2,1,0:T(8,128)S(1)}, u32[]{:S(2)}, u32[]{:S(2)}) %collective-permute-start.1) | collective-permute-done | bytes 327712 | tf_op jit(solution)/shard_map/ppermute | solution.py:534
  17.6 0.6 join0.1
  18.2 3.6 %collective-permute-start.3 = (f32[5,8,32,128]{3,2,1,0:T(8,128)S(1)}, f32[5,8,32,128]{3,2,1,0:T(8,128)S(1)}, u32[]{:S(2)}, u32[]{:S(2)}) collective-permute-start(f32[5,8,32,128]{3,2,1,0:T(8,128)S(1)} %get-tuple-element.20.first), channel_id=1, source_target_pairs={{32,0},{64,32},{96,64},{128,96},{160,128},{192,160},{224,192},{33,... | collective-permute-start | bytes 1966088 | tf_op jit(solution)/shard_map/ppermute | solution.py:534
  21.8 3.1 %collective-permute-start.2 = (f32[5,8,32,128]{3,2,1,0:T(8,128)S(1)}, f32[5,8,32,128]{3,2,1,0:T(8,128)S(1)}, u32[]{:S(2)}, u32[]{:S(2)}) collective-permute-start(f32[5,8,32,128]{3,2,1,0:T(8,128)S(1)} %get-tuple-element.21.second), channel_id=1, source_target_pairs={{0,32},{32,64},{64,96},{96,128},{128,160},{160,192},{192,224},{1,3... | collective-permute-start | bytes 1966088 | tf_op jit(solution)/shard_map/ppermute | solution.py:534
  24.9 6.3 %collective-permute-done.3.hi = f32[5,8,32,128]{3,2,1,0:T(8,128)S(1)} collective-permute-done((f32[5,8,32,128]{3,2,1,0:T(8,128)S(1)}, f32[5,8,32,128]{3,2,1,0:T(8,128)S(1)}, u32[]{:S(2)}, u32[]{:S(2)}) %collective-permute-start.3) | collective-permute-done | bytes 655392 | tf_op jit(solution)/shard_map/ppermute | solution.py:534
  31.2 1.2 collective-permute-done.2.lo
  32.4 20.4 %down0.1 = (f32[5,32,32,128]{3,2,1,0:T(8,128)}, f32[3,24,32,128]{3,2,1,0:T(8,128)}, f32[5,8,16,128]{3,2,1,0:T(8,128)S(1)}) custom-call(s32[4]{0:T(128)S(1)} %pad_add_fusion.place, f32[5,8,32,128]{3,2,1,0:T(8,128)S(1)} %get-tuple-element.20.first, f32[5,8,32,128]{3,2,1,0:T(8,128)S(1)} %get-tuple-element.21.second, ...), custom_call_target="tpu_custom_call" | custom-call | tf_op jit(solution)/shard_map/down0/pallas_call | solution.py:203
  52.8 1.9 %collective-permute-start.5 = (f32[5,8,16,128]{3,2,1,0:T(8,128)S(1)}, f32[5,8,16,128]{3,2,1,0:T(8,128)S(1)}, u32[]{:S(2)}, u32[]{:S(2)}) collective-permute-start(f32[5,8,16,128]{3,2,1,0:T(8,128)S(1)} %get-tuple-element.22.own), channel_id=1, source_target_pairs={{1,0},{2,1},{3,2},{4,3},{5,4},{6,5},{7,6},{8,7},{9,8},{10,9},{11,1... | collective-permute-start | bytes 983048 | tf_op jit(solution)/shard_map/ppermute | solution.py:534
  54.7 4.8 %collective-permute-start.4 = (f32[5,8,16,128]{3,2,1,0:T(8,128)S(1)}, f32[5,8,16,128]{3,2,1,0:T(8,128)S(1)}, u32[]{:S(2)}, u32[]{:S(2)}) collective-permute-start(f32[5,8,16,128]{3,2,1,0:T(8,128)S(1)} %get-tuple-element.22.own), channel_id=1, source_target_pairs={{0,1},{1,2},{2,3},{3,4},{4,5},{5,6},{6,7},{7,8},{8,9},{9,10},{10,1... | collective-permute-start | bytes 983048 | tf_op jit(solution)/shard_map/ppermute | solution.py:534
  59.5 2.5 %collective-permute-done.5.right = f32[5,8,16,128]{3,2,1,0:T(8,128)S(1)} collective-permute-done((f32[5,8,16,128]{3,2,1,0:T(8,128)S(1)}, f32[5,8,16,128]{3,2,1,0:T(8,128)S(1)}, u32[]{:S(2)}, u32[]{:S(2)}) %collective-permute-start.5) | collective-permute-done | bytes 327712 | tf_op jit(solution)/shard_map/ppermute | solution.py:534
  62.0 1.5 collective-permute-done.4.left
  63.5 0.7 cut1.1
  64.2 7.0 %collective-permute-start.6 = (f32[5,5,32,128]{3,2,1,0:T(8,128)S(1)}, f32[5,5,32,128]{3,2,1,0:T(8,128)S(1)}, u32[]{:S(2)}, u32[]{:S(2)}) collective-permute-start(f32[5,5,32,128]{3,2,1,0:T(8,128)S(1)} %get-tuple-element.24), channel_id=1, source_target_pairs={{0,32},{32,64},{64,96},{96,128},{128,160},{160,192},{192,224},{1,3... | collective-permute-start | bytes 1228808 | tf_op jit(solution)/shard_map/ppermute | solution.py:534
  71.2 1.9 %collective-permute-start.7 = (f32[5,5,32,128]{3,2,1,0:T(8,128)S(1)}, f32[5,5,32,128]{3,2,1,0:T(8,128)S(1)}, u32[]{:S(2)}, u32[]{:S(2)}) collective-permute-start(f32[5,5,32,128]{3,2,1,0:T(8,128)S(1)} %get-tuple-element.25), channel_id=1, source_target_pairs={{32,0},{64,32},{96,64},{128,96},{160,128},{192,160},{224,192},{33,... | collective-permute-start | bytes 1228808 | tf_op jit(solution)/shard_map/ppermute | solution.py:534
  73.1 2.9 %collective-permute-done.6.lo = f32[5,5,32,128]{3,2,1,0:T(8,128)S(1)} collective-permute-done((f32[5,5,32,128]{3,2,1,0:T(8,128)S(1)}, f32[5,5,32,128]{3,2,1,0:T(8,128)S(1)}, u32[]{:S(2)}, u32[]{:S(2)}) %collective-permute-start.6) | collective-permute-done | bytes 409632 | tf_op jit(solution)/shard_map/ppermute | solution.py:534
  76.1 4.4 %collective-permute-done.7.hi = f32[5,5,32,128]{3,2,1,0:T(8,128)S(1)} collective-permute-done((f32[5,5,32,128]{3,2,1,0:T(8,128)S(1)}, f32[5,5,32,128]{3,2,1,0:T(8,128)S(1)}, u32[]{:S(2)}, u32[]{:S(2)}) %collective-permute-start.7) | collective-permute-done | bytes 409632 | tf_op jit(solution)/shard_map/ppermute | solution.py:534
  80.5 10.8 %down1.1 = (f32[5,16,32,128]{3,2,1,0:T(8,128)S(1)}, f32[3,16,32,128]{3,2,1,0:T(8,128)S(1)}, f32[5,16,128]{2,1,0:T(8,128)S(1)}) custom-call(s32[4]{0:T(128)S(1)} %pad_add_fusion.place, f32[5,8,32,128]{3,2,1,0:T(8,128)S(1)} %get-tuple-element.23.centre, f32[5,5,32,128]{3,2,1,0:T(8,128)S(1)} %collective-permute-done.6.lo, ...), custom_call_target="tpu_custom_call" | custom-call | tf_op jit(solution)/shard_map/down1/pallas_call | solution.py:203
  91.3 0.0 copy-start.1
  91.3 1.1 copy-done.1
  92.4 24.8 %all_to_all.10.parts = f32[32,20,128]{2,1,0:T(8,128)S(1)} all-to-all(f32[32,20,128]{2,1,0:T(8,128)S(1)} %broadcast_in_dim.14), channel_id=1, replica_groups=mesh['grp'=8,'brick'=32] {'brick'}, dimensions={0} | all-to-all | bytes 655360 | tf_op jit(solution)/shard_map/all_to_all | solution.py:595
  117.2 0.6 column.1
  117.8 0.0 copy-start.2
  117.8 0.1 broadcast_in_dim.15
  117.9 21.5 %all_to_all.11.parts = f32[8,5,48,128]{3,2,1,0:T(8,128)S(1)} all-to-all(f32[8,5,48,128]{3,2,1,0:T(8,128)S(1)} %broadcast_in_dim.15), channel_id=1, replica_groups=mesh['grp'=8,'brick'=32] {'grp'}, dimensions={0} | all-to-all | bytes 1966080 | tf_op jit(solution)/shard_map/all_to_all | solution.py:599
  139.4 0.0 copy-done.2
  139.4 44.0 %climb.1 = f32[3,16,16,128]{3,2,1,0:T(8,128)} custom-call(s32[4]{0:T(128)S(1)} %pad_add_fusion.place, f32[8,5,48,128]{3,2,1,0:T(8,128)S(1)} %all_to_all.11.parts, f32[5,16,32,128]{3,2,1,0:T(8,128)} %copy-done.1, f32[3,16,32,128]{3,2,1,0:T(8,128)S(1)} %get-tuple-element.28.saved1, f32[5,32,32,128]{3,2,1,0:T(8,128)} %get-tuple-element.29.data0, ...), custom_call_target="tpu_custom_call" | custom-call | tf_op jit(solution)/shard_map/climb/pallas_call | solution.py:203
  (3 shorter events, 0.0 us)
Async XLA Ops:
  0.1 1.0 copy-start
  1.1 0.9 copy-start.3
  2.0 0.9 copy-start.4
  3.5 10.5 %collective-permute-start = (f32[5,16,8,128]{3,2,1,0:T(8,128)S(1)}, f32[5,16,8,128]{3,2,1,0:T(8,128)S(1)}, u32[]{:S(2)}, u32[]{:S(2)}) collective-permute-start(f32[5,16,8,128]{3,2,1,0:T(8,128)S(1)} %get-tuple-element.18), channel_id=1, source_target_pairs={{0,1},{1,2},{2,3},{3,4},{4,5},{5,6},{6,7},{7,8},{8,9},{9,10},{10,1... | collective-permute-start | bytes 983048 | tf_op jit(solution)/shard_map/ppermute | solution.py:534
  7.0 10.5 %collective-permute-start.1 = (f32[5,16,8,128]{3,2,1,0:T(8,128)S(1)}, f32[5,16,8,128]{3,2,1,0:T(8,128)S(1)}, u32[]{:S(2)}, u32[]{:S(2)}) collective-permute-start(f32[5,16,8,128]{3,2,1,0:T(8,128)S(1)} %get-tuple-element.19), channel_id=1, source_target_pairs={{1,0},{2,1},{3,2},{4,3},{5,4},{6,5},{7,6},{8,7},{9,8},{10,9},{11,1... | collective-permute-start | bytes 983048 | tf_op jit(solution)/shard_map/ppermute | solution.py:534
  18.2 13.0 %collective-permute-start.3 = (f32[5,8,32,128]{3,2,1,0:T(8,128)S(1)}, f32[5,8,32,128]{3,2,1,0:T(8,128)S(1)}, u32[]{:S(2)}, u32[]{:S(2)}) collective-permute-start(f32[5,8,32,128]{3,2,1,0:T(8,128)S(1)} %get-tuple-element.20.first), channel_id=1, source_target_pairs={{32,0},{64,32},{96,64},{128,96},{160,128},{192,160},{224,192},{33,... | collective-permute-start | bytes 1966088 | tf_op jit(solution)/shard_map/ppermute | solution.py:534
  21.8 10.6 %collective-permute-start.2 = (f32[5,8,32,128]{3,2,1,0:T(8,128)S(1)}, f32[5,8,32,128]{3,2,1,0:T(8,128)S(1)}, u32[]{:S(2)}, u32[]{:S(2)}) collective-permute-start(f32[5,8,32,128]{3,2,1,0:T(8,128)S(1)} %get-tuple-element.21.second), channel_id=1, source_target_pairs={{0,32},{32,64},{64,96},{96,128},{128,160},{160,192},{192,224},{1,3... | collective-permute-start | bytes 1966088 | tf_op jit(solution)/shard_map/ppermute | solution.py:534
  52.8 9.2 %collective-permute-start.5 = (f32[5,8,16,128]{3,2,1,0:T(8,128)S(1)}, f32[5,8,16,128]{3,2,1,0:T(8,128)S(1)}, u32[]{:S(2)}, u32[]{:S(2)}) collective-permute-start(f32[5,8,16,128]{3,2,1,0:T(8,128)S(1)} %get-tuple-element.22.own), channel_id=1, source_target_pairs={{1,0},{2,1},{3,2},{4,3},{5,4},{6,5},{7,6},{8,7},{9,8},{10,9},{11,1... | collective-permute-start | bytes 983048 | tf_op jit(solution)/shard_map/ppermute | solution.py:534
  54.7 8.8 %collective-permute-start.4 = (f32[5,8,16,128]{3,2,1,0:T(8,128)S(1)}, f32[5,8,16,128]{3,2,1,0:T(8,128)S(1)}, u32[]{:S(2)}, u32[]{:S(2)}) collective-permute-start(f32[5,8,16,128]{3,2,1,0:T(8,128)S(1)} %get-tuple-element.22.own), channel_id=1, source_target_pairs={{0,1},{1,2},{2,3},{3,4},{4,5},{5,6},{6,7},{7,8},{8,9},{9,10},{10,1... | collective-permute-start | bytes 983048 | tf_op jit(solution)/shard_map/ppermute | solution.py:534
  64.2 11.9 %collective-permute-start.6 = (f32[5,5,32,128]{3,2,1,0:T(8,128)S(1)}, f32[5,5,32,128]{3,2,1,0:T(8,128)S(1)}, u32[]{:S(2)}, u32[]{:S(2)}) collective-permute-start(f32[5,5,32,128]{3,2,1,0:T(8,128)S(1)} %get-tuple-element.24), channel_id=1, source_target_pairs={{0,32},{32,64},{64,96},{96,128},{128,160},{160,192},{192,224},{1,3... | collective-permute-start | bytes 1228808 | tf_op jit(solution)/shard_map/ppermute | solution.py:534
  71.2 9.3 %collective-permute-start.7 = (f32[5,5,32,128]{3,2,1,0:T(8,128)S(1)}, f32[5,5,32,128]{3,2,1,0:T(8,128)S(1)}, u32[]{:S(2)}, u32[]{:S(2)}) collective-permute-start(f32[5,5,32,128]{3,2,1,0:T(8,128)S(1)} %get-tuple-element.25), channel_id=1, source_target_pairs={{32,0},{64,32},{96,64},{128,96},{160,128},{192,160},{224,192},{33,... | collective-permute-start | bytes 1228808 | tf_op jit(solution)/shard_map/ppermute | solution.py:534
  91.3 1.1 copy-start.1
  117.8 21.6 %copy-start.2 = (f32[3,24,32,128]{3,2,1,0:T(8,128)S(1)}, f32[3,24,32,128]{3,2,1,0:T(8,128)}, u32[]{:S(2)}) copy-start(f32[3,24,32,128]{3,2,1,0:T(8,128)} %get-tuple-element.30.saved0) | copy-start | bytes 3538948

commit v2 on v1

--- a/solution.py
+++ b/solution.py
@@ -106,7 +106,7 @@
         inv[i] = jnp.where(inside(i), 1.0 / (total + 2.0 * BETA * level.scale), 0.0)
         return 0
 
-    lax.fori_loop(lo, hi, body, 0)
+    lax.fori_loop(lo, hi, body, 0, unroll=2)
 
 
 def begin(level, src, coef, state, direction, lo, hi):
@@ -120,7 +120,7 @@
             direction[c, i] = value
         return 0
 
-    lax.fori_loop(lo, hi, body, 0)
+    lax.fori_loop(lo, hi, body, 0, unroll=2)
     for c in range(3):
         ghosts(level, state, (c,))
 
@@ -155,7 +155,7 @@
             emit(i, c, u, resid)
         return here
 
-    lax.fori_loop(lo, hi, body, spread(lo - 1))
+    lax.fori_loop(lo, hi, body, spread(lo - 1), unroll=4)
 
 
 def step(level, number, src, coef, state, fresh, direction, lo, hi):
@@ -206,26 +206,61 @@
         in_specs=[smem] + vmem(len(args) - 1),
         out_specs=vmem(len(outs)),
         scratch_shapes=[pltpu.VMEM(s, F32) for s in scratch],
-        compiler_params=pltpu.CompilerParams(vmem_limit_bytes=50 * 2**20),
+        compiler_params=pltpu.CompilerParams(vmem_limit_bytes=28 * 2**20),
         name=name,
     )(*args)
 
 
-def cut_kernel(place, f, k, r, lo, hi):
-    for q in range(5):
-        part = (lambda s: f[q, :, s]) if q < 3 else (lambda s: (k, r)[q - 3][:, s])
-        lo[q] = part(slice(0, HALO))
-        hi[q] = part(slice(HALO, 2 * HALO))
-
-
-def join_kernel(place, f, k, r, lo, hi, first, second):
-    for q in range(5):
-        for half, out in enumerate((first, second)):
+def cut_kernel(f, k, r, own, lo, hi, sems):
+    copies = [
+        pltpu.make_async_copy(f, own.at[0:3], sems.at[0]),
+        pltpu.make_async_copy(k, own.at[3], sems.at[1]),
+        pltpu.make_async_copy(r, own.at[4], sems.at[2]),
+    ]
+    for copy in copies:
+        copy.start()
+    for copy in copies:
+        copy.wait()
+    lo[...] = own[:, :, 0:HALO]
+    hi[...] = own[:, :, HALO : 2 * HALO]
+
+
+def cut(f, k, r):
+    block = (5, 16, 16, LANES)
+    strip = (5, 16, HALO, LANES)
+    return pl.pallas_call(
+        cut_kernel,
+        out_shape=[jax.ShapeDtypeStruct(shape, F32) for shape in (block, strip, strip)],
+        in_specs=[pl.BlockSpec(memory_space=pl.ANY)] * 3,
+        out_specs=vmem(3),
+        scratch_shapes=[pltpu.SemaphoreType.DMA((3,))],
+        compiler_params=pltpu.CompilerParams(vmem_limit_bytes=28 * 2**20),
+        name="cut0",
+    )(f, k, r)
+
+
+def by_parity(place, act):
+    odd = place[0] % 2
+
+    @pl.when(odd == 0)
+    def _():
+        act(True)
+
+    @pl.when(odd == 1)
+    def _():
+        act(False)
+
+
+def join_kernel(place, own, lo, hi, near, far):
+    def act(even):
+        for half, out in enumerate((far, near) if even else (near, far)):
             rows = slice(8 * half, 8 * half + 8)
-            part = f[q, rows] if q < 3 else (k, r)[q - 3][rows]
-            out[q, :, 0:8] = lo[q, rows]
-            out[q, :, 8:24] = part
-            out[q, :, 24:32] = hi[q, rows]
+            for q in range(5):
+                out[q, :, 0:8] = lo[q, rows]
+                out[q, :, 8:24] = own[q, rows]
+                out[q, :, 24:32] = hi[q, rows]
+
+    by_parity(place, act)
 
 
 FINE = Level(1.0, 128, 30, 32)
@@ -249,12 +284,15 @@
     return inside
 
 
-def fine_down(place, first, second, lo, hi, data, saved, packed, s0, d0, t0, sums, *coef):
-    for q in range(5):
-        data[q, 0:8] = lo[q]
-        data[q, 8:16] = first[q]
-        data[q, 16:24] = second[q]
-        data[q, 24:32] = hi[q]
+def fine_down(place, near, far, near_in, far_in, data, saved, packed, kept, s0, d0, t0, sums):
+    coef = [kept.at[j] for j in range(7)]
+
+    def act(even):
+        order = (far_in, far, near, near_in) if even else (near_in, near, far, far_in)
+        for number, part in enumerate(order):
+            data[:, 8 * number : 8 * number + 8] = part[...]
+
+    by_parity(place, act)
     inside = fine_inside(place)
     setup(FINE, lambda i: data[3, i], lambda i: data[4, i], coef, inside, 1, 31)
     begin(FINE, data, coef, s0, d0, 1, 31)
@@ -283,7 +321,7 @@
     packed[...] = mix(wide[...].reshape(5 * 8 * 16, 2 * LANES), matrix).reshape(5, 8, 16, LANES)
 
 
-def middle_cut(place, own, left, right, up, down, centre):
+def middle_cut(place, own, left, right, near, far, centre):
     lane = lane_of((32, LANES))
 
     for q in range(5):
@@ -291,11 +329,17 @@
             centre[q, i, 0:12] = left[q, i, 0:12]
             centre[q, i, 12:20] = own[q, i, 4:12]
             centre[q, i, 20:32] = right[q, i, 4:16]
-        for t in range(5):
-            tail = pltpu.roll(centre[q, 7], 64, 1) if t == 0 else centre[q, t - 1]
-            up[q, t] = jnp.where(lane < 64, centre[q, 2 + t], tail)
-            head = pltpu.roll(centre[q, 0], 64, 1) if t == 4 else centre[q, 4 + t]
-            down[q, t] = jnp.where(lane < 64, head, centre[q, 1 + t])
+
+    def act(even):
+        up, down = (near, far) if even else (far, near)
+        for q in range(5):
+            for t in range(5):
+                tail = pltpu.roll(centre[q, 7], 64, 1) if t == 0 else centre[q, t - 1]
+                up[q, t] = jnp.where(lane < 64, centre[q, 2 + t], tail)
+                head = pltpu.roll(centre[q, 0], 64, 1) if t == 4 else centre[q, 4 + t]
+                down[q, t] = jnp.where(lane < 64, head, centre[q, 1 + t])
+
+    by_parity(place, act)
 
 
 def middle_inside(place):
@@ -310,9 +354,8 @@
     return inside
 
 
-def middle_down(place, centre, lo, hi, data, saved, packed, s1, d1, t1, pair, sums, *coef):
-    lane = lane_of((32, LANES))
-    low = lane < 64
+def middle_join(centre, lo, hi, data):
+    low = lane_of((32, LANES)) < 64
     for q in range(5):
         for i in range(14):
             if i < 5:
@@ -329,6 +372,13 @@
                 b = hi[q, i - 9]
             data[q, i + 1] = jnp.where(low, a, b)
         ghosts(MIDDLE, data, (q,))
+
+
+def middle_down(place, centre, near, far, data, saved, packed, kept, s1, d1, t1, pair, sums):
+    coef = [kept.at[j] for j in range(7)]
+    lane = lane_of((32, LANES))
+    low = lane < 64
+    by_parity(place, lambda even: middle_join(centre, *((far, near) if even else (near, far)), data))
     setup(MIDDLE, lambda i: data[3, i], lambda i: data[4, i], coef, middle_inside(place), 1, 15)
     begin(MIDDLE, data, coef, s1, d1, 1, 15)
     step(MIDDLE, 1, data, coef, s1, t1, d1, 1, 15)
@@ -362,7 +412,7 @@
         valid = (at >= 0) & (at < place[3])
         safe = jnp.clip(at, 0, place[3] - 1)
         for q in range(5):
-            block = parts[safe, 4 * q : 4 * q + 4]
+            block = parts[safe, q]
             out[q, 2 + 4 * d : 6 + 4 * d] = jnp.where(valid, block, zero)
 
 
@@ -379,7 +429,7 @@
     return lambda i: fits
 
 
-def climb(place, parts, data1, saved1, data0, saved0, out, *scratch):
+def climb(place, mine, other, data1, saved1, kept1, data0, saved0, kept0, out, *scratch):
     scratch = list(scratch)
 
     def take(count):
@@ -393,22 +443,26 @@
     coef3 = take(7)
     grown3, grown2, grown1 = take(3)
     s1, t1, d1 = take(3)
-    coef1 = take(7)
     s0, t0, d0 = take(3)
-    coef0 = take(7)
-
-    lane = lane_of((48, LANES))
-    group = lane // 32
-    for q in range(5):
-        for i in range(8):
-            row = None
-            for g in range(4):
-                block = parts[2 * g + i // 4, q]
-                shift = ((g - i % 4) * 32) % LANES
-                block = pltpu.roll(block, shift, 1) if shift else block
-                row = block if row is None else jnp.where(group == g, block, row)
-            data2[q, i + 1] = row
-        ghosts(COARSE, data2, (q,))
+    coef1 = [kept1.at[j] for j in range(7)]
+    coef0 = [kept0.at[j] for j in range(7)]
+
+    group = lane_of((48, LANES)) // 32
+
+    def act(even):
+        order = (mine, other) if even else (other, mine)
+        for q in range(5):
+            for i in range(8):
+                row = None
+                for g in range(4):
+                    block = order[i // 4][g, q]
+                    shift = ((g - i % 4) * 32) % LANES
+                    block = pltpu.roll(block, shift, 1) if shift else block
+                    row = block if row is None else jnp.where(group == g, block, row)
+                data2[q, i + 1] = row
+            ghosts(COARSE, data2, (q,))
+
+    by_parity(place, act)
     setup(COARSE, lambda i: data2[3, i], lambda i: data2[4, i], coef2, coarse_inside(place), 1, 9)
     begin(COARSE, data2, coef2, s2, d2, 1, 9)
     step(COARSE, 1, data2, coef2, s2, t2, d2, 1, 9)
@@ -464,7 +518,6 @@
     step(COARSE, 2, data2, coef2, s2, t2, d2, 1, 9)
     step(COARSE, 3, data2, coef2, t2, s2, d2, 1, 9)
 
-    setup(MIDDLE, lambda i: data1[3, i], lambda i: data1[4, i], coef1, middle_inside(place), 1, 15)
     matrix = pick(
         LANES,
         LANES,
@@ -501,7 +554,6 @@
     step(MIDDLE, 2, data1, coef1, s1, t1, d1, 1, 15)
     step(MIDDLE, 3, data1, coef1, t1, s1, d1, 1, 15)
 
-    setup(FINE, lambda i: data0[3, i], lambda i: data0[4, i], coef0, fine_inside(place), 5, 27)
     for half in range(2):
         matrix = pick(LANES, LANES, lambda a, b: a == 64 * half + b // 2, 1.0)
         rows = [9 + t for t in range(6)] if half == 0 else [1 + t for t in range(6)]
@@ -536,39 +588,39 @@
     )
 
 
+def swap(value, first):
+    count = lax.axis_size("grp")
+    ends = [(i, i + 1) for i in range(first, count - 1, 2)]
+    return lax.ppermute(value, "grp", ends + [(b, a) for a, b in ends])
+
+
 def on_device(right_side, stiffness, reaction):
+    bricks = lax.axis_size("brick")
+    count = lax.axis_size("grp")
     place = jnp.stack(
-        [
-            lax.axis_index("grp"),
-            lax.axis_index("brick"),
-            jnp.int32(lax.axis_size("grp")),
-            jnp.int32(lax.axis_size("brick")),
-        ]
+        [lax.axis_index("grp"), lax.axis_index("brick"), jnp.int32(count), jnp.int32(bricks)]
     ).astype(jnp.int32)
-    local = (right_side, stiffness, reaction)
-    low, high = call(cut_kernel, [(5, 16, 8, 128)] * 2, [], place, *local, name="cut0")
+    own, low, high = cut(right_side, stiffness, reaction)
     left = shift(high, "brick", 1)
     right = shift(low, "brick", -1)
-    first, second = call(
-        join_kernel, [(5, 8, 32, 128)] * 2, [], place, *local, left, right, name="join0"
-    )
-    below = shift(second, "grp", 1)
-    above = shift(first, "grp", -1)
+    near, far = call(join_kernel, [(5, 8, 32, 128)] * 2, [], place, own, left, right, name="join0")
+    far_in = swap(far, 1)
+    near_in = swap(near, 0)
     fine = [FINE.shape(3)] * 3
-    data0, saved0, packed1 = call(
+    data0, saved0, packed1, kept0 = call(
         fine_down,
-        [FINE.shape(5), (3, 24, 32, 128), (5, 8, 16, 128)],
-        fine + [(5, 8, 16, 256)] + coef_shapes(FINE),
+        [FINE.shape(5), (3, 24, 32, 128), (5, 8, 16, 128), FINE.shape(7)],
+        fine + [(5, 8, 16, 256)],
         place,
-        first,
-        second,
-        below,
-        above,
+        near,
+        far,
+        near_in,
+        far_in,
         name="down0",
     )
     left = shift(packed1, "brick", 1)
     right = shift(packed1, "brick", -1)
-    up, down, centre = call(
+    near, far, centre = call(
         middle_cut,
         [(5, 5, 32, 128)] * 2 + [(5, 8, 32, 128)],
         [],
@@ -578,40 +630,46 @@
         right,
         name="cut1",
     )
-    below = shift(up, "grp", 1)
-    above = shift(down, "grp", -1)
+    far_in = swap(far, 1)
+    near_in = swap(near, 0)
     middle = [MIDDLE.shape(3)] * 3
-    data1, saved1, packed2 = call(
+    data1, saved1, packed2, kept1 = call(
         middle_down,
-        [MIDDLE.shape(5), MIDDLE.shape(3), (5, 16, 128)],
-        middle + [(5, 2, 32, 128), (5, 16, 256)] + coef_shapes(MIDDLE),
+        [MIDDLE.shape(5), MIDDLE.shape(3), (5, 16, 128), MIDDLE.shape(7)],
+        middle + [(5, 2, 32, 128), (5, 16, 256)],
         place,
         centre,
-        below,
-        above,
+        near_in,
+        far_in,
         name="down1",
     )
-    block = packed2[:, 6:10].reshape(1, 20, 128)
-    parts = lax.all_to_all(
-        jnp.broadcast_to(block, (lax.axis_size("brick"), 20, 128)), "brick", 0, 0
-    )
+    block = packed2[:, 6:10]
+    parts = lax.all_to_all(jnp.broadcast_to(block[None], (bricks, 5, 4, 128)), "brick", 0, 0)
     (column,) = call(column_kernel, [(5, 48, 128)], [], place, parts, name="column")
-    parts = lax.all_to_all(
-        jnp.broadcast_to(column[None], (lax.axis_size("grp"), 5, 48, 128)), "grp", 0, 0
-    )
+    mine = lax.all_to_all(
+        jnp.broadcast_to(column[None], (count // 2, 5, 48, 128)),
+        "grp",
+        0,
+        0,
+        axis_index_groups=[list(range(core, count, 2)) for core in range(2)],
+    )
+    other = swap(mine, 0)
     coarse = [COARSE.shape(5)] + [COARSE.shape(3)] * 4 + coef_shapes(COARSE)
     last = [(5, 2, 24, 256), LAST.shape(5)] + [LAST.shape(3)] * 3 + coef_shapes(LAST)
     grown = [(3, 4, 48, 128), (3, 7, 32, 128), (3, 6, 32, 128)]
     (answer,) = call(
         climb,
         [(3, 16, 16, 128)],
-        coarse + last + grown + middle + coef_shapes(MIDDLE) + fine + coef_shapes(FINE),
+        coarse + last + grown + middle + fine,
         place,
-        parts,
+        mine,
+        other,
         data1,
         saved1,
+        kept1,
         data0,
         saved0,
+        kept0,
         name="climb",
     )
     return answer

time: 184 us -> 141 us (0.77)
  Pallas kernels: 77.7 us -> 44.5 us
  blocking collectives: 46.3 us -> 37.6 us
    pallas_call x7 -> x6, Pallas kernels: 77.7 us -> 44 us  [call(): pl.pallas_call(kernel, out_shape=[jax.ShapeDtypeStruct(s, F32) for s in o...]
    ppermute x0 -> x5, waiting for transfers between devices: none -> 15.9 us  [swap(): return lax.ppermute(value, 'grp', ends + [(b, a) for a, b in ends])]
    ppermute x8 -> x4, starting transfers between devices: 27.7 us -> 12.1 us  [shift(): lax.ppermute(value, axis, [(i, i + by) for i in range(count) if 0 <= i +...]
    ppermute x0 -> x5, starting transfers between devices: none -> 15.1 us  [swap(): return lax.ppermute(value, 'grp', ends + [(b, a) for a, b in ends])]
    ppermute x8 -> x4, waiting for transfers between devices: 27.5 us -> 12.5 us  [shift(): lax.ppermute(value, axis, [(i, i + by) for i in range(count) if 0 <= i +...]
    all_to_all x2, blocking collectives: 46.3 us -> 37.6 us  [the longest x1 23.9 us: on_device(): lax.all_to_all(jnp.broadcast_to(block[None], (bricks, 5, 4, 128)), 'brick...]
    unnamed x10 -> x6, local copies, waits for them, and re-layouts: 3.86 us -> 2.8 us
  transfers between devices with their start and end apart: 8 -> 9, of which waited for: 8 -> 7; matrix products, arithmetic and copies ran while one was open for 0% -> 0% of each run, Pallas kernels for 0% -> 0%
where the time goes in v2:
time: 141 us
  Pallas kernels  44.5 us (32%)
  blocking collectives  37.6 us (27%)
  waiting for transfers between devices  28.4 us (20%)
  starting transfers between devices  27.3 us (19%)
  local copies, waits for them, and re-layouts  2.89 us (2%)
    pallas_call x6, Pallas kernels, call(): pl.pallas_call(kernel, out_shape=[jax.ShapeDtypeStruct(s, F32) for s in o...  44 us
    all_to_all x1, blocking collectives, on_device(): lax.all_to_all(jnp.broadcast_to(block[None], (bricks, 5, 4, 128)), 'brick...  23.9 us
    ppermute x5, waiting for transfers between devices, swap(): return lax.ppermute(value, 'grp', ends + [(b, a) for a, b in ends])  15.9 us
    ppermute x5, starting transfers between devices, swap(): return lax.ppermute(value, 'grp', ends + [(b, a) for a, b in ends])  15.1 us
    all_to_all x1, blocking collectives, on_device(): lax.all_to_all(jnp.broadcast_to(column[None], (count // 2, 5, 48, 128)),...  13.7 us
    ppermute x4, waiting for transfers between devices, shift(): lax.ppermute(value, axis, [(i, i + by) for i in range(count) if 0 <= i +...  12.5 us
    ppermute x4, starting transfers between devices, shift(): lax.ppermute(value, axis, [(i, i + by) for i in range(count) if 0 <= i +...  12.1 us
  transfers between devices with their start and end apart: 9, of which 7 were waited for; matrix products, arithmetic and copies ran while one was open for 0% of the time, Pallas kernels for 0%

profile of v2, /device:TPU:33, one launch (start us, length us, event | category | flops | bytes accessed | tf_op | source)
XLA Modules:
  0.0 140.9 jit_solution(9769232191627594493)
XLA Ops:
  0.0 0.0 copy-start
  0.0 1.0 copy-done
  1.0 0.0 copy-start.1
  1.0 0.9 copy-done.1
  1.9 0.0 copy-start.2
  1.9 0.9 copy-done.2
  2.8 0.6 cut0.1
  3.4 3.5 %collective-permute-start = (f32[5,16,8,128]{3,2,1,0:T(8,128)S(1)}, f32[5,16,8,128]{3,2,1,0:T(8,128)S(1)}, u32[]{:S(2)}, u32[]{:S(2)}) collective-permute-start(f32[5,16,8,128]{3,2,1,0:T(8,128)S(1)} %get-tuple-element.22), channel_id=1, source_target_pairs={{0,1},{1,2},{2,3},{3,4},{4,5},{5,6},{6,7},{7,8},{8,9},{9,10},{10,1... | collective-permute-start | bytes 983048 | tf_op jit(solution)/shard_map/ppermute | solution.py:586
  7.0 1.9 %collective-permute-start.1 = (f32[5,16,8,128]{3,2,1,0:T(8,128)S(1)}, f32[5,16,8,128]{3,2,1,0:T(8,128)S(1)}, u32[]{:S(2)}, u32[]{:S(2)}) collective-permute-start(f32[5,16,8,128]{3,2,1,0:T(8,128)S(1)} %get-tuple-element.23), channel_id=1, source_target_pairs={{1,0},{2,1},{3,2},{4,3},{5,4},{6,5},{7,6},{8,7},{9,8},{10,9},{11,1... | collective-permute-start | bytes 983048 | tf_op jit(solution)/shard_map/ppermute | solution.py:586
  8.9 0.1 pad_add_fusion.place
  9.0 4.9 %collective-permute-done.lo = f32[5,16,8,128]{3,2,1,0:T(8,128)S(1)} collective-permute-done((f32[5,16,8,128]{3,2,1,0:T(8,128)S(1)}, f32[5,16,8,128]{3,2,1,0:T(8,128)S(1)}, u32[]{:S(2)}, u32[]{:S(2)}) %collective-permute-start) | collective-permute-done | bytes 327712 | tf_op jit(solution)/shard_map/ppermute | solution.py:586
  13.9 3.6 %collective-permute-done.1.hi = f32[5,16,8,128]{3,2,1,0:T(8,128)S(1)} collective-permute-done((f32[5,16,8,128]{3,2,1,0:T(8,128)S(1)}, f32[5,16,8,128]{3,2,1,0:T(8,128)S(1)}, u32[]{:S(2)}, u32[]{:S(2)}) %collective-permute-start.1) | collective-permute-done | bytes 327712 | tf_op jit(solution)/shard_map/ppermute | solution.py:586
  17.5 0.6 join0.1
  18.2 1.7 %collective-permute-start.2 = (f32[5,8,32,128]{3,2,1,0:T(8,128)S(1)}, f32[5,8,32,128]{3,2,1,0:T(8,128)S(1)}, u32[]{:S(2)}, u32[]{:S(2)}) collective-permute-start(f32[5,8,32,128]{3,2,1,0:T(8,128)S(1)} %get-tuple-element.24.near), channel_id=1, source_target_pairs={{0,32},{64,96},{128,160},{192,224},{32,0},{96,64},{160,128},{224,1... | collective-permute-start | bytes 1966088 | tf_op jit(solution)/shard_map/ppermute | solution.py:594
  19.9 3.1 %collective-permute-start.3 = (f32[5,8,32,128]{3,2,1,0:T(8,128)S(1)}, f32[5,8,32,128]{3,2,1,0:T(8,128)S(1)}, u32[]{:S(2)}, u32[]{:S(2)}) collective-permute-start(f32[5,8,32,128]{3,2,1,0:T(8,128)S(1)} %get-tuple-element.25.far), channel_id=1, source_target_pairs={{32,64},{96,128},{160,192},{64,32},{128,96},{192,160},{33,65},{97,... | collective-permute-start | bytes 1966088 | tf_op jit(solution)/shard_map/ppermute | solution.py:594
  23.0 0.0 collective-permute-done.2.near_in
  23.0 8.8 %collective-permute-done.3.far_in = f32[5,8,32,128]{3,2,1,0:T(8,128)S(1)} collective-permute-done((f32[5,8,32,128]{3,2,1,0:T(8,128)S(1)}, f32[5,8,32,128]{3,2,1,0:T(8,128)S(1)}, u32[]{:S(2)}, u32[]{:S(2)}) %collective-permute-start.3) | collective-permute-done | bytes 655392 | tf_op jit(solution)/shard_map/ppermute | solution.py:594
  31.8 10.4 %down0.1 = (f32[5,32,32,128]{3,2,1,0:T(8,128)S(1)}, f32[3,24,32,128]{3,2,1,0:T(8,128)S(1)}, f32[5,8,16,128]{3,2,1,0:T(8,128)S(1)}, f32[7,32,32,128]{3,2,1,0:T(8,128)S(1)}) custom-call(s32[4]{0:T(128)S(1)} %pad_add_fusion.place, f32[5,8,32,128]{3,2,1,0:T(8,128)S(1)} %get-tuple-element.24.near, f32[5,8,32,128]{3,2,1,0:T(8,128)S(1)} %get-tuple-element.25.far, ...), custom_call_target="tpu_custom_call" | custom-call | tf_op jit(solution)/shard_map/down0/pallas_call | solution.py:203
  42.2 1.9 %collective-permute-start.5 = (f32[5,8,16,128]{3,2,1,0:T(8,128)S(1)}, f32[5,8,16,128]{3,2,1,0:T(8,128)S(1)}, u32[]{:S(2)}, u32[]{:S(2)}) collective-permute-start(f32[5,8,16,128]{3,2,1,0:T(8,128)S(1)} %get-tuple-element.26.own), channel_id=1, source_target_pairs={{1,0},{2,1},{3,2},{4,3},{5,4},{6,5},{7,6},{8,7},{9,8},{10,9},{11,1... | collective-permute-start | bytes 983048 | tf_op jit(solution)/shard_map/ppermute | solution.py:586
  44.1 4.8 %collective-permute-start.4 = (f32[5,8,16,128]{3,2,1,0:T(8,128)S(1)}, f32[5,8,16,128]{3,2,1,0:T(8,128)S(1)}, u32[]{:S(2)}, u32[]{:S(2)}) collective-permute-start(f32[5,8,16,128]{3,2,1,0:T(8,128)S(1)} %get-tuple-element.26.own), channel_id=1, source_target_pairs={{0,1},{1,2},{2,3},{3,4},{4,5},{5,6},{6,7},{7,8},{8,9},{9,10},{10,1... | collective-permute-start | bytes 983048 | tf_op jit(solution)/shard_map/ppermute | solution.py:586
  48.8 2.5 %collective-permute-done.5.right = f32[5,8,16,128]{3,2,1,0:T(8,128)S(1)} collective-permute-done((f32[5,8,16,128]{3,2,1,0:T(8,128)S(1)}, f32[5,8,16,128]{3,2,1,0:T(8,128)S(1)}, u32[]{:S(2)}, u32[]{:S(2)}) %collective-permute-start.5) | collective-permute-done | bytes 327712 | tf_op jit(solution)/shard_map/ppermute | solution.py:586
  51.4 1.5 %collective-permute-done.4.left = f32[5,8,16,128]{3,2,1,0:T(8,128)S(1)} collective-permute-done((f32[5,8,16,128]{3,2,1,0:T(8,128)S(1)}, f32[5,8,16,128]{3,2,1,0:T(8,128)S(1)}, u32[]{:S(2)}, u32[]{:S(2)}) %collective-permute-start.4) | collective-permute-done | bytes 327712 | tf_op jit(solution)/shard_map/ppermute | solution.py:586
  52.8 0.7 cut1.1
  53.5 0.1 collective-permute-start.6
  53.7 7.0 %collective-permute-start.7 = (f32[5,5,32,128]{3,2,1,0:T(8,128)S(1)}, f32[5,5,32,128]{3,2,1,0:T(8,128)S(1)}, u32[]{:S(2)}, u32[]{:S(2)}) collective-permute-start(f32[5,5,32,128]{3,2,1,0:T(8,128)S(1)} %get-tuple-element.29), channel_id=1, source_target_pairs={{32,64},{96,128},{160,192},{64,32},{128,96},{192,160},{33,65},{97,... | collective-permute-start | bytes 1228808 | tf_op jit(solution)/shard_map/ppermute | solution.py:594
  60.7 0.0 collective-permute-done.6.near
  60.7 5.6 %collective-permute-done.7.far = f32[5,5,32,128]{3,2,1,0:T(8,128)S(1)} collective-permute-done((f32[5,5,32,128]{3,2,1,0:T(8,128)S(1)}, f32[5,5,32,128]{3,2,1,0:T(8,128)S(1)}, u32[]{:S(2)}, u32[]{:S(2)}) %collective-permute-start.7) | collective-permute-done | bytes 409632 | tf_op jit(solution)/shard_map/ppermute | solution.py:594
  66.3 6.6 %down1.1 = (f32[5,16,32,128]{3,2,1,0:T(8,128)S(1)}, f32[3,16,32,128]{3,2,1,0:T(8,128)S(1)}, f32[5,16,128]{2,1,0:T(8,128)S(1)}, f32[7,16,32,128]{3,2,1,0:T(8,128)S(1)}) custom-call(s32[4]{0:T(128)S(1)} %pad_add_fusion.place, f32[5,8,32,128]{3,2,1,0:T(8,128)S(1)} %get-tuple-element.27.centre, f32[5,5,32,128]{3,2,1,0:T(8,128)S(1)} %collective-permute-done.6.near, ...), custom_call_target="tpu_custom_call" | custom-call | tf_op jit(solution)/shard_map/down1/pallas_call | solution.py:203
  72.9 23.9 %all_to_all.10.parts = f32[32,5,4,128]{3,2,1,0:T(4,128)S(1)} all-to-all(f32[32,5,4,128]{3,2,1,0:T(4,128)S(1)} %broadcast_in_dim.4), channel_id=1, replica_groups=mesh['grp'=8,'brick'=32] {'brick'}, dimensions={0} | all-to-all | bytes 655360 | tf_op jit(solution)/shard_map/all_to_all | solution.py:647
  96.8 0.6 column.1
  97.4 13.7 %all_to_all.11.mine = f32[4,5,48,128]{3,2,1,0:T(8,128)S(1)} all-to-all(f32[4,5,48,128]{3,2,1,0:T(8,128)S(1)} %broadcast_in_dim.5), channel_id=1, replica_groups={{0,64,128,192},{32,96,160,224},{1,65,129,193},{33,97,161,225},{2,66,130..., dimensions={0} | all-to-all | bytes 983040 | tf_op jit(solution)/shard_map/all_to_all | solution.py:649
  111.1 3.2 %collective-permute-start.8 = (f32[4,5,48,128]{3,2,1,0:T(8,128)S(1)}, f32[4,5,48,128]{3,2,1,0:T(8,128)S(1)}, u32[]{:S(2)}, u32[]{:S(2)}) collective-permute-start(f32[4,5,48,128]{3,2,1,0:T(8,128)S(1)} %all_to_all.11.mine), channel_id=1, source_target_pairs={{0,32},{64,96},{128,160},{192,224},{32,0},{96,64},{160,128},{224,1... | collective-permute-start | bytes 1474568 | tf_op jit(solution)/shard_map/ppermute | solution.py:594
  114.3 1.5 %collective-permute-done.8.other = f32[4,5,48,128]{3,2,1,0:T(8,128)S(1)} collective-permute-done((f32[4,5,48,128]{3,2,1,0:T(8,128)S(1)}, f32[4,5,48,128]{3,2,1,0:T(8,128)S(1)}, u32[]{:S(2)}, u32[]{:S(2)}) %collective-permute-start.8) | collective-permute-done | bytes 491552 | tf_op jit(solution)/shard_map/ppermute | solution.py:594
  115.8 25.1 %climb.1 = f32[3,16,16,128]{3,2,1,0:T(8,128)} custom-call(s32[4]{0:T(128)S(1)} %pad_add_fusion.place, f32[4,5,48,128]{3,2,1,0:T(8,128)S(1)} %all_to_all.11.mine, f32[4,5,48,128]{3,2,1,0:T(8,128)S(1)} %collective-permute-done.8.other, f32[5,16,32,128]{3,2,1,0:T(8,128)S(1)} %get-tuple-element.31.data1, f32[3,16,32,128]{3,2,1,0:T(8,128)S(1)} %get-tuple-element.32.saved1, ...), custom_call_target="tpu_custom_call" | custom-call | tf_op jit(solution)/shard_map/climb/pallas_call | solution.py:203
  (3 shorter events, 0.1 us)
Async XLA Ops:
  0.0 1.0 copy-start
  1.0 0.9 copy-start.1
  1.9 0.9 copy-start.2
  3.4 10.5 %collective-permute-start = (f32[5,16,8,128]{3,2,1,0:T(8,128)S(1)}, f32[5,16,8,128]{3,2,1,0:T(8,128)S(1)}, u32[]{:S(2)}, u32[]{:S(2)}) collective-permute-start(f32[5,16,8,128]{3,2,1,0:T(8,128)S(1)} %get-tuple-element.22), channel_id=1, source_target_pairs={{0,1},{1,2},{2,3},{3,4},{4,5},{5,6},{6,7},{7,8},{8,9},{9,10},{10,1... | collective-permute-start | bytes 983048 | tf_op jit(solution)/shard_map/ppermute | solution.py:586
  7.0 10.5 %collective-permute-start.1 = (f32[5,16,8,128]{3,2,1,0:T(8,128)S(1)}, f32[5,16,8,128]{3,2,1,0:T(8,128)S(1)}, u32[]{:S(2)}, u32[]{:S(2)}) collective-permute-start(f32[5,16,8,128]{3,2,1,0:T(8,128)S(1)} %get-tuple-element.23), channel_id=1, source_target_pairs={{1,0},{2,1},{3,2},{4,3},{5,4},{6,5},{7,6},{8,7},{9,8},{10,9},{11,1... | collective-permute-start | bytes 983048 | tf_op jit(solution)/shard_map/ppermute | solution.py:586
  18.2 4.9 %collective-permute-start.2 = (f32[5,8,32,128]{3,2,1,0:T(8,128)S(1)}, f32[5,8,32,128]{3,2,1,0:T(8,128)S(1)}, u32[]{:S(2)}, u32[]{:S(2)}) collective-permute-start(f32[5,8,32,128]{3,2,1,0:T(8,128)S(1)} %get-tuple-element.24.near), channel_id=1, source_target_pairs={{0,32},{64,96},{128,160},{192,224},{32,0},{96,64},{160,128},{224,1... | collective-permute-start | bytes 1966088 | tf_op jit(solution)/shard_map/ppermute | solution.py:594
  19.9 11.9 %collective-permute-start.3 = (f32[5,8,32,128]{3,2,1,0:T(8,128)S(1)}, f32[5,8,32,128]{3,2,1,0:T(8,128)S(1)}, u32[]{:S(2)}, u32[]{:S(2)}) collective-permute-start(f32[5,8,32,128]{3,2,1,0:T(8,128)S(1)} %get-tuple-element.25.far), channel_id=1, source_target_pairs={{32,64},{96,128},{160,192},{64,32},{128,96},{192,160},{33,65},{97,... | collective-permute-start | bytes 1966088 | tf_op jit(solution)/shard_map/ppermute | solution.py:594
  42.2 9.2 %collective-permute-start.5 = (f32[5,8,16,128]{3,2,1,0:T(8,128)S(1)}, f32[5,8,16,128]{3,2,1,0:T(8,128)S(1)}, u32[]{:S(2)}, u32[]{:S(2)}) collective-permute-start(f32[5,8,16,128]{3,2,1,0:T(8,128)S(1)} %get-tuple-element.26.own), channel_id=1, source_target_pairs={{1,0},{2,1},{3,2},{4,3},{5,4},{6,5},{7,6},{8,7},{9,8},{10,9},{11,1... | collective-permute-start | bytes 983048 | tf_op jit(solution)/shard_map/ppermute | solution.py:586
  44.1 8.8 %collective-permute-start.4 = (f32[5,8,16,128]{3,2,1,0:T(8,128)S(1)}, f32[5,8,16,128]{3,2,1,0:T(8,128)S(1)}, u32[]{:S(2)}, u32[]{:S(2)}) collective-permute-start(f32[5,8,16,128]{3,2,1,0:T(8,128)S(1)} %get-tuple-element.26.own), channel_id=1, source_target_pairs={{0,1},{1,2},{2,3},{3,4},{4,5},{5,6},{6,7},{7,8},{8,9},{9,10},{10,1... | collective-permute-start | bytes 983048 | tf_op jit(solution)/shard_map/ppermute | solution.py:586
  53.5 7.1 %collective-permute-start.6 = (f32[5,5,32,128]{3,2,1,0:T(8,128)S(1)}, f32[5,5,32,128]{3,2,1,0:T(8,128)S(1)}, u32[]{:S(2)}, u32[]{:S(2)}) collective-permute-start(f32[5,5,32,128]{3,2,1,0:T(8,128)S(1)} %get-tuple-element.28), channel_id=1, source_target_pairs={{0,32},{64,96},{128,160},{192,224},{32,0},{96,64},{160,128},{224,1... | collective-permute-start | bytes 1228808 | tf_op jit(solution)/shard_map/ppermute | solution.py:594
  53.7 12.6 %collective-permute-start.7 = (f32[5,5,32,128]{3,2,1,0:T(8,128)S(1)}, f32[5,5,32,128]{3,2,1,0:T(8,128)S(1)}, u32[]{:S(2)}, u32[]{:S(2)}) collective-permute-start(f32[5,5,32,128]{3,2,1,0:T(8,128)S(1)} %get-tuple-element.29), channel_id=1, source_target_pairs={{32,64},{96,128},{160,192},{64,32},{128,96},{192,160},{33,65},{97,... | collective-permute-start | bytes 1228808 | tf_op jit(solution)/shard_map/ppermute | solution.py:594
  111.1 4.7 %collective-permute-start.8 = (f32[4,5,48,128]{3,2,1,0:T(8,128)S(1)}, f32[4,5,48,128]{3,2,1,0:T(8,128)S(1)}, u32[]{:S(2)}, u32[]{:S(2)}) collective-permute-start(f32[4,5,48,128]{3,2,1,0:T(8,128)S(1)} %all_to_all.11.mine), channel_id=1, source_target_pairs={{0,32},{64,96},{128,160},{192,224},{32,0},{96,64},{160,128},{224,1... | collective-permute-start | bytes 1474568 | tf_op jit(solution)/shard_map/ppermute | solution.py:594

commit v3 on v2

--- a/solution.py
+++ b/solution.py
@@ -198,7 +198,7 @@
     return [pl.BlockSpec(memory_space=pltpu.VMEM)] * count
 
 
-def call(kernel, outs, scratch, *args, name):
+def call(kernel, outs, scratch, *args, name, aliases={}):
     smem = pl.BlockSpec(memory_space=pltpu.SMEM)
     return pl.pallas_call(
         kernel,
@@ -207,11 +207,24 @@
         out_specs=vmem(len(outs)),
         scratch_shapes=[pltpu.VMEM(s, F32) for s in scratch],
         compiler_params=pltpu.CompilerParams(vmem_limit_bytes=28 * 2**20),
+        input_output_aliases=aliases,
         name=name,
     )(*args)
 
 
-def cut_kernel(f, k, r, own, lo, hi, sems):
+def by_parity(index, act):
+    odd = index % 2
+
+    @pl.when(odd == 0)
+    def _():
+        act(True)
+
+    @pl.when(odd == 1)
+    def _():
+        act(False)
+
+
+def cut_kernel(place, f, k, r, own, first, second, sems):
     copies = [
         pltpu.make_async_copy(f, own.at[0:3], sems.at[0]),
         pltpu.make_async_copy(k, own.at[3], sems.at[1]),
@@ -221,51 +234,53 @@
         copy.start()
     for copy in copies:
         copy.wait()
-    lo[...] = own[:, :, 0:HALO]
-    hi[...] = own[:, :, HALO : 2 * HALO]
-
-
-def cut(f, k, r):
+
+    def act(even):
+        lo, hi = (second, first) if even else (first, second)
+        lo[...] = own[:, :, 0:HALO]
+        hi[...] = own[:, :, HALO : 2 * HALO]
+
+    by_parity(place[1], act)
+
+
+def cut(place, f, k, r):
     block = (5, 16, 16, LANES)
     strip = (5, 16, HALO, LANES)
     return pl.pallas_call(
         cut_kernel,
         out_shape=[jax.ShapeDtypeStruct(shape, F32) for shape in (block, strip, strip)],
-        in_specs=[pl.BlockSpec(memory_space=pl.ANY)] * 3,
+        in_specs=[pl.BlockSpec(memory_space=pltpu.SMEM)]
+        + [pl.BlockSpec(memory_space=pltpu.HBM)] * 3,
         out_specs=vmem(3),
         scratch_shapes=[pltpu.SemaphoreType.DMA((3,))],
         compiler_params=pltpu.CompilerParams(vmem_limit_bytes=28 * 2**20),
         name="cut0",
-    )(f, k, r)
-
-
-def by_parity(place, act):
-    odd = place[0] % 2
-
-    @pl.when(odd == 0)
-    def _():
-        act(True)
-
-    @pl.when(odd == 1)
-    def _():
-        act(False)
-
-
-def join_kernel(place, own, lo, hi, near, far):
-    def act(even):
-        for half, out in enumerate((far, near) if even else (near, far)):
-            rows = slice(8 * half, 8 * half + 8)
-            for q in range(5):
-                out[q, :, 0:8] = lo[q, rows]
-                out[q, :, 8:24] = own[q, rows]
-                out[q, :, 24:32] = hi[q, rows]
-
-    by_parity(place, act)
+    )(place, f, k, r)
+
+
+def join_kernel(place, own, first, second, near, far):
+    def sides(swapped):
+        lo, hi = (second, first) if swapped else (first, second)
+
+        def act(even):
+            for half, out in enumerate((far, near) if even else (near, far)):
+                rows = slice(8 * half, 8 * half + 8)
+                for q in range(5):
+                    out[q, :, 0:8] = lo[q, rows]
+                    out[q, :, 8:24] = own[q, rows]
+                    out[q, :, 24:32] = hi[q, rows]
+
+        by_parity(place[0], act)
+
+    by_parity(place[1], sides)
 
 
 FINE = Level(1.0, 128, 30, 32)
+FINE_UP = Level(1.0, 128, 22, 24)
 MIDDLE = Level(0.25, 64, 14, 32)
+MIDDLE_UP = Level(0.25, 64, 10, 24)
 COARSE = Level(0.0625, 32, 8, 48)
+COARSE_UP = Level(0.0625, 32, 8, 32)
 LAST = Level(0.015625, 16, 2, 24)
 
 
@@ -284,23 +299,43 @@
     return inside
 
 
-def fine_down(place, near, far, near_in, far_in, data, saved, packed, kept, s0, d0, t0, sums):
+def fine_inner(place, near, far, data, kept, s0, d0, t0):
     coef = [kept.at[j] for j in range(7)]
 
     def act(even):
-        order = (far_in, far, near, near_in) if even else (near_in, near, far, far_in)
-        for number, part in enumerate(order):
-            data[:, 8 * number : 8 * number + 8] = part[...]
-
-    by_parity(place, act)
+        for number, part in enumerate((far, near) if even else (near, far)):
+            data[:, 8 * number + 8 : 8 * number + 16] = part[...]
+
+    by_parity(place[0], act)
+    setup(FINE, lambda i: data[3, i], lambda i: data[4, i], coef, fine_inside(place), 9, 23)
+    begin(FINE, data, coef, s0, d0, 9, 23)
+    step(FINE, 1, data, coef, s0, t0, d0, 10, 22)
+    step(FINE, 2, data, coef, t0, s0, d0, 11, 21)
+    step(FINE, 3, data, coef, s0, t0, d0, 12, 20)
+
+
+def fine_outer(place, near, far, *refs):
+    data, kept, s0, d0, t0, saved, packed, first, second, sums, resid = refs[5:]
+    coef = [kept.at[j] for j in range(7)]
+
+    def act(even):
+        lo, hi = (far, near) if even else (near, far)
+        data[:, 0:8] = lo[...]
+        data[:, 24:32] = hi[...]
+
+    by_parity(place[0], act)
     inside = fine_inside(place)
-    setup(FINE, lambda i: data[3, i], lambda i: data[4, i], coef, inside, 1, 31)
-    begin(FINE, data, coef, s0, d0, 1, 31)
-    step(FINE, 1, data, coef, s0, t0, d0, 2, 30)
-    step(FINE, 2, data, coef, t0, s0, d0, 3, 29)
-    step(FINE, 3, data, coef, s0, t0, d0, 4, 28)
-    saved[...] = t0[:, 4:28]
-    residual(FINE, data, coef, t0, d0, 6, 26)
+    for lo, hi in ((1, 9), (23, 31)):
+        setup(FINE, lambda i: data[3, i], lambda i: data[4, i], coef, inside, lo, hi)
+        begin(FINE, data, coef, s0, d0, lo, hi)
+    for lo, hi in ((2, 10), (22, 30)):
+        step(FINE, 1, data, coef, s0, t0, d0, lo, hi)
+    for lo, hi in ((3, 11), (21, 29)):
+        step(FINE, 2, data, coef, t0, s0, d0, lo, hi)
+    for lo, hi in ((4, 12), (20, 28)):
+        step(FINE, 3, data, coef, s0, t0, d0, lo, hi)
+    saved[...] = t0[:, 4:28, 4:28]
+    residual(FINE, data, coef, t0, resid, 6, 26)
     pair = s0.at[0]
     wide = sums
     for q in range(5):
@@ -310,7 +345,7 @@
             if q >= 3:
                 pair[t] = data[q, 2 * t] + data[q, 2 * t + 1]
             elif 3 <= t <= 12:
-                pair[t] = d0[q, 2 * t] + d0[q, 2 * t + 1]
+                pair[t] = resid[q, 2 * t] + resid[q, 2 * t + 1]
             else:
                 wide[where] = jnp.zeros((16, LANES), F32)
                 continue
@@ -320,26 +355,53 @@
     )
     packed[...] = mix(wide[...].reshape(5 * 8 * 16, 2 * LANES), matrix).reshape(5, 8, 16, LANES)
 
-
-def middle_cut(place, own, left, right, near, far, centre):
-    lane = lane_of((32, LANES))
-
-    for q in range(5):
-        for i in range(8):
-            centre[q, i, 0:12] = left[q, i, 0:12]
-            centre[q, i, 12:20] = own[q, i, 4:12]
-            centre[q, i, 20:32] = right[q, i, 4:16]
+    def send(even):
+        left, right = (second, first) if even else (first, second)
+        for q in range(5):
+            skip = 1 if q < 3 else 2
+            left[q] = packed[q, :, 4 + skip : 12 + skip]
+            right[q] = packed[q, :, 4 - skip : 12 - skip]
+
+    by_parity(place[1], send)
+
+
+def fine_trim(place, data, kept, data_up, kept_up):
+    for q in range(3):
+        data_up[q] = data[q, 4:28, 4:28]
+    for j in range(7):
+        kept_up[j] = kept[j, 4:28, 4:28]
+
+
+def middle_cut(place, own, first, second, near, far, centre):
+    low = lane_of((32, LANES)) < 64
+    zero = jnp.zeros((4, LANES), F32)
+
+    def sides(even):
+        left, right = (second, first) if even else (first, second)
+        for q in range(5):
+            skip = 1 if q < 3 else 2
+            for i in range(8):
+                centre[q, i, 0 : 4 - skip] = zero[0 : 4 - skip]
+                centre[q, i, 4 - skip : 12 - skip] = left[q, i]
+                centre[q, i, 12 - skip : 20 + skip] = own[q, i, 4 - skip : 12 + skip]
+                centre[q, i, 20 + skip : 28 + skip] = right[q, i]
+                centre[q, i, 28 + skip : 32] = zero[0 : 4 - skip]
+
+    by_parity(place[1], sides)
+
+    def at(q, x, half):
+        value = centre[q, x + 4 if x < 4 else x - 4]
+        return value if (x >= 4) == (half == 1) else pltpu.roll(value, 64, 1)
 
     def act(even):
         up, down = (near, far) if even else (far, near)
         for q in range(5):
-            for t in range(5):
-                tail = pltpu.roll(centre[q, 7], 64, 1) if t == 0 else centre[q, t - 1]
-                up[q, t] = jnp.where(lane < 64, centre[q, 2 + t], tail)
-                head = pltpu.roll(centre[q, 0], 64, 1) if t == 4 else centre[q, 4 + t]
-                down[q, t] = jnp.where(lane < 64, head, centre[q, 1 + t])
-
-    by_parity(place, act)
+            skip = 1 if q < 3 else 2
+            for t in range(4):
+                up[q, t] = jnp.where(low, at(q, t - skip, 0), at(q, t - skip + 4, 1))
+                down[q, t] = jnp.where(low, at(q, t + skip, 0), at(q, t + skip + 4, 1))
+
+    by_parity(place[0], act)
 
 
 def middle_inside(place):
@@ -356,20 +418,29 @@
 
 def middle_join(centre, lo, hi, data):
     low = lane_of((32, LANES)) < 64
+    zero = jnp.zeros((32, LANES), F32)
+
+    def moved(ref, q, t, half):
+        value = ref[q, t % 4]
+        return value if t // 4 == half else pltpu.roll(value, 64, 1)
+
     for q in range(5):
+        skip = 1 if q < 3 else 2
         for i in range(14):
-            if i < 5:
-                a = lo[q, i]
-            elif i < 10:
-                a = pltpu.roll(lo[q, i - 5], 64, 1)
+            t = i - (2 - skip)
+            if t < 0:
+                a = zero
+            elif t < 8:
+                a = moved(lo, q, t, 0)
             else:
                 a = centre[q, i - 6]
-            if i < 4:
+            t = i - (4 + skip)
+            if t < 0:
                 b = centre[q, i]
-            elif i < 9:
-                b = pltpu.roll(hi[q, i - 4], 64, 1)
+            elif t < 8:
+                b = moved(hi, q, t, 1)
             else:
-                b = hi[q, i - 9]
+                b = zero
             data[q, i + 1] = jnp.where(low, a, b)
         ghosts(MIDDLE, data, (q,))
 
@@ -378,7 +449,10 @@
     coef = [kept.at[j] for j in range(7)]
     lane = lane_of((32, LANES))
     low = lane < 64
-    by_parity(place, lambda even: middle_join(centre, *((far, near) if even else (near, far)), data))
+    by_parity(
+        place[0],
+        lambda even: middle_join(centre, *((far, near) if even else (near, far)), data),
+    )
     setup(MIDDLE, lambda i: data[3, i], lambda i: data[4, i], coef, middle_inside(place), 1, 15)
     begin(MIDDLE, data, coef, s1, d1, 1, 15)
     step(MIDDLE, 1, data, coef, s1, t1, d1, 1, 15)
@@ -402,6 +476,15 @@
     packed[...] = mix(sums[...].reshape(5 * 16, 2 * LANES), matrix).reshape(5, 16, LANES)
 
 
+def middle_trim(place, data, saved, kept, data_up, saved_up, kept_up):
+    low = lane_of((24, LANES)) < 64
+    groups = [(data, data_up, 3), (saved, saved_up, 3), (kept, kept_up, 7)]
+    for old, new, count in groups:
+        for q in range(count):
+            for j in range(12):
+                new[q, j] = jnp.where(low, old[q, 4 + j, 2:26], old[q, j, 2:26])
+
+
 def column_kernel(place, parts, out):
     zero = jnp.zeros((4, LANES), F32)
     for q in range(5):
@@ -462,7 +545,7 @@
                 data2[q, i + 1] = row
             ghosts(COARSE, data2, (q,))
 
-    by_parity(place, act)
+    by_parity(place[0], act)
     setup(COARSE, lambda i: data2[3, i], lambda i: data2[4, i], coef2, coarse_inside(place), 1, 9)
     begin(COARSE, data2, coef2, s2, d2, 1, 9)
     step(COARSE, 1, data2, coef2, s2, t2, d2, 1, 9)
@@ -494,6 +577,8 @@
     step(LAST, 2, data3, coef3, t3, s3, d3, 1, 3)
     step(LAST, 3, data3, coef3, s3, t3, d3, 1, 3)
 
+    data2u, s2u, t2u, d2u = (ref.at[:, :, 8:40] for ref in (data2, s2, t2, d2))
+    coef2u = [ref.at[:, 8:40] for ref in coef2]
     matrix = pick(
         LANES,
         2 * LANES,
@@ -509,14 +594,14 @@
             piece = wide[at : at + 24, half * LANES : half * LANES + LANES]
             grown3[c, t, pl.ds(0, 24, 2)] = piece
             grown3[c, t, pl.ds(1, 24, 2)] = piece
-            more = grown3[c, t]
-            s2[c, 1 + 2 * t] = keep2[c, 1 + 2 * t] + more
-            s2[c, 2 + 2 * t] = keep2[c, 2 + 2 * t] + more
-        ghosts(COARSE, s2, (c,))
-    step(COARSE, 0, data2, coef2, s2, t2, d2, 1, 9)
-    step(COARSE, 1, data2, coef2, t2, s2, d2, 1, 9)
-    step(COARSE, 2, data2, coef2, s2, t2, d2, 1, 9)
-    step(COARSE, 3, data2, coef2, t2, s2, d2, 1, 9)
+            more = grown3[c, t, 8:40]
+            s2u[c, 1 + 2 * t] = keep2[c, 1 + 2 * t, 8:40] + more
+            s2u[c, 2 + 2 * t] = keep2[c, 2 + 2 * t, 8:40] + more
+        ghosts(COARSE_UP, s2u, (c,))
+    step(COARSE_UP, 0, data2u, coef2u, s2u, t2u, d2u, 1, 9)
+    step(COARSE_UP, 1, data2u, coef2u, t2u, s2u, d2u, 1, 9)
+    step(COARSE_UP, 2, data2u, coef2u, s2u, t2u, d2u, 1, 9)
+    step(COARSE_UP, 3, data2u, coef2u, t2u, s2u, d2u, 1, 9)
 
     matrix = pick(
         LANES,
@@ -535,28 +620,28 @@
 
     pieces = []
     for c in range(3):
-        for m in range(7):
-            x = place[0] * 4 - 5 + m
-            pieces.append(jnp.where(small, window(c, x, 0), window(c, x + 7, 1)))
+        for m in range(5):
+            x = place[0] * 4 - 3 + m
+            pieces.append(jnp.where(small, window(c, x, 0), window(c, x + 5, 1)))
     wide = mix(jnp.concatenate(pieces, axis=0), matrix)
     for c in range(3):
-        for m in range(7):
-            at = (c * 7 + m) * 16
+        for m in range(5):
+            at = (c * 5 + m) * 16
             piece = wide[at : at + 16]
             grown2[c, m, pl.ds(0, 16, 2)] = piece
             grown2[c, m, pl.ds(1, 16, 2)] = piece
-            more = grown2[c, m]
+            more = grown2[c, m, 2:26]
             s1[c, 1 + 2 * m] = saved1[c, 1 + 2 * m] + more
             s1[c, 2 + 2 * m] = saved1[c, 2 + 2 * m] + more
-        ghosts(MIDDLE, s1, (c,))
-    step(MIDDLE, 0, data1, coef1, s1, t1, d1, 1, 15)
-    step(MIDDLE, 1, data1, coef1, t1, s1, d1, 1, 15)
-    step(MIDDLE, 2, data1, coef1, s1, t1, d1, 1, 15)
-    step(MIDDLE, 3, data1, coef1, t1, s1, d1, 1, 15)
+        ghosts(MIDDLE_UP, s1, (c,))
+    step(MIDDLE_UP, 0, data1, coef1, s1, t1, d1, 1, 11)
+    step(MIDDLE_UP, 1, data1, coef1, t1, s1, d1, 1, 11)
+    step(MIDDLE_UP, 2, data1, coef1, s1, t1, d1, 1, 11)
+    step(MIDDLE_UP, 3, data1, coef1, t1, s1, d1, 1, 11)
 
     for half in range(2):
         matrix = pick(LANES, LANES, lambda a, b: a == 64 * half + b // 2, 1.0)
-        rows = [9 + t for t in range(6)] if half == 0 else [1 + t for t in range(6)]
+        rows = [5 + t for t in range(6)] if half == 0 else [1 + t for t in range(6)]
         flat = jnp.concatenate([s1[c, i, 8:24] for c in range(3) for i in rows], axis=0)
         wide = mix(flat, matrix)
         for c in range(3):
@@ -565,33 +650,26 @@
                 piece = wide[at : at + 16]
                 grown1[c, t, pl.ds(0, 16, 2)] = piece
                 grown1[c, t, pl.ds(1, 16, 2)] = piece
-                more = grown1[c, t]
+                more = grown1[c, t, 0:24]
                 row = 2 * (t + 6 * half)
-                s0[c, 4 + row] = saved0[c, row] + more
-                s0[c, 5 + row] = saved0[c, row + 1] + more
-    step(FINE, 0, data0, coef0, s0, t0, d0, 5, 27)
-    step(FINE, 1, data0, coef0, t0, s0, d0, 6, 26)
-    step(FINE, 2, data0, coef0, s0, t0, d0, 7, 25)
+                s0[c, row] = saved0[c, row] + more
+                s0[c, row + 1] = saved0[c, row + 1] + more
+    step(FINE_UP, 0, data0, coef0, s0, t0, d0, 1, 23)
+    step(FINE_UP, 1, data0, coef0, t0, s0, d0, 2, 22)
+    step(FINE_UP, 2, data0, coef0, s0, t0, d0, 3, 21)
     keep, gain = STEPS[3]
 
     def emit(i, c, u, resid):
         move = (gain * coef0[6][i]) * resid + keep * d0[c, i]
-        out[c, i - 8] = (u + move)[8:24]
-
-    sweep(FINE, data0, coef0, t0, 8, 24, emit)
-
-
-def shift(value, axis, by):
+        out[c, i - 4] = (u + move)[4:20]
+
+    sweep(FINE_UP, data0, coef0, t0, 4, 20, emit)
+
+
+def swap(value, axis, first):
     count = lax.axis_size(axis)
-    return lax.ppermute(
-        value, axis, [(i, i + by) for i in range(count) if 0 <= i + by < count]
-    )
-
-
-def swap(value, first):
-    count = lax.axis_size("grp")
     ends = [(i, i + 1) for i in range(first, count - 1, 2)]
-    return lax.ppermute(value, "grp", ends + [(b, a) for a, b in ends])
+    return lax.ppermute(value, axis, ends + [(b, a) for a, b in ends])
 
 
 def on_device(right_side, stiffness, reaction):
@@ -600,43 +678,48 @@
     place = jnp.stack(
         [lax.axis_index("grp"), lax.axis_index("brick"), jnp.int32(count), jnp.int32(bricks)]
     ).astype(jnp.int32)
-    own, low, high = cut(right_side, stiffness, reaction)
-    left = shift(high, "brick", 1)
-    right = shift(low, "brick", -1)
-    near, far = call(join_kernel, [(5, 8, 32, 128)] * 2, [], place, own, left, right, name="join0")
-    far_in = swap(far, 1)
-    near_in = swap(near, 0)
-    fine = [FINE.shape(3)] * 3
-    data0, saved0, packed1, kept0 = call(
-        fine_down,
-        [FINE.shape(5), (3, 24, 32, 128), (5, 8, 16, 128), FINE.shape(7)],
-        fine + [(5, 8, 16, 256)],
+    own, first, second = cut(place, right_side, stiffness, reaction)
+    first = swap(first, "brick", 0)
+    second = swap(second, "brick", 1)
+    near, far = call(
+        join_kernel, [(5, 8, 32, 128)] * 2, [], place, own, first, second, name="join0"
+    )
+    far_in = swap(far, "grp", 1)
+    near_in = swap(near, "grp", 0)
+    states = [FINE.shape(5), FINE.shape(7)] + [FINE.shape(3)] * 3
+    inner = call(fine_inner, states, [], place, near, far, name="inner0")
+    data0, kept0, _, _, _, saved0, packed1, first, second = call(
+        fine_outer,
+        states + [(3, 24, 24, 128), (5, 8, 16, 128)] + [(5, 8, 8, 128)] * 2,
+        [(5, 8, 16, 256), FINE.shape(3)],
         place,
-        near,
-        far,
         near_in,
         far_in,
-        name="down0",
-    )
-    left = shift(packed1, "brick", 1)
-    right = shift(packed1, "brick", -1)
+        *inner,
+        name="outer0",
+        aliases={3 + j: j for j in range(5)},
+    )
+    first = swap(first, "brick", 0)
+    second = swap(second, "brick", 1)
+    data0, kept0 = call(
+        fine_trim, [FINE_UP.shape(3), FINE_UP.shape(7)], [], place, data0, kept0, name="trim0"
+    )
     near, far, centre = call(
         middle_cut,
-        [(5, 5, 32, 128)] * 2 + [(5, 8, 32, 128)],
+        [(5, 4, 32, 128)] * 2 + [(5, 8, 32, 128)],
         [],
         place,
         packed1,
-        left,
-        right,
+        first,
+        second,
         name="cut1",
     )
-    far_in = swap(far, 1)
-    near_in = swap(near, 0)
-    middle = [MIDDLE.shape(3)] * 3
+    far_in = swap(far, "grp", 1)
+    near_in = swap(near, "grp", 0)
     data1, saved1, packed2, kept1 = call(
         middle_down,
         [MIDDLE.shape(5), MIDDLE.shape(3), (5, 16, 128), MIDDLE.shape(7)],
-        middle + [(5, 2, 32, 128), (5, 16, 256)],
+        [MIDDLE.shape(3)] * 3 + [(5, 2, 32, 128), (5, 16, 256)],
         place,
         centre,
         near_in,
@@ -653,14 +736,24 @@
         0,
         axis_index_groups=[list(range(core, count, 2)) for core in range(2)],
     )
-    other = swap(mine, 0)
+    other = swap(mine, "grp", 0)
+    data1, saved1, kept1 = call(
+        middle_trim,
+        [MIDDLE_UP.shape(3)] * 2 + [MIDDLE_UP.shape(7)],
+        [],
+        place,
+        data1,
+        saved1,
+        kept1,
+        name="trim1",
+    )
     coarse = [COARSE.shape(5)] + [COARSE.shape(3)] * 4 + coef_shapes(COARSE)
     last = [(5, 2, 24, 256), LAST.shape(5)] + [LAST.shape(3)] * 3 + coef_shapes(LAST)
-    grown = [(3, 4, 48, 128), (3, 7, 32, 128), (3, 6, 32, 128)]
+    grown = [(3, 4, 48, 128), (3, 5, 32, 128), (3, 6, 32, 128)]
     (answer,) = call(
         climb,
         [(3, 16, 16, 128)],
-        coarse + last + grown + middle + fine,
+        coarse + last + grown + [MIDDLE_UP.shape(3)] * 3 + [FINE_UP.shape(3)] * 3,
         place,
         mine,
         other,

time: 141 us -> 126 us (0.89)
  waiting for transfers between devices: 28.4 us -> 19.4 us
  starting transfers between devices: 27.3 us -> 24.4 us
  blocking collectives: 37.6 us -> 34.7 us
    ppermute x9, waiting for transfers between devices: 28.4 us -> 19.4 us  [swap(): return lax.ppermute(value, axis, ends + [(b, a) for a, b in ends])]
    all_to_all x1, blocking collectives: 23.9 us -> 20.9 us  [on_device(): lax.all_to_all(jnp.broadcast_to(block[None], (bricks, 5, 4, 128)), 'brick...]
    ppermute x9, starting transfers between devices: 27.3 us -> 24.4 us  [swap(): return lax.ppermute(value, axis, ends + [(b, a) for a, b in ends])]
    pallas_call x6 -> x9, Pallas kernels: 44 us -> 43 us  [call(): pl.pallas_call(kernel, out_shape=[jax.ShapeDtypeStruct(s, F32) for s in o...]
  transfers between devices with their start and end apart: 9 -> 9, of which waited for: 7 -> 6; matrix products, arithmetic and copies ran while one was open for 0% -> 0% of each run, Pallas kernels for 0% -> 4%
where the time goes in v3:
time: 126 us
  Pallas kernels  44.2 us (35%)
  blocking collectives  34.7 us (28%)
  starting transfers between devices  24.4 us (19%)
  waiting for transfers between devices  19.4 us (15%)
  local copies, waits for them, and re-layouts  2.89 us (2%)
    pallas_call x9, Pallas kernels, call(): pl.pallas_call(kernel, out_shape=[jax.ShapeDtypeStruct(s, F32) for s in o...  43 us
    ppermute x9, starting transfers between devices, swap(): return lax.ppermute(value, axis, ends + [(b, a) for a, b in ends])  24.4 us
    all_to_all x1, blocking collectives, on_device(): lax.all_to_all(jnp.broadcast_to(block[None], (bricks, 5, 4, 128)), 'brick...  20.9 us
    ppermute x9, waiting for transfers between devices, swap(): return lax.ppermute(value, axis, ends + [(b, a) for a, b in ends])  19.4 us
    all_to_all x1, blocking collectives, on_device(): lax.all_to_all(jnp.broadcast_to(column[None], (count // 2, 5, 48, 128)),...  13.8 us
    unnamed x6, local copies, waits for them, and re-layouts  2.8 us
  transfers between devices with their start and end apart: 9, of which 6 were waited for; matrix products, arithmetic and copies ran while one was open for 0% of the time, Pallas kernels for 4%

profile of v3, /device:TPU:33, one launch (start us, length us, event | category | flops | bytes accessed | tf_op | source)
XLA Modules:
  0.0 125.7 jit_solution(608956323608873955)
XLA Ops:
  0.0 0.1 pad_add_fusion.place
  0.1 0.0 copy-start
  0.1 1.0 copy-done
  1.1 0.0 copy-start.1
  1.1 0.9 copy-done.1
  2.0 0.0 copy-start.2
  2.0 0.9 copy-done.2
  2.9 1.1 cut0.1
  4.0 0.1 collective-permute-start
  4.1 5.2 %collective-permute-start.1 = (f32[5,16,8,128]{3,2,1,0:T(8,128)S(1)}, f32[5,16,8,128]{3,2,1,0:T(8,128)S(1)}, u32[]{:S(2)}, u32[]{:S(2)}) collective-permute-start(f32[5,16,8,128]{3,2,1,0:T(8,128)S(1)} %get-tuple-element.35), channel_id=1, source_target_pairs={{1,2},{3,4},{5,6},{7,8},{9,10},{11,12},{13,14},{15,16},{17,18},{19... | collective-permute-start | bytes 983048 | tf_op jit(solution)/shard_map/ppermute | solution.py:672
  9.3 3.4 %collective-permute-done.first = f32[5,16,8,128]{3,2,1,0:T(8,128)S(1)} collective-permute-done((f32[5,16,8,128]{3,2,1,0:T(8,128)S(1)}, f32[5,16,8,128]{3,2,1,0:T(8,128)S(1)}, u32[]{:S(2)}, u32[]{:S(2)}) %collective-permute-start) | collective-permute-done | bytes 327712 | tf_op jit(solution)/shard_map/ppermute | solution.py:672
  12.7 3.7 %collective-permute-done.1.second = f32[5,16,8,128]{3,2,1,0:T(8,128)S(1)} collective-permute-done((f32[5,16,8,128]{3,2,1,0:T(8,128)S(1)}, f32[5,16,8,128]{3,2,1,0:T(8,128)S(1)}, u32[]{:S(2)}, u32[]{:S(2)}) %collective-permute-start.1) | collective-permute-done | bytes 327712 | tf_op jit(solution)/shard_map/ppermute | solution.py:672
  16.4 0.7 join0.1
  17.0 1.7 %collective-permute-start.2 = (f32[5,8,32,128]{3,2,1,0:T(8,128)S(1)}, f32[5,8,32,128]{3,2,1,0:T(8,128)S(1)}, u32[]{:S(2)}, u32[]{:S(2)}) collective-permute-start(f32[5,8,32,128]{3,2,1,0:T(8,128)S(1)} %get-tuple-element.36.near), channel_id=1, source_target_pairs={{0,32},{64,96},{128,160},{192,224},{32,0},{96,64},{160,128},{224,1... | collective-permute-start | bytes 1966088 | tf_op jit(solution)/shard_map/ppermute | solution.py:672
  18.7 3.1 %collective-permute-start.3 = (f32[5,8,32,128]{3,2,1,0:T(8,128)S(1)}, f32[5,8,32,128]{3,2,1,0:T(8,128)S(1)}, u32[]{:S(2)}, u32[]{:S(2)}) collective-permute-start(f32[5,8,32,128]{3,2,1,0:T(8,128)S(1)} %get-tuple-element.37.far), channel_id=1, source_target_pairs={{32,64},{96,128},{160,192},{64,32},{128,96},{192,160},{33,65},{97,... | collective-permute-start | bytes 1966088 | tf_op jit(solution)/shard_map/ppermute | solution.py:672
  21.8 3.9 %inner0.1 = (f32[5,32,32,128]{3,2,1,0:T(8,128)S(1)}, f32[7,32,32,128]{3,2,1,0:T(8,128)S(1)}, f32[3,32,32,128]{3,2,1,0:T(8,128)S(1)}, f32[3,32,32,128]{3,2,1,0:T(8,128)S(1)}, f32[3,32,32,128]{3,2,1,0:T(8,128)S(1)}) custom-call(s32[4]{0:T(128)S(1)} %pad_add_fusion.place, f32[5,8,32,128]{3,2,1,0:T(8,128)S(1)} %get-tuple-element.36.near, ...), custom_call_target="tpu_custom_call" | custom-call | tf_op jit(solution)/shard_map/inner0/pallas_call | solution.py:203
  25.8 0.0 collective-permute-done.2.near
  25.8 4.8 %collective-permute-done.3.far = f32[5,8,32,128]{3,2,1,0:T(8,128)S(1)} collective-permute-done((f32[5,8,32,128]{3,2,1,0:T(8,128)S(1)}, f32[5,8,32,128]{3,2,1,0:T(8,128)S(1)}, u32[]{:S(2)}, u32[]{:S(2)}) %collective-permute-start.3) | collective-permute-done | bytes 655392 | tf_op jit(solution)/shard_map/ppermute | solution.py:672
  30.6 7.4 %outer0.1 = (f32[5,32,32,128]{3,2,1,0:T(8,128)S(1)}, f32[7,32,32,128]{3,2,1,0:T(8,128)S(1)}, f32[3,32,32,128]{3,2,1,0:T(8,128)S(1)}, f32[3,32,32,128]{3,2,1,0:T(...) custom-call(s32[4]{0:T(128)S(1)} %pad_add_fusion.place, ...), custom_call_target="tpu_custom_call", output_to_operand_aliasing={{0}: (3, {}), {1}: (4, {}), {2}: (5, {}), {3}: (6, {}), {4}... | custom-call | tf_op jit(solution)/shard_map/outer0/pallas_call | solution.py:203
  38.0 0.1 collective-permute-start.4
  38.1 5.5 %collective-permute-start.5 = (f32[5,8,8,128]{3,2,1,0:T(8,128)S(1)}, f32[5,8,8,128]{3,2,1,0:T(8,128)S(1)}, u32[]{:S(2)}, u32[]{:S(2)}) collective-permute-start(f32[5,8,8,128]{3,2,1,0:T(8,128)S(1)} %get-tuple-element.45), channel_id=1, source_target_pairs={{1,2},{3,4},{5,6},{7,8},{9,10},{11,12},{13,14},{15,16},{17,18},{19... | collective-permute-start | bytes 491528 | tf_op jit(solution)/shard_map/ppermute | solution.py:672
  43.6 0.0 collective-permute-done.4.first
  43.6 2.7 %collective-permute-done.5.second = f32[5,8,8,128]{3,2,1,0:T(8,128)S(1)} collective-permute-done((f32[5,8,8,128]{3,2,1,0:T(8,128)S(1)}, f32[5,8,8,128]{3,2,1,0:T(8,128)S(1)}, u32[]{:S(2)}, u32[]{:S(2)}) %collective-permute-start.5) | collective-permute-done | bytes 163872 | tf_op jit(solution)/shard_map/ppermute | solution.py:672
  46.2 0.8 cut1.1
  47.0 0.1 collective-permute-start.6
  47.1 5.5 %collective-permute-start.7 = (f32[5,4,32,128]{3,2,1,0:T(8,128)S(1)}, f32[5,4,32,128]{3,2,1,0:T(8,128)S(1)}, u32[]{:S(2)}, u32[]{:S(2)}) collective-permute-start(f32[5,4,32,128]{3,2,1,0:T(8,128)S(1)} %get-tuple-element.48), channel_id=1, source_target_pairs={{32,64},{96,128},{160,192},{64,32},{128,96},{192,160},{33,65},{97,... | collective-permute-start | bytes 983048 | tf_op jit(solution)/shard_map/ppermute | solution.py:672
  52.7 0.0 collective-permute-done.6.near
  52.7 4.7 %collective-permute-done.7.far = f32[5,4,32,128]{3,2,1,0:T(8,128)S(1)} collective-permute-done((f32[5,4,32,128]{3,2,1,0:T(8,128)S(1)}, f32[5,4,32,128]{3,2,1,0:T(8,128)S(1)}, u32[]{:S(2)}, u32[]{:S(2)}) %collective-permute-start.7) | collective-permute-done | bytes 327712 | tf_op jit(solution)/shard_map/ppermute | solution.py:672
  57.4 6.5 %down1.1 = (f32[5,16,32,128]{3,2,1,0:T(8,128)S(1)}, f32[3,16,32,128]{3,2,1,0:T(8,128)S(1)}, f32[5,16,128]{2,1,0:T(8,128)S(1)}, f32[7,16,32,128]{3,2,1,0:T(8,128)S(1)}) custom-call(s32[4]{0:T(128)S(1)} %pad_add_fusion.place, f32[5,8,32,128]{3,2,1,0:T(8,128)S(1)} %get-tuple-element.46.centre, f32[5,4,32,128]{3,2,1,0:T(8,128)S(1)} %collective-permute-done.6.near, ...), custom_call_target="tpu_custom_call" | custom-call | tf_op jit(solution)/shard_map/down1/pallas_call | solution.py:203
  64.0 20.9 %all_to_all.10.parts = f32[32,5,4,128]{3,2,1,0:T(4,128)S(1)} all-to-all(f32[32,5,4,128]{3,2,1,0:T(4,128)S(1)} %broadcast_in_dim.4), channel_id=1, replica_groups=mesh['grp'=8,'brick'=32] {'brick'}, dimensions={0} | all-to-all | bytes 655360 | tf_op jit(solution)/shard_map/all_to_all | solution.py:730
  84.9 0.6 column.1
  85.6 13.8 %all_to_all.11.mine = f32[4,5,48,128]{3,2,1,0:T(8,128)S(1)} all-to-all(f32[4,5,48,128]{3,2,1,0:T(8,128)S(1)} %broadcast_in_dim.5), channel_id=1, replica_groups={{0,64,128,192},{32,96,160,224},{1,65,129,193},{33,97,161,225},{2,66,130..., dimensions={0} | all-to-all | bytes 983040 | tf_op jit(solution)/shard_map/all_to_all | solution.py:732
  99.3 3.2 %collective-permute-start.8 = (f32[4,5,48,128]{3,2,1,0:T(8,128)S(1)}, f32[4,5,48,128]{3,2,1,0:T(8,128)S(1)}, u32[]{:S(2)}, u32[]{:S(2)}) collective-permute-start(f32[4,5,48,128]{3,2,1,0:T(8,128)S(1)} %all_to_all.11.mine), channel_id=1, source_target_pairs={{0,32},{64,96},{128,160},{192,224},{32,0},{96,64},{160,128},{224,1... | collective-permute-start | bytes 1474568 | tf_op jit(solution)/shard_map/ppermute | solution.py:672
  102.5 0.7 trim0.1
  103.2 0.7 trim1.1
  103.9 0.1 collective-permute-done.8.other
  104.0 21.8 %climb.1 = f32[3,16,16,128]{3,2,1,0:T(8,128)} custom-call(s32[4]{0:T(128)S(1)} %pad_add_fusion.place, f32[4,5,48,128]{3,2,1,0:T(8,128)S(1)} %all_to_all.11.mine, f32[4,5,48,128]{3,2,1,0:T(8,128)S(1)} %collective-permute-done.8.other, f32[3,12,24,128]{3,2,1,0:T(8,128)S(1)} %get-tuple-element.53.data1, f32[3,12,24,128]{3,2,1,0:T(8,128)S(1)} %get-tuple-element.54.saved1, ...), custom_call_target="tpu_custom_call" | custom-call | tf_op jit(solution)/shard_map/climb/pallas_call | solution.py:203
  (3 shorter events, 0.1 us)
Async XLA Ops:
  0.1 1.0 copy-start
  1.1 0.9 copy-start.1
  2.0 0.9 copy-start.2
  4.0 8.7 %collective-permute-start = (f32[5,16,8,128]{3,2,1,0:T(8,128)S(1)}, f32[5,16,8,128]{3,2,1,0:T(8,128)S(1)}, u32[]{:S(2)}, u32[]{:S(2)}) collective-permute-start(f32[5,16,8,128]{3,2,1,0:T(8,128)S(1)} %get-tuple-element.34), channel_id=1, source_target_pairs={{0,1},{2,3},{4,5},{6,7},{8,9},{10,11},{12,13},{14,15},{16,17},{18,... | collective-permute-start | bytes 983048 | tf_op jit(solution)/shard_map/ppermute | solution.py:672
  4.1 12.2 %collective-permute-start.1 = (f32[5,16,8,128]{3,2,1,0:T(8,128)S(1)}, f32[5,16,8,128]{3,2,1,0:T(8,128)S(1)}, u32[]{:S(2)}, u32[]{:S(2)}) collective-permute-start(f32[5,16,8,128]{3,2,1,0:T(8,128)S(1)} %get-tuple-element.35), channel_id=1, source_target_pairs={{1,2},{3,4},{5,6},{7,8},{9,10},{11,12},{13,14},{15,16},{17,18},{19... | collective-permute-start | bytes 983048 | tf_op jit(solution)/shard_map/ppermute | solution.py:672
  17.0 8.7 %collective-permute-start.2 = (f32[5,8,32,128]{3,2,1,0:T(8,128)S(1)}, f32[5,8,32,128]{3,2,1,0:T(8,128)S(1)}, u32[]{:S(2)}, u32[]{:S(2)}) collective-permute-start(f32[5,8,32,128]{3,2,1,0:T(8,128)S(1)} %get-tuple-element.36.near), channel_id=1, source_target_pairs={{0,32},{64,96},{128,160},{192,224},{32,0},{96,64},{160,128},{224,1... | collective-permute-start | bytes 1966088 | tf_op jit(solution)/shard_map/ppermute | solution.py:672
  18.7 11.9 %collective-permute-start.3 = (f32[5,8,32,128]{3,2,1,0:T(8,128)S(1)}, f32[5,8,32,128]{3,2,1,0:T(8,128)S(1)}, u32[]{:S(2)}, u32[]{:S(2)}) collective-permute-start(f32[5,8,32,128]{3,2,1,0:T(8,128)S(1)} %get-tuple-element.37.far), channel_id=1, source_target_pairs={{32,64},{96,128},{160,192},{64,32},{128,96},{192,160},{33,65},{97,... | collective-permute-start | bytes 1966088 | tf_op jit(solution)/shard_map/ppermute | solution.py:672
  38.0 5.6 %collective-permute-start.4 = (f32[5,8,8,128]{3,2,1,0:T(8,128)S(1)}, f32[5,8,8,128]{3,2,1,0:T(8,128)S(1)}, u32[]{:S(2)}, u32[]{:S(2)}) collective-permute-start(f32[5,8,8,128]{3,2,1,0:T(8,128)S(1)} %get-tuple-element.44), channel_id=1, source_target_pairs={{0,1},{2,3},{4,5},{6,7},{8,9},{10,11},{12,13},{14,15},{16,17},{18,... | collective-permute-start | bytes 491528 | tf_op jit(solution)/shard_map/ppermute | solution.py:672
  38.1 8.2 %collective-permute-start.5 = (f32[5,8,8,128]{3,2,1,0:T(8,128)S(1)}, f32[5,8,8,128]{3,2,1,0:T(8,128)S(1)}, u32[]{:S(2)}, u32[]{:S(2)}) collective-permute-start(f32[5,8,8,128]{3,2,1,0:T(8,128)S(1)} %get-tuple-element.45), channel_id=1, source_target_pairs={{1,2},{3,4},{5,6},{7,8},{9,10},{11,12},{13,14},{15,16},{17,18},{19... | collective-permute-start | bytes 491528 | tf_op jit(solution)/shard_map/ppermute | solution.py:672
  47.0 5.6 %collective-permute-start.6 = (f32[5,4,32,128]{3,2,1,0:T(8,128)S(1)}, f32[5,4,32,128]{3,2,1,0:T(8,128)S(1)}, u32[]{:S(2)}, u32[]{:S(2)}) collective-permute-start(f32[5,4,32,128]{3,2,1,0:T(8,128)S(1)} %get-tuple-element.47), channel_id=1, source_target_pairs={{0,32},{64,96},{128,160},{192,224},{32,0},{96,64},{160,128},{224,1... | collective-permute-start | bytes 983048 | tf_op jit(solution)/shard_map/ppermute | solution.py:672
  47.1 10.3 %collective-permute-start.7 = (f32[5,4,32,128]{3,2,1,0:T(8,128)S(1)}, f32[5,4,32,128]{3,2,1,0:T(8,128)S(1)}, u32[]{:S(2)}, u32[]{:S(2)}) collective-permute-start(f32[5,4,32,128]{3,2,1,0:T(8,128)S(1)} %get-tuple-element.48), channel_id=1, source_target_pairs={{32,64},{96,128},{160,192},{64,32},{128,96},{192,160},{33,65},{97,... | collective-permute-start | bytes 983048 | tf_op jit(solution)/shard_map/ppermute | solution.py:672
  99.3 4.6 %collective-permute-start.8 = (f32[4,5,48,128]{3,2,1,0:T(8,128)S(1)}, f32[4,5,48,128]{3,2,1,0:T(8,128)S(1)}, u32[]{:S(2)}, u32[]{:S(2)}) collective-permute-start(f32[4,5,48,128]{3,2,1,0:T(8,128)S(1)} %all_to_all.11.mine), channel_id=1, source_target_pairs={{0,32},{64,96},{128,160},{192,224},{32,0},{96,64},{160,128},{224,1... | collective-permute-start | bytes 1474568 | tf_op jit(solution)/shard_map/ppermute | solution.py:672

commit v4 on v3

--- a/solution.py
+++ b/solution.py
@@ -14,6 +14,7 @@
 NEAR = 10
 SKIRT = 12
 REACH = 5
+CUT_LIMIT = 28 * 2**20
 F32 = jnp.float32
 
 
@@ -55,7 +56,8 @@
 
 
 class Level:
-    def __init__(self, scale, depth, rows, height):
+    def __init__(self, scale, depth, rows, height, unroll=4):
+        self.unroll = unroll
         self.scale = scale
         self.depth = depth
         self.groups = LANES // depth
@@ -125,7 +127,7 @@
         ghosts(level, state, (c,))
 
 
-def sweep(level, src, coef, state, lo, hi, emit):
+def sweep(level, src, coef, state, lo, hi, prepare, emit):
     kx, ky, kym, kz, kzm, diag, inv = coef
     front, back = level.lanes()
     bulk = BETA * level.scale
@@ -140,6 +142,7 @@
 
     def body(i, before):
         here = spread(i)
+        extra = prepare(i)
         for c in range(3):
             u = state[c, i]
             flux = kx[i] * state[c, i + 1] + kx[i - 1] * state[c, i - 1]
@@ -152,33 +155,33 @@
             else:
                 other = jnp.where(front, bulk * u, behind_z(here))
             resid = src[c, i] - diag[i] * u + flux + (here - other)
-            emit(i, c, u, resid)
+            emit(i, c, u, resid, extra)
         return here
 
-    lax.fori_loop(lo, hi, body, spread(lo - 1), unroll=4)
+    lax.fori_loop(lo, hi, body, spread(lo - 1), unroll=level.unroll)
 
 
 def step(level, number, src, coef, state, fresh, direction, lo, hi):
     keep, gain = STEPS[number]
     inv = coef[6]
 
-    def emit(i, c, u, resid):
-        move = (gain * inv[i]) * resid
+    def emit(i, c, u, resid, scaled):
+        move = scaled * resid
         if number > 0:
             move = move + keep * direction[c, i]
         direction[c, i] = move
         fresh[c, i] = u + move
 
-    sweep(level, src, coef, state, lo, hi, emit)
+    sweep(level, src, coef, state, lo, hi, lambda i: gain * inv[i], emit)
     for c in range(3):
         ghosts(level, fresh, (c,))
 
 
 def residual(level, src, coef, state, out, lo, hi):
-    def emit(i, c, u, resid):
+    def emit(i, c, u, resid, extra):
         out[c, i] = resid
 
-    sweep(level, src, coef, state, lo, hi, emit)
+    sweep(level, src, coef, state, lo, hi, lambda i: None, emit)
 
 
 def pick(rows, cols, rule, value):
@@ -224,63 +227,65 @@
         act(False)
 
 
-def cut_kernel(place, f, k, r, own, first, second, sems):
-    copies = [
-        pltpu.make_async_copy(f, own.at[0:3], sems.at[0]),
-        pltpu.make_async_copy(k, own.at[3], sems.at[1]),
-        pltpu.make_async_copy(r, own.at[4], sems.at[2]),
-    ]
-    for copy in copies:
-        copy.start()
-    for copy in copies:
-        copy.wait()
-
+def cut_kernel(place, f, k, r, first, second, sems):
     def act(even):
-        lo, hi = (second, first) if even else (first, second)
-        lo[...] = own[:, :, 0:HALO]
-        hi[...] = own[:, :, HALO : 2 * HALO]
+        copies = []
+        for side, out in enumerate((second, first) if even else (first, second)):
+            rows = pl.ds(HALO * side, HALO)
+            copies += [
+                pltpu.make_async_copy(f.at[:, :, rows], out.at[0:3], sems.at[3 * side]),
+                pltpu.make_async_copy(k.at[:, rows], out.at[3], sems.at[3 * side + 1]),
+                pltpu.make_async_copy(r.at[:, rows], out.at[4], sems.at[3 * side + 2]),
+            ]
+        for copy in copies:
+            copy.start()
+        for copy in copies:
+            copy.wait()
 
     by_parity(place[1], act)
 
 
 def cut(place, f, k, r):
-    block = (5, 16, 16, LANES)
-    strip = (5, 16, HALO, LANES)
     return pl.pallas_call(
         cut_kernel,
-        out_shape=[jax.ShapeDtypeStruct(shape, F32) for shape in (block, strip, strip)],
+        out_shape=[jax.ShapeDtypeStruct((5, 16, HALO, LANES), F32)] * 2,
         in_specs=[pl.BlockSpec(memory_space=pltpu.SMEM)]
         + [pl.BlockSpec(memory_space=pltpu.HBM)] * 3,
-        out_specs=vmem(3),
-        scratch_shapes=[pltpu.SemaphoreType.DMA((3,))],
-        compiler_params=pltpu.CompilerParams(vmem_limit_bytes=28 * 2**20),
+        out_specs=vmem(2),
+        scratch_shapes=[pltpu.SemaphoreType.DMA((6,))],
+        compiler_params=pltpu.CompilerParams(vmem_limit_bytes=CUT_LIMIT),
         name="cut0",
     )(place, f, k, r)
 
 
-def join_kernel(place, own, first, second, near, far):
-    def sides(swapped):
-        lo, hi = (second, first) if swapped else (first, second)
-
-        def act(even):
-            for half, out in enumerate((far, near) if even else (near, far)):
-                rows = slice(8 * half, 8 * half + 8)
-                for q in range(5):
-                    out[q, :, 0:8] = lo[q, rows]
-                    out[q, :, 8:24] = own[q, rows]
-                    out[q, :, 24:32] = hi[q, rows]
-
-        by_parity(place[0], act)
+MESSAGE = [(0, 0, 7), (1, 7, 7), (2, 14, 7), (4, 21, 7), (3, 28, 8)]
+
+
+def join_kernel(place, f, k, r, first, second, data, near, far):
+    def sides(even):
+        lo, hi = (second, first) if even else (first, second)
+        for q in range(5):
+            data[q, 8:24, 0:8] = lo[q]
+            data[q, 8:24, 8:24] = f[q] if q < 3 else (k, r)[q - 3][...]
+            data[q, 8:24, 24:32] = hi[q]
 
     by_parity(place[1], sides)
+
+    def act(even):
+        up, down = (near, far) if even else (far, near)
+        for q, at, rows in MESSAGE:
+            down[at : at + rows] = data[q, 8 : 8 + rows]
+            up[at : at + rows] = data[q, 24 - rows : 24]
+
+    by_parity(place[0], act)
 
 
 FINE = Level(1.0, 128, 30, 32)
 FINE_UP = Level(1.0, 128, 22, 24)
 MIDDLE = Level(0.25, 64, 14, 32)
-MIDDLE_UP = Level(0.25, 64, 10, 24)
-COARSE = Level(0.0625, 32, 8, 48)
-COARSE_UP = Level(0.0625, 32, 8, 32)
+MIDDLE_UP = Level(0.25, 64, 10, 24, 5)
+COARSE = Level(0.0625, 32, 8, 48, 8)
+COARSE_UP = Level(0.0625, 32, 8, 32, 8)
 LAST = Level(0.015625, 16, 2, 24)
 
 
@@ -299,29 +304,29 @@
     return inside
 
 
-def fine_inner(place, near, far, data, kept, s0, d0, t0):
+def fine_inner(place, given, near_in, data, kept, s0, d0, t0, resid, near):
     coef = [kept.at[j] for j in range(7)]
-
-    def act(even):
-        for number, part in enumerate((far, near) if even else (near, far)):
-            data[:, 8 * number + 8 : 8 * number + 16] = part[...]
-
-    by_parity(place[0], act)
     setup(FINE, lambda i: data[3, i], lambda i: data[4, i], coef, fine_inside(place), 9, 23)
     begin(FINE, data, coef, s0, d0, 9, 23)
     step(FINE, 1, data, coef, s0, t0, d0, 10, 22)
     step(FINE, 2, data, coef, t0, s0, d0, 11, 21)
     step(FINE, 3, data, coef, s0, t0, d0, 12, 20)
+    residual(FINE, data, coef, t0, resid, 13, 19)
 
 
 def fine_outer(place, near, far, *refs):
-    data, kept, s0, d0, t0, saved, packed, first, second, sums, resid = refs[5:]
+    data, kept, s0, d0, t0, resid, saved, packed, first, second, sums = refs[6:]
     coef = [kept.at[j] for j in range(7)]
+    zero = jnp.zeros((32, LANES), F32)
 
     def act(even):
         lo, hi = (far, near) if even else (near, far)
-        data[:, 0:8] = lo[...]
-        data[:, 24:32] = hi[...]
+        for q, at, rows in MESSAGE:
+            data[q, 8 - rows : 8] = lo[at : at + rows]
+            data[q, 24 : 24 + rows] = hi[at : at + rows]
+            if rows < 8:
+                data[q, 0] = zero
+                data[q, 31] = zero
 
     by_parity(place[0], act)
     inside = fine_inside(place)
@@ -335,7 +340,8 @@
     for lo, hi in ((4, 12), (20, 28)):
         step(FINE, 3, data, coef, s0, t0, d0, lo, hi)
     saved[...] = t0[:, 4:28, 4:28]
-    residual(FINE, data, coef, t0, resid, 6, 26)
+    residual(FINE, data, coef, t0, resid, 6, 13)
+    residual(FINE, data, coef, t0, resid, 19, 26)
     pair = s0.at[0]
     wide = sums
     for q in range(5):
@@ -372,7 +378,7 @@
         kept_up[j] = kept[j, 4:28, 4:28]
 
 
-def middle_cut(place, own, first, second, near, far, centre):
+def middle_cut(place, own, first, second, trimmed, near, far, centre):
     low = lane_of((32, LANES)) < 64
     zero = jnp.zeros((4, LANES), F32)
 
@@ -659,11 +665,11 @@
     step(FINE_UP, 2, data0, coef0, s0, t0, d0, 3, 21)
     keep, gain = STEPS[3]
 
-    def emit(i, c, u, resid):
-        move = (gain * coef0[6][i]) * resid + keep * d0[c, i]
+    def emit(i, c, u, resid, scaled):
+        move = scaled * resid + keep * d0[c, i]
         out[c, i - 4] = (u + move)[4:20]
 
-    sweep(FINE_UP, data0, coef0, t0, 4, 20, emit)
+    sweep(FINE_UP, data0, coef0, t0, 4, 20, lambda i: gain * coef0[6][i], emit)
 
 
 def swap(value, axis, first):
@@ -678,26 +684,43 @@
     place = jnp.stack(
         [lax.axis_index("grp"), lax.axis_index("brick"), jnp.int32(count), jnp.int32(bricks)]
     ).astype(jnp.int32)
-    own, first, second = cut(place, right_side, stiffness, reaction)
+    local = (right_side, stiffness, reaction)
+    first, second = cut(place, *local)
     first = swap(first, "brick", 0)
     second = swap(second, "brick", 1)
-    near, far = call(
-        join_kernel, [(5, 8, 32, 128)] * 2, [], place, own, first, second, name="join0"
+    data0, near, far = call(
+        join_kernel,
+        [FINE.shape(5)] + [(36, 32, 128)] * 2,
+        [],
+        place,
+        *local,
+        first,
+        second,
+        name="join0",
     )
     far_in = swap(far, "grp", 1)
+    states = [FINE.shape(5), FINE.shape(7)] + [FINE.shape(3)] * 4
+    *inner, near = call(
+        fine_inner,
+        states + [(36, 32, 128)],
+        [],
+        place,
+        data0,
+        near,
+        name="inner0",
+        aliases={1: 0, 2: 6},
+    )
     near_in = swap(near, "grp", 0)
-    states = [FINE.shape(5), FINE.shape(7)] + [FINE.shape(3)] * 3
-    inner = call(fine_inner, states, [], place, near, far, name="inner0")
-    data0, kept0, _, _, _, saved0, packed1, first, second = call(
+    data0, kept0, _, _, _, _, saved0, packed1, first, second = call(
         fine_outer,
         states + [(3, 24, 24, 128), (5, 8, 16, 128)] + [(5, 8, 8, 128)] * 2,
-        [(5, 8, 16, 256), FINE.shape(3)],
+        [(5, 8, 16, 256)],
         place,
         near_in,
         far_in,
         *inner,
         name="outer0",
-        aliases={3 + j: j for j in range(5)},
+        aliases={3 + j: j for j in range(6)},
     )
     first = swap(first, "brick", 0)
     second = swap(second, "brick", 1)
@@ -712,6 +735,7 @@
         packed1,
         first,
         second,
+        data0,
         name="cut1",
     )
     far_in = swap(far, "grp", 1)

time: 126 us -> 121 us (0.960)
  Pallas kernels: 44.2 us -> 41.3 us
    pallas_call x9, Pallas kernels: 43 us -> 40.6 us  [call(): pl.pallas_call(kernel, out_shape=[jax.ShapeDtypeStruct(s, F32) for s in o...]
  transfers between devices with their start and end apart: 9 -> 9, of which waited for: 6 -> 6; matrix products, arithmetic and copies ran while one was open for 0% -> 0% of each run, Pallas kernels for 4% -> 5%
where the time goes in v4:
time: 121 us
  Pallas kernels  41.3 us (34%)
  blocking collectives  34.6 us (29%)
  starting transfers between devices  23.2 us (19%)
  waiting for transfers between devices  18.9 us (16%)
  local copies, waits for them, and re-layouts  2.89 us (2%)
    pallas_call x9, Pallas kernels, call(): pl.pallas_call(kernel, out_shape=[jax.ShapeDtypeStruct(s, F32) for s in o...  40.6 us
    ppermute x9, starting transfers between devices, swap(): return lax.ppermute(value, axis, ends + [(b, a) for a, b in ends])  23.2 us
    all_to_all x1, blocking collectives, on_device(): lax.all_to_all(jnp.broadcast_to(block[None], (bricks, 5, 4, 128)), 'brick...  20.9 us
    ppermute x9, waiting for transfers between devices, swap(): return lax.ppermute(value, axis, ends + [(b, a) for a, b in ends])  18.9 us
    all_to_all x1, blocking collectives, on_device(): lax.all_to_all(jnp.broadcast_to(column[None], (count // 2, 5, 48, 128)),...  13.6 us
    unnamed x6, local copies, waits for them, and re-layouts  2.8 us
  transfers between devices with their start and end apart: 9, of which 6 were waited for; matrix products, arithmetic and copies ran while one was open for 0% of the time, Pallas kernels for 5%

profile of v4, /device:TPU:33, one launch (start us, length us, event | category | flops | bytes accessed | tf_op | source)
XLA Modules:
  0.0 121.1 jit_solution(2825731960745160650)
XLA Ops:
  0.0 0.1 pad_add_fusion.place
  0.1 0.0 copy-start
  0.1 1.0 copy-done
  1.1 0.0 copy-start.1
  1.1 0.9 copy-done.1
  2.0 0.0 copy-start.2
  2.0 0.9 copy-done.2
  2.9 0.7 cut0.1
  3.6 0.1 collective-permute-start
  3.7 5.2 %collective-permute-start.1 = (f32[5,16,8,128]{3,2,1,0:T(8,128)S(1)}, f32[5,16,8,128]{3,2,1,0:T(8,128)S(1)}, u32[]{:S(2)}, u32[]{:S(2)}) collective-permute-start(f32[5,16,8,128]{3,2,1,0:T(8,128)S(1)} %get-tuple-element.36), channel_id=1, source_target_pairs={{1,2},{3,4},{5,6},{7,8},{9,10},{11,12},{13,14},{15,16},{17,18},{19... | collective-permute-start | bytes 983048 | tf_op jit(solution)/shard_map/ppermute | solution.py:678
  8.8 3.4 %collective-permute-done.first = f32[5,16,8,128]{3,2,1,0:T(8,128)S(1)} collective-permute-done((f32[5,16,8,128]{3,2,1,0:T(8,128)S(1)}, f32[5,16,8,128]{3,2,1,0:T(8,128)S(1)}, u32[]{:S(2)}, u32[]{:S(2)}) %collective-permute-start) | collective-permute-done | bytes 327712 | tf_op jit(solution)/shard_map/ppermute | solution.py:678
  12.2 3.7 %collective-permute-done.1.second = f32[5,16,8,128]{3,2,1,0:T(8,128)S(1)} collective-permute-done((f32[5,16,8,128]{3,2,1,0:T(8,128)S(1)}, f32[5,16,8,128]{3,2,1,0:T(8,128)S(1)}, u32[]{:S(2)}, u32[]{:S(2)}) %collective-permute-start.1) | collective-permute-done | bytes 327712 | tf_op jit(solution)/shard_map/ppermute | solution.py:678
  15.9 0.7 join0.1
  16.7 4.7 %collective-permute-start.3 = (f32[36,32,128]{2,1,0:T(8,128)S(1)}, f32[36,32,128]{2,1,0:T(8,128)S(1)}, u32[]{:S(2)}, u32[]{:S(2)}) collective-permute-start(f32[36,32,128]{2,1,0:T(8,128)S(1)} %get-tuple-element.40), channel_id=1, source_target_pairs={{32,64},{96,128},{160,192},{64,32},{128,96},{192,160},{33,65},{97,... | collective-permute-start | bytes 1769480 | tf_op jit(solution)/shard_map/ppermute | solution.py:678
  21.3 4.4 %inner0.1 = (f32[5,32,32,128]{3,2,1,0:T(8,128)S(1)}, f32[7,32,32,128]{3,2,1,0:T(8,128)S(1)}, f32[3,32,32,128]{3,2,1,0:T(8,128)S(1)}, f32[3,32,32,128]{3,2,1,0:T(...) custom-call(s32[4]{0:T(128)S(1)} %pad_add_fusion.place, ...), custom_call_target="tpu_custom_call", output_to_operand_aliasing={{0}: (1, {}), {6}: (2, {})} | custom-call | tf_op jit(solution)/shard_map/inner0/pallas_call | solution.py:206
  25.7 0.1 collective-permute-start.2
  25.8 3.1 %collective-permute-done.3.far = f32[36,32,128]{2,1,0:T(8,128)S(1)} collective-permute-done((f32[36,32,128]{2,1,0:T(8,128)S(1)}, f32[36,32,128]{2,1,0:T(8,128)S(1)}, u32[]{:S(2)}, u32[]{:S(2)}) %collective-permute-start.3) | collective-permute-done | bytes 589856 | tf_op jit(solution)/shard_map/ppermute | solution.py:678
  28.9 0.0 collective-permute-done.2.near
  28.9 7.4 %outer0.1 = (f32[5,32,32,128]{3,2,1,0:T(8,128)S(1)}, f32[7,32,32,128]{3,2,1,0:T(8,128)S(1)}, f32[3,32,32,128]{3,2,1,0:T(8,128)S(1)}, f32[3,32,32,128]{3,2,1,0:T(...) custom-call(s32[4]{0:T(128)S(1)} %pad_add_fusion.place, ...), custom_call_target="tpu_custom_call", output_to_operand_aliasing={{0}: (3, {}), {1}: (4, {}), {2}: (5, {}), {3}: (6, {}), {4}... | custom-call | tf_op jit(solution)/shard_map/outer0/pallas_call | solution.py:206
  36.3 0.1 collective-permute-start.4
  36.4 5.5 %collective-permute-start.5 = (f32[5,8,8,128]{3,2,1,0:T(8,128)S(1)}, f32[5,8,8,128]{3,2,1,0:T(8,128)S(1)}, u32[]{:S(2)}, u32[]{:S(2)}) collective-permute-start(f32[5,8,8,128]{3,2,1,0:T(8,128)S(1)} %get-tuple-element.49), channel_id=1, source_target_pairs={{1,2},{3,4},{5,6},{7,8},{9,10},{11,12},{13,14},{15,16},{17,18},{19... | collective-permute-start | bytes 491528 | tf_op jit(solution)/shard_map/ppermute | solution.py:678
  41.9 0.7 trim0.1
  42.7 0.0 collective-permute-done.4.first
  42.7 3.2 %collective-permute-done.5.second = f32[5,8,8,128]{3,2,1,0:T(8,128)S(1)} collective-permute-done((f32[5,8,8,128]{3,2,1,0:T(8,128)S(1)}, f32[5,8,8,128]{3,2,1,0:T(8,128)S(1)}, u32[]{:S(2)}, u32[]{:S(2)}) %collective-permute-start.5) | collective-permute-done | bytes 163872 | tf_op jit(solution)/shard_map/ppermute | solution.py:678
  45.9 0.8 cut1.1
  46.6 0.3 collective-permute-start.6
  47.0 4.2 %collective-permute-start.7 = (f32[5,4,32,128]{3,2,1,0:T(8,128)S(1)}, f32[5,4,32,128]{3,2,1,0:T(8,128)S(1)}, u32[]{:S(2)}, u32[]{:S(2)}) collective-permute-start(f32[5,4,32,128]{3,2,1,0:T(8,128)S(1)} %get-tuple-element.55), channel_id=1, source_target_pairs={{32,64},{96,128},{160,192},{64,32},{128,96},{192,160},{33,65},{97,... | collective-permute-start | bytes 983048 | tf_op jit(solution)/shard_map/ppermute | solution.py:678
  51.2 0.0 collective-permute-done.6.near
  51.2 4.7 %collective-permute-done.7.far = f32[5,4,32,128]{3,2,1,0:T(8,128)S(1)} collective-permute-done((f32[5,4,32,128]{3,2,1,0:T(8,128)S(1)}, f32[5,4,32,128]{3,2,1,0:T(8,128)S(1)}, u32[]{:S(2)}, u32[]{:S(2)}) %collective-permute-start.7) | collective-permute-done | bytes 327712 | tf_op jit(solution)/shard_map/ppermute | solution.py:678
  55.9 6.5 %down1.1 = (f32[5,16,32,128]{3,2,1,0:T(8,128)S(1)}, f32[3,16,32,128]{3,2,1,0:T(8,128)S(1)}, f32[5,16,128]{2,1,0:T(8,128)S(1)}, f32[7,16,32,128]{3,2,1,0:T(8,128)S(1)}) custom-call(s32[4]{0:T(128)S(1)} %pad_add_fusion.place, f32[5,8,32,128]{3,2,1,0:T(8,128)S(1)} %get-tuple-element.53.centre, f32[5,4,32,128]{3,2,1,0:T(8,128)S(1)} %collective-permute-done.6.near, ...), custom_call_target="tpu_custom_call" | custom-call | tf_op jit(solution)/shard_map/down1/pallas_call | solution.py:206
  62.5 20.9 %all_to_all.10.parts = f32[32,5,4,128]{3,2,1,0:T(4,128)S(1)} all-to-all(f32[32,5,4,128]{3,2,1,0:T(4,128)S(1)} %broadcast_in_dim.4), channel_id=1, replica_groups=mesh['grp'=8,'brick'=32] {'brick'}, dimensions={0} | all-to-all | bytes 655360 | tf_op jit(solution)/shard_map/all_to_all | solution.py:754
  83.4 0.6 column.1
  84.0 13.6 %all_to_all.11.mine = f32[4,5,48,128]{3,2,1,0:T(8,128)S(1)} all-to-all(f32[4,5,48,128]{3,2,1,0:T(8,128)S(1)} %broadcast_in_dim.5), channel_id=1, replica_groups={{0,64,128,192},{32,96,160,224},{1,65,129,193},{33,97,161,225},{2,66,130..., dimensions={0} | all-to-all | bytes 983040 | tf_op jit(solution)/shard_map/all_to_all | solution.py:756
  97.7 3.1 %collective-permute-start.8 = (f32[4,5,48,128]{3,2,1,0:T(8,128)S(1)}, f32[4,5,48,128]{3,2,1,0:T(8,128)S(1)}, u32[]{:S(2)}, u32[]{:S(2)}) collective-permute-start(f32[4,5,48,128]{3,2,1,0:T(8,128)S(1)} %all_to_all.11.mine), channel_id=1, source_target_pairs={{0,32},{64,96},{128,160},{192,224},{32,0},{96,64},{160,128},{224,1... | collective-permute-start | bytes 1474568 | tf_op jit(solution)/shard_map/ppermute | solution.py:678
  100.8 0.7 trim1.1
  101.5 0.8 collective-permute-done.8.other
  102.3 18.8 %climb.1 = f32[3,16,16,128]{3,2,1,0:T(8,128)} custom-call(s32[4]{0:T(128)S(1)} %pad_add_fusion.place, f32[4,5,48,128]{3,2,1,0:T(8,128)S(1)} %all_to_all.11.mine, f32[4,5,48,128]{3,2,1,0:T(8,128)S(1)} %collective-permute-done.8.other, f32[3,12,24,128]{3,2,1,0:T(8,128)S(1)} %get-tuple-element.60.data1, f32[3,12,24,128]{3,2,1,0:T(8,128)S(1)} %get-tuple-element.61.saved1, ...), custom_call_target="tpu_custom_call" | custom-call | tf_op jit(solution)/shard_map/climb/pallas_call | solution.py:206
  (3 shorter events, 0.1 us)
Async XLA Ops:
  0.1 1.0 copy-start
  1.1 0.9 copy-start.1
  2.0 0.9 copy-start.2
  3.6 8.7 %collective-permute-start = (f32[5,16,8,128]{3,2,1,0:T(8,128)S(1)}, f32[5,16,8,128]{3,2,1,0:T(8,128)S(1)}, u32[]{:S(2)}, u32[]{:S(2)}) collective-permute-start(f32[5,16,8,128]{3,2,1,0:T(8,128)S(1)} %get-tuple-element.35), channel_id=1, source_target_pairs={{0,1},{2,3},{4,5},{6,7},{8,9},{10,11},{12,13},{14,15},{16,17},{18,... | collective-permute-start | bytes 983048 | tf_op jit(solution)/shard_map/ppermute | solution.py:678
  3.7 12.2 %collective-permute-start.1 = (f32[5,16,8,128]{3,2,1,0:T(8,128)S(1)}, f32[5,16,8,128]{3,2,1,0:T(8,128)S(1)}, u32[]{:S(2)}, u32[]{:S(2)}) collective-permute-start(f32[5,16,8,128]{3,2,1,0:T(8,128)S(1)} %get-tuple-element.36), channel_id=1, source_target_pairs={{1,2},{3,4},{5,6},{7,8},{9,10},{11,12},{13,14},{15,16},{17,18},{19... | collective-permute-start | bytes 983048 | tf_op jit(solution)/shard_map/ppermute | solution.py:678
  16.7 12.2 %collective-permute-start.3 = (f32[36,32,128]{2,1,0:T(8,128)S(1)}, f32[36,32,128]{2,1,0:T(8,128)S(1)}, u32[]{:S(2)}, u32[]{:S(2)}) collective-permute-start(f32[36,32,128]{2,1,0:T(8,128)S(1)} %get-tuple-element.40), channel_id=1, source_target_pairs={{32,64},{96,128},{160,192},{64,32},{128,96},{192,160},{33,65},{97,... | collective-permute-start | bytes 1769480 | tf_op jit(solution)/shard_map/ppermute | solution.py:678
  25.7 3.2 %collective-permute-start.2 = (f32[36,32,128]{2,1,0:T(8,128)S(1)}, f32[36,32,128]{2,1,0:T(8,128)S(1)}, u32[]{:S(2)}, u32[]{:S(2)}) collective-permute-start(f32[36,32,128]{2,1,0:T(8,128)S(1)} %get-tuple-element.39), channel_id=1, source_target_pairs={{0,32},{64,96},{128,160},{192,224},{32,0},{96,64},{160,128},{224,1... | collective-permute-start | bytes 1769480 | tf_op jit(solution)/shard_map/ppermute | solution.py:678
  36.3 6.3 %collective-permute-start.4 = (f32[5,8,8,128]{3,2,1,0:T(8,128)S(1)}, f32[5,8,8,128]{3,2,1,0:T(8,128)S(1)}, u32[]{:S(2)}, u32[]{:S(2)}) collective-permute-start(f32[5,8,8,128]{3,2,1,0:T(8,128)S(1)} %get-tuple-element.48), channel_id=1, source_target_pairs={{0,1},{2,3},{4,5},{6,7},{8,9},{10,11},{12,13},{14,15},{16,17},{18,... | collective-permute-start | bytes 491528 | tf_op jit(solution)/shard_map/ppermute | solution.py:678
  36.4 9.4 %collective-permute-start.5 = (f32[5,8,8,128]{3,2,1,0:T(8,128)S(1)}, f32[5,8,8,128]{3,2,1,0:T(8,128)S(1)}, u32[]{:S(2)}, u32[]{:S(2)}) collective-permute-start(f32[5,8,8,128]{3,2,1,0:T(8,128)S(1)} %get-tuple-element.49), channel_id=1, source_target_pairs={{1,2},{3,4},{5,6},{7,8},{9,10},{11,12},{13,14},{15,16},{17,18},{19... | collective-permute-start | bytes 491528 | tf_op jit(solution)/shard_map/ppermute | solution.py:678
  46.6 4.6 %collective-permute-start.6 = (f32[5,4,32,128]{3,2,1,0:T(8,128)S(1)}, f32[5,4,32,128]{3,2,1,0:T(8,128)S(1)}, u32[]{:S(2)}, u32[]{:S(2)}) collective-permute-start(f32[5,4,32,128]{3,2,1,0:T(8,128)S(1)} %get-tuple-element.54), channel_id=1, source_target_pairs={{0,32},{64,96},{128,160},{192,224},{32,0},{96,64},{160,128},{224,1... | collective-permute-start | bytes 983048 | tf_op jit(solution)/shard_map/ppermute | solution.py:678
  47.0 9.0 %collective-permute-start.7 = (f32[5,4,32,128]{3,2,1,0:T(8,128)S(1)}, f32[5,4,32,128]{3,2,1,0:T(8,128)S(1)}, u32[]{:S(2)}, u32[]{:S(2)}) collective-permute-start(f32[5,4,32,128]{3,2,1,0:T(8,128)S(1)} %get-tuple-element.55), channel_id=1, source_target_pairs={{32,64},{96,128},{160,192},{64,32},{128,96},{192,160},{33,65},{97,... | collective-permute-start | bytes 983048 | tf_op jit(solution)/shard_map/ppermute | solution.py:678
  97.7 4.6 %collective-permute-start.8 = (f32[4,5,48,128]{3,2,1,0:T(8,128)S(1)}, f32[4,5,48,128]{3,2,1,0:T(8,128)S(1)}, u32[]{:S(2)}, u32[]{:S(2)}) collective-permute-start(f32[4,5,48,128]{3,2,1,0:T(8,128)S(1)} %all_to_all.11.mine), channel_id=1, source_target_pairs={{0,32},{64,96},{128,160},{192,224},{32,0},{96,64},{160,128},{224,1... | collective-permute-start | bytes 1474568 | tf_op jit(solution)/shard_map/ppermute | solution.py:678

commit v5 on v4

--- a/solution.py
+++ b/solution.py
@@ -108,7 +108,7 @@
         inv[i] = jnp.where(inside(i), 1.0 / (total + 2.0 * BETA * level.scale), 0.0)
         return 0
 
-    lax.fori_loop(lo, hi, body, 0, unroll=2)
+    lax.fori_loop(lo, hi, body, 0, unroll=4)
 
 
 def begin(level, src, coef, state, direction, lo, hi):
@@ -122,7 +122,7 @@
             direction[c, i] = value
         return 0
 
-    lax.fori_loop(lo, hi, body, 0, unroll=2)
+    lax.fori_loop(lo, hi, body, 0, unroll=4)
     for c in range(3):
         ghosts(level, state, (c,))
 
@@ -190,7 +190,7 @@
 
 
 def mix(values, matrix):
-    return jnp.dot(values, matrix, precision=lax.Precision.HIGHEST, preferred_element_type=F32)
+    return jnp.dot(values, matrix, precision=lax.Precision.HIGH, preferred_element_type=F32)
 
 
 def pairs(ref, index, start, count):
@@ -304,58 +304,71 @@
     return inside
 
 
-def fine_inner(place, given, near_in, data, kept, s0, d0, t0, resid, near):
+def fine_take(data, message, low):
+    zero = jnp.zeros((32, LANES), F32)
+    for q, at, rows in MESSAGE:
+        start = 8 - rows if low else 24
+        data[q, start : start + rows] = message[at : at + rows]
+        if rows < 8:
+            data[q, 0 if low else 31] = zero
+
+
+def fine_pass(place, refs, pair, ranges, known):
+    data, kept, s0, d0, t0, resid, wide, saved = refs
     coef = [kept.at[j] for j in range(7)]
-    setup(FINE, lambda i: data[3, i], lambda i: data[4, i], coef, fine_inside(place), 9, 23)
-    begin(FINE, data, coef, s0, d0, 9, 23)
-    step(FINE, 1, data, coef, s0, t0, d0, 10, 22)
-    step(FINE, 2, data, coef, t0, s0, d0, 11, 21)
-    step(FINE, 3, data, coef, s0, t0, d0, 12, 20)
-    residual(FINE, data, coef, t0, resid, 13, 19)
-
-
-def fine_outer(place, near, far, *refs):
-    data, kept, s0, d0, t0, resid, saved, packed, first, second, sums = refs[6:]
-    coef = [kept.at[j] for j in range(7)]
-    zero = jnp.zeros((32, LANES), F32)
+    setup(FINE, lambda i: data[3, i], lambda i: data[4, i], coef, fine_inside(place), *ranges[0])
+    begin(FINE, data, coef, s0, d0, *ranges[0])
+    step(FINE, 1, data, coef, s0, t0, d0, *ranges[1])
+    step(FINE, 2, data, coef, t0, s0, d0, *ranges[2])
+    step(FINE, 3, data, coef, s0, t0, d0, *ranges[3])
+    lo, hi = ranges[3]
+    saved[:, lo - 4 : hi - 4] = t0[:, lo:hi, 4:28]
+    residual(FINE, data, coef, t0, resid, *ranges[4])
+    for q in range(5):
+        ref = resid if q < 3 else data
+        for t in known[q < 3]:
+            half, i = divmod(t, 8)
+            pair[t] = ref[q, 2 * t] + ref[q, 2 * t + 1]
+            wide[q, i, :, half * LANES : half * LANES + LANES] = pairs(pair, (t,), 0, 16)
+
+
+def fine_inner(place, given, near, *refs):
+    *refs, pair = refs
+    data, wide = refs[0], refs[6]
+    zero = jnp.zeros((16, LANES), F32)
 
     def act(even):
-        lo, hi = (far, near) if even else (near, far)
-        for q, at, rows in MESSAGE:
-            data[q, 8 - rows : 8] = lo[at : at + rows]
-            data[q, 24 : 24 + rows] = hi[at : at + rows]
-            if rows < 8:
-                data[q, 0] = zero
-                data[q, 31] = zero
+        fine_take(data, near, not even)
+        for q in range(3):
+            for t in (0, 1, 2, 13, 14, 15):
+                half, i = divmod(t, 8)
+                wide[q, i, :, half * LANES : half * LANES + LANES] = zero
+        if even:
+            ranges = ((9, 31), (10, 30), (11, 29), (12, 28), (13, 26))
+            known = (range(4, 16), range(7, 13))
+        else:
+            ranges = ((1, 23), (2, 22), (3, 21), (4, 20), (6, 19))
+            known = (range(0, 12), range(3, 9))
+        fine_pass(place, refs, pair, ranges, known)
 
     by_parity(place[0], act)
-    inside = fine_inside(place)
-    for lo, hi in ((1, 9), (23, 31)):
-        setup(FINE, lambda i: data[3, i], lambda i: data[4, i], coef, inside, lo, hi)
-        begin(FINE, data, coef, s0, d0, lo, hi)
-    for lo, hi in ((2, 10), (22, 30)):
-        step(FINE, 1, data, coef, s0, t0, d0, lo, hi)
-    for lo, hi in ((3, 11), (21, 29)):
-        step(FINE, 2, data, coef, t0, s0, d0, lo, hi)
-    for lo, hi in ((4, 12), (20, 28)):
-        step(FINE, 3, data, coef, s0, t0, d0, lo, hi)
-    saved[...] = t0[:, 4:28, 4:28]
-    residual(FINE, data, coef, t0, resid, 6, 13)
-    residual(FINE, data, coef, t0, resid, 19, 26)
-    pair = s0.at[0]
-    wide = sums
-    for q in range(5):
-        for t in range(16):
-            half, i = divmod(t, 8)
-            where = (q, i, slice(None), slice(half * LANES, half * LANES + LANES))
-            if q >= 3:
-                pair[t] = data[q, 2 * t] + data[q, 2 * t + 1]
-            elif 3 <= t <= 12:
-                pair[t] = resid[q, 2 * t] + resid[q, 2 * t + 1]
-            else:
-                wide[where] = jnp.zeros((16, LANES), F32)
-                continue
-            wide[where] = pairs(pair, (t,), 0, 16)
+
+
+def fine_outer(place, far, *refs):
+    *refs, packed, first, second, pair = refs[8:]
+    data, wide = refs[0], refs[6]
+
+    def act(even):
+        fine_take(data, far, even)
+        if even:
+            ranges = ((1, 9), (2, 10), (3, 11), (4, 12), (6, 13))
+            known = (range(0, 4), range(3, 7))
+        else:
+            ranges = ((23, 31), (22, 30), (21, 29), (20, 28), (19, 26))
+            known = (range(12, 16), range(9, 13))
+        fine_pass(place, refs, pair, ranges, known)
+
+    by_parity(place[0], act)
     matrix = pick(
         2 * LANES, LANES, lambda a, b: (a % LANES) // 2 + 64 * (a // LANES) == b, 0.125
     )
@@ -699,28 +712,20 @@
         name="join0",
     )
     far_in = swap(far, "grp", 1)
+    near_in = swap(near, "grp", 0)
     states = [FINE.shape(5), FINE.shape(7)] + [FINE.shape(3)] * 4
-    *inner, near = call(
-        fine_inner,
-        states + [(36, 32, 128)],
-        [],
+    states += [(5, 8, 16, 256), (3, 24, 24, 128)]
+    pair = [(16, 32, 128)]
+    inner = call(fine_inner, states, pair, place, data0, near_in, name="inner0", aliases={1: 0})
+    data0, kept0, _, _, _, _, _, saved0, packed1, first, second = call(
+        fine_outer,
+        states + [(5, 8, 16, 128)] + [(5, 8, 8, 128)] * 2,
+        pair,
         place,
-        data0,
-        near,
-        name="inner0",
-        aliases={1: 0, 2: 6},
-    )
-    near_in = swap(near, "grp", 0)
-    data0, kept0, _, _, _, _, saved0, packed1, first, second = call(
-        fine_outer,
-        states + [(3, 24, 24, 128), (5, 8, 16, 128)] + [(5, 8, 8, 128)] * 2,
-        [(5, 8, 16, 256)],
-        place,
-        near_in,
         far_in,
         *inner,
         name="outer0",
-        aliases={3 + j: j for j in range(6)},
+        aliases={2 + j: j for j in range(8)},
     )
     first = swap(first, "brick", 0)
     second = swap(second, "brick", 1)

time: 121 us -> 118 us (0.975)
  waiting for transfers between devices: 18.9 us -> 15.9 us
  Pallas kernels: 41.3 us -> 39.7 us
    ppermute x9, waiting for transfers between devices: 18.9 us -> 15.9 us  [swap(): return lax.ppermute(value, axis, ends + [(b, a) for a, b in ends])]
    pallas_call x9, Pallas kernels: 40.6 us -> 39 us  [call(): pl.pallas_call(kernel, out_shape=[jax.ShapeDtypeStruct(s, F32) for s in o...]
  transfers between devices with their start and end apart: 9 -> 9, of which waited for: 6 -> 6; matrix products, arithmetic and copies ran while one was open for 0% -> 0% of each run, Pallas kernels for 5% -> 7%
where the time goes in v5:
time: 118 us
  Pallas kernels  39.7 us (34%)
  blocking collectives  34.9 us (30%)
  starting transfers between devices  24.4 us (21%)
  waiting for transfers between devices  15.9 us (13%)
  local copies, waits for them, and re-layouts  2.89 us (2%)
    pallas_call x9, Pallas kernels, call(): pl.pallas_call(kernel, out_shape=[jax.ShapeDtypeStruct(s, F32) for s in o...  39 us
    ppermute x9, starting transfers between devices, swap(): return lax.ppermute(value, axis, ends + [(b, a) for a, b in ends])  24.4 us
    all_to_all x1, blocking collectives, on_device(): lax.all_to_all(jnp.broadcast_to(block[None], (bricks, 5, 4, 128)), 'brick...  21.1 us
    ppermute x9, waiting for transfers between devices, swap(): return lax.ppermute(value, axis, ends + [(b, a) for a, b in ends])  15.9 us
    all_to_all x1, blocking collectives, on_device(): lax.all_to_all(jnp.broadcast_to(column[None], (count // 2, 5, 48, 128)),...  13.8 us
    unnamed x6, local copies, waits for them, and re-layouts  2.8 us
  transfers between devices with their start and end apart: 9, of which 6 were waited for; matrix products, arithmetic and copies ran while one was open for 0% of the time, Pallas kernels for 7%

profile of v5, /device:TPU:33, one launch (start us, length us, event | category | flops | bytes accessed | tf_op | source)
XLA Modules:
  0.0 117.9 jit_solution(6322249922233025116)
XLA Ops:
  0.0 0.1 pad_add_fusion.place
  0.1 0.0 copy-start
  0.1 1.0 copy-done
  1.1 0.0 copy-start.1
  1.1 0.9 copy-done.1
  2.0 0.0 copy-start.2
  2.0 0.9 copy-done.2
  2.9 0.7 cut0.1
  3.6 0.1 collective-permute-start
  3.7 5.2 %collective-permute-start.1 = (f32[5,16,8,128]{3,2,1,0:T(8,128)S(1)}, f32[5,16,8,128]{3,2,1,0:T(8,128)S(1)}, u32[]{:S(2)}, u32[]{:S(2)}) collective-permute-start(f32[5,16,8,128]{3,2,1,0:T(8,128)S(1)} %get-tuple-element.37), channel_id=1, source_target_pairs={{1,2},{3,4},{5,6},{7,8},{9,10},{11,12},{13,14},{15,16},{17,18},{19... | collective-permute-start | bytes 983048 | tf_op jit(solution)/shard_map/ppermute | solution.py:691
  8.8 3.4 %collective-permute-done.first = f32[5,16,8,128]{3,2,1,0:T(8,128)S(1)} collective-permute-done((f32[5,16,8,128]{3,2,1,0:T(8,128)S(1)}, f32[5,16,8,128]{3,2,1,0:T(8,128)S(1)}, u32[]{:S(2)}, u32[]{:S(2)}) %collective-permute-start) | collective-permute-done | bytes 327712 | tf_op jit(solution)/shard_map/ppermute | solution.py:691
  12.2 3.7 %collective-permute-done.1.second = f32[5,16,8,128]{3,2,1,0:T(8,128)S(1)} collective-permute-done((f32[5,16,8,128]{3,2,1,0:T(8,128)S(1)}, f32[5,16,8,128]{3,2,1,0:T(8,128)S(1)}, u32[]{:S(2)}, u32[]{:S(2)}) %collective-permute-start.1) | collective-permute-done | bytes 327712 | tf_op jit(solution)/shard_map/ppermute | solution.py:691
  15.9 0.7 join0.1
  16.7 1.7 %collective-permute-start.3 = (f32[36,32,128]{2,1,0:T(8,128)S(1)}, f32[36,32,128]{2,1,0:T(8,128)S(1)}, u32[]{:S(2)}, u32[]{:S(2)}) collective-permute-start(f32[36,32,128]{2,1,0:T(8,128)S(1)} %get-tuple-element.40), channel_id=1, source_target_pairs={{0,32},{64,96},{128,160},{192,224},{32,0},{96,64},{160,128},{224,1... | collective-permute-start | bytes 1769480 | tf_op jit(solution)/shard_map/ppermute | solution.py:691
  18.3 3.1 %collective-permute-start.2 = (f32[36,32,128]{2,1,0:T(8,128)S(1)}, f32[36,32,128]{2,1,0:T(8,128)S(1)}, u32[]{:S(2)}, u32[]{:S(2)}) collective-permute-start(f32[36,32,128]{2,1,0:T(8,128)S(1)} %get-tuple-element.38), channel_id=1, source_target_pairs={{32,64},{96,128},{160,192},{64,32},{128,96},{192,160},{33,65},{97,... | collective-permute-start | bytes 1769480 | tf_op jit(solution)/shard_map/ppermute | solution.py:691
  21.4 0.0 collective-permute-done.3.near
  21.4 6.7 %inner0.1 = (f32[5,32,32,128]{3,2,1,0:T(8,128)S(1)}, f32[7,32,32,128]{3,2,1,0:T(8,128)S(1)}, f32[3,32,32,128]{3,2,1,0:T(8,128)S(1)}, f32[3,32,32,128]{3,2,1,0:T(...) custom-call(s32[4]{0:T(128)S(1)} %pad_add_fusion.place, ...), custom_call_target="tpu_custom_call", output_to_operand_aliasing={{0}: (1, {})} | custom-call | tf_op jit(solution)/shard_map/inner0/pallas_call | solution.py:206
  28.2 1.3 %collective-permute-done.2.far = f32[36,32,128]{2,1,0:T(8,128)S(1)} collective-permute-done((f32[36,32,128]{2,1,0:T(8,128)S(1)}, f32[36,32,128]{2,1,0:T(8,128)S(1)}, u32[]{:S(2)}, u32[]{:S(2)}) %collective-permute-start.2) | collective-permute-done | bytes 589856 | tf_op jit(solution)/shard_map/ppermute | solution.py:691
  29.5 4.0 %outer0.1 = (f32[5,32,32,128]{3,2,1,0:T(8,128)S(1)}, f32[7,32,32,128]{3,2,1,0:T(8,128)S(1)}, f32[3,32,32,128]{3,2,1,0:T(8,128)S(1)}, f32[3,32,32,128]{3,2,1,0:T(...) custom-call(s32[4]{0:T(128)S(1)} %pad_add_fusion.place, ...), custom_call_target="tpu_custom_call", output_to_operand_aliasing={{0}: (2, {}), {1}: (3, {}), {2}: (4, {}), {3}: (5, {}), {4}... | custom-call | tf_op jit(solution)/shard_map/outer0/pallas_call | solution.py:206
  33.5 0.1 collective-permute-start.4
  33.6 5.5 %collective-permute-start.5 = (f32[5,8,8,128]{3,2,1,0:T(8,128)S(1)}, f32[5,8,8,128]{3,2,1,0:T(8,128)S(1)}, u32[]{:S(2)}, u32[]{:S(2)}) collective-permute-start(f32[5,8,8,128]{3,2,1,0:T(8,128)S(1)} %get-tuple-element.51), channel_id=1, source_target_pairs={{1,2},{3,4},{5,6},{7,8},{9,10},{11,12},{13,14},{15,16},{17,18},{19... | collective-permute-start | bytes 491528 | tf_op jit(solution)/shard_map/ppermute | solution.py:691
  39.1 0.7 trim0.1
  39.8 0.0 collective-permute-done.4.first
  39.8 1.9 %collective-permute-done.5.second = f32[5,8,8,128]{3,2,1,0:T(8,128)S(1)} collective-permute-done((f32[5,8,8,128]{3,2,1,0:T(8,128)S(1)}, f32[5,8,8,128]{3,2,1,0:T(8,128)S(1)}, u32[]{:S(2)}, u32[]{:S(2)}) %collective-permute-start.5) | collective-permute-done | bytes 163872 | tf_op jit(solution)/shard_map/ppermute | solution.py:691
  41.8 0.8 cut1.1
  42.5 0.1 collective-permute-start.6
  42.6 5.5 %collective-permute-start.7 = (f32[5,4,32,128]{3,2,1,0:T(8,128)S(1)}, f32[5,4,32,128]{3,2,1,0:T(8,128)S(1)}, u32[]{:S(2)}, u32[]{:S(2)}) collective-permute-start(f32[5,4,32,128]{3,2,1,0:T(8,128)S(1)} %get-tuple-element.57), channel_id=1, source_target_pairs={{32,64},{96,128},{160,192},{64,32},{128,96},{192,160},{33,65},{97,... | collective-permute-start | bytes 983048 | tf_op jit(solution)/shard_map/ppermute | solution.py:691
  48.2 0.0 collective-permute-done.6.near
  48.2 4.7 %collective-permute-done.7.far = f32[5,4,32,128]{3,2,1,0:T(8,128)S(1)} collective-permute-done((f32[5,4,32,128]{3,2,1,0:T(8,128)S(1)}, f32[5,4,32,128]{3,2,1,0:T(8,128)S(1)}, u32[]{:S(2)}, u32[]{:S(2)}) %collective-permute-start.7) | collective-permute-done | bytes 327712 | tf_op jit(solution)/shard_map/ppermute | solution.py:691
  52.9 6.2 %down1.1 = (f32[5,16,32,128]{3,2,1,0:T(8,128)S(1)}, f32[3,16,32,128]{3,2,1,0:T(8,128)S(1)}, f32[5,16,128]{2,1,0:T(8,128)S(1)}, f32[7,16,32,128]{3,2,1,0:T(8,128)S(1)}) custom-call(s32[4]{0:T(128)S(1)} %pad_add_fusion.place, f32[5,8,32,128]{3,2,1,0:T(8,128)S(1)} %get-tuple-element.55.centre, f32[5,4,32,128]{3,2,1,0:T(8,128)S(1)} %collective-permute-done.6.near, ...), custom_call_target="tpu_custom_call" | custom-call | tf_op jit(solution)/shard_map/down1/pallas_call | solution.py:206
  59.2 21.1 %all_to_all.10.parts = f32[32,5,4,128]{3,2,1,0:T(4,128)S(1)} all-to-all(f32[32,5,4,128]{3,2,1,0:T(4,128)S(1)} %broadcast_in_dim.4), channel_id=1, replica_groups=mesh['grp'=8,'brick'=32] {'brick'}, dimensions={0} | all-to-all | bytes 655360 | tf_op jit(solution)/shard_map/all_to_all | solution.py:759
  80.3 0.6 column.1
  81.0 13.8 %all_to_all.11.mine = f32[4,5,48,128]{3,2,1,0:T(8,128)S(1)} all-to-all(f32[4,5,48,128]{3,2,1,0:T(8,128)S(1)} %broadcast_in_dim.5), channel_id=1, replica_groups={{0,64,128,192},{32,96,160,224},{1,65,129,193},{33,97,161,225},{2,66,130..., dimensions={0} | all-to-all | bytes 983040 | tf_op jit(solution)/shard_map/all_to_all | solution.py:761
  94.7 3.2 %collective-permute-start.8 = (f32[4,5,48,128]{3,2,1,0:T(8,128)S(1)}, f32[4,5,48,128]{3,2,1,0:T(8,128)S(1)}, u32[]{:S(2)}, u32[]{:S(2)}) collective-permute-start(f32[4,5,48,128]{3,2,1,0:T(8,128)S(1)} %all_to_all.11.mine), channel_id=1, source_target_pairs={{0,32},{64,96},{128,160},{192,224},{32,0},{96,64},{160,128},{224,1... | collective-permute-start | bytes 1474568 | tf_op jit(solution)/shard_map/ppermute | solution.py:691
  97.9 0.7 trim1.1
  98.6 0.8 collective-permute-done.8.other
  99.4 18.5 %climb.1 = f32[3,16,16,128]{3,2,1,0:T(8,128)} custom-call(s32[4]{0:T(128)S(1)} %pad_add_fusion.place, f32[4,5,48,128]{3,2,1,0:T(8,128)S(1)} %all_to_all.11.mine, f32[4,5,48,128]{3,2,1,0:T(8,128)S(1)} %collective-permute-done.8.other, f32[3,12,24,128]{3,2,1,0:T(8,128)S(1)} %get-tuple-element.62.data1, f32[3,12,24,128]{3,2,1,0:T(8,128)S(1)} %get-tuple-element.63.saved1, ...), custom_call_target="tpu_custom_call" | custom-call | tf_op jit(solution)/shard_map/climb/pallas_call | solution.py:206
  (3 shorter events, 0.1 us)
Async XLA Ops:
  0.1 1.0 copy-start
  1.1 0.9 copy-start.1
  2.0 0.9 copy-start.2
  3.6 8.7 %collective-permute-start = (f32[5,16,8,128]{3,2,1,0:T(8,128)S(1)}, f32[5,16,8,128]{3,2,1,0:T(8,128)S(1)}, u32[]{:S(2)}, u32[]{:S(2)}) collective-permute-start(f32[5,16,8,128]{3,2,1,0:T(8,128)S(1)} %get-tuple-element.36), channel_id=1, source_target_pairs={{0,1},{2,3},{4,5},{6,7},{8,9},{10,11},{12,13},{14,15},{16,17},{18,... | collective-permute-start | bytes 983048 | tf_op jit(solution)/shard_map/ppermute | solution.py:691
  3.7 12.2 %collective-permute-start.1 = (f32[5,16,8,128]{3,2,1,0:T(8,128)S(1)}, f32[5,16,8,128]{3,2,1,0:T(8,128)S(1)}, u32[]{:S(2)}, u32[]{:S(2)}) collective-permute-start(f32[5,16,8,128]{3,2,1,0:T(8,128)S(1)} %get-tuple-element.37), channel_id=1, source_target_pairs={{1,2},{3,4},{5,6},{7,8},{9,10},{11,12},{13,14},{15,16},{17,18},{19... | collective-permute-start | bytes 983048 | tf_op jit(solution)/shard_map/ppermute | solution.py:691
  16.7 4.8 %collective-permute-start.3 = (f32[36,32,128]{2,1,0:T(8,128)S(1)}, f32[36,32,128]{2,1,0:T(8,128)S(1)}, u32[]{:S(2)}, u32[]{:S(2)}) collective-permute-start(f32[36,32,128]{2,1,0:T(8,128)S(1)} %get-tuple-element.40), channel_id=1, source_target_pairs={{0,32},{64,96},{128,160},{192,224},{32,0},{96,64},{160,128},{224,1... | collective-permute-start | bytes 1769480 | tf_op jit(solution)/shard_map/ppermute | solution.py:691
  18.3 11.2 %collective-permute-start.2 = (f32[36,32,128]{2,1,0:T(8,128)S(1)}, f32[36,32,128]{2,1,0:T(8,128)S(1)}, u32[]{:S(2)}, u32[]{:S(2)}) collective-permute-start(f32[36,32,128]{2,1,0:T(8,128)S(1)} %get-tuple-element.38), channel_id=1, source_target_pairs={{32,64},{96,128},{160,192},{64,32},{128,96},{192,160},{33,65},{97,... | collective-permute-start | bytes 1769480 | tf_op jit(solution)/shard_map/ppermute | solution.py:691
  33.5 6.3 %collective-permute-start.4 = (f32[5,8,8,128]{3,2,1,0:T(8,128)S(1)}, f32[5,8,8,128]{3,2,1,0:T(8,128)S(1)}, u32[]{:S(2)}, u32[]{:S(2)}) collective-permute-start(f32[5,8,8,128]{3,2,1,0:T(8,128)S(1)} %get-tuple-element.50), channel_id=1, source_target_pairs={{0,1},{2,3},{4,5},{6,7},{8,9},{10,11},{12,13},{14,15},{16,17},{18,... | collective-permute-start | bytes 491528 | tf_op jit(solution)/shard_map/ppermute | solution.py:691
  33.6 8.2 %collective-permute-start.5 = (f32[5,8,8,128]{3,2,1,0:T(8,128)S(1)}, f32[5,8,8,128]{3,2,1,0:T(8,128)S(1)}, u32[]{:S(2)}, u32[]{:S(2)}) collective-permute-start(f32[5,8,8,128]{3,2,1,0:T(8,128)S(1)} %get-tuple-element.51), channel_id=1, source_target_pairs={{1,2},{3,4},{5,6},{7,8},{9,10},{11,12},{13,14},{15,16},{17,18},{19... | collective-permute-start | bytes 491528 | tf_op jit(solution)/shard_map/ppermute | solution.py:691
  42.5 5.6 %collective-permute-start.6 = (f32[5,4,32,128]{3,2,1,0:T(8,128)S(1)}, f32[5,4,32,128]{3,2,1,0:T(8,128)S(1)}, u32[]{:S(2)}, u32[]{:S(2)}) collective-permute-start(f32[5,4,32,128]{3,2,1,0:T(8,128)S(1)} %get-tuple-element.56), channel_id=1, source_target_pairs={{0,32},{64,96},{128,160},{192,224},{32,0},{96,64},{160,128},{224,1... | collective-permute-start | bytes 983048 | tf_op jit(solution)/shard_map/ppermute | solution.py:691
  42.6 10.3 %collective-permute-start.7 = (f32[5,4,32,128]{3,2,1,0:T(8,128)S(1)}, f32[5,4,32,128]{3,2,1,0:T(8,128)S(1)}, u32[]{:S(2)}, u32[]{:S(2)}) collective-permute-start(f32[5,4,32,128]{3,2,1,0:T(8,128)S(1)} %get-tuple-element.57), channel_id=1, source_target_pairs={{32,64},{96,128},{160,192},{64,32},{128,96},{192,160},{33,65},{97,... | collective-permute-start | bytes 983048 | tf_op jit(solution)/shard_map/ppermute | solution.py:691
  94.7 4.6 %collective-permute-start.8 = (f32[4,5,48,128]{3,2,1,0:T(8,128)S(1)}, f32[4,5,48,128]{3,2,1,0:T(8,128)S(1)}, u32[]{:S(2)}, u32[]{:S(2)}) collective-permute-start(f32[4,5,48,128]{3,2,1,0:T(8,128)S(1)} %all_to_all.11.mine), channel_id=1, source_target_pairs={{0,32},{64,96},{128,160},{192,224},{32,0},{96,64},{160,128},{224,1... | collective-permute-start | bytes 1474568 | tf_op jit(solution)/shard_map/ppermute | solution.py:691

commit v6 on v5

--- a/solution.py
+++ b/solution.py
@@ -108,7 +108,7 @@
         inv[i] = jnp.where(inside(i), 1.0 / (total + 2.0 * BETA * level.scale), 0.0)
         return 0
 
-    lax.fori_loop(lo, hi, body, 0, unroll=4)
+    lax.fori_loop(lo, hi, body, 0, unroll=8 if hi - lo == 8 else 7 if hi - lo == 14 else 4)
 
 
 def begin(level, src, coef, state, direction, lo, hi):
@@ -122,7 +122,7 @@
             direction[c, i] = value
         return 0
 
-    lax.fori_loop(lo, hi, body, 0, unroll=4)
+    lax.fori_loop(lo, hi, body, 0, unroll=8 if hi - lo == 8 else 7 if hi - lo == 14 else 4)
     for c in range(3):
         ghosts(level, state, (c,))
 

time: 118 us -> 118 us (level)
  no operation moved by 1% of the time
where the time goes in v6:
time: 118 us; the launch traced here: 117 us
  Pallas kernels  39.2 us (33%)
  blocking collectives  34.7 us (29%)
  starting transfers between devices  24.4 us (21%)
  waiting for transfers between devices  15.9 us (13%)
  local copies, waits for them, and re-layouts  2.89 us (2%)
    pallas_call x9, Pallas kernels, call(): pl.pallas_call(kernel, out_shape=[jax.ShapeDtypeStruct(s, F32) for s in o...  38.6 us
    ppermute x9, starting transfers between devices, swap(): return lax.ppermute(value, axis, ends + [(b, a) for a, b in ends])  24.4 us
    all_to_all x1, blocking collectives, on_device(): lax.all_to_all(jnp.broadcast_to(block[None], (bricks, 5, 4, 128)), 'brick...  20.9 us
    ppermute x9, waiting for transfers between devices, swap(): return lax.ppermute(value, axis, ends + [(b, a) for a, b in ends])  15.9 us
    all_to_all x1, blocking collectives, on_device(): lax.all_to_all(jnp.broadcast_to(column[None], (count // 2, 5, 48, 128)),...  13.7 us
    unnamed x6, local copies, waits for them, and re-layouts  2.8 us
  transfers between devices with their start and end apart: 9, of which 6 were waited for; matrix products, arithmetic and copies ran while one was open for 0% of the time, Pallas kernels for 7%

profile of v6, /device:TPU:33, one launch (start us, length us, event | category | flops | bytes accessed | tf_op | source)
XLA Modules:
  0.0 117.3 jit_solution(13149142523790322110)
XLA Ops:
  0.0 0.1 pad_add_fusion.place
  0.1 0.0 copy-start
  0.1 1.0 copy-done
  1.1 0.0 copy-start.1
  1.1 0.9 copy-done.1
  2.0 0.0 copy-start.2
  2.0 0.9 copy-done.2
  2.9 0.7 cut0.1
  3.6 0.1 collective-permute-start
  3.7 5.2 %collective-permute-start.1 = (f32[5,16,8,128]{3,2,1,0:T(8,128)S(1)}, f32[5,16,8,128]{3,2,1,0:T(8,128)S(1)}, u32[]{:S(2)}, u32[]{:S(2)}) collective-permute-start(f32[5,16,8,128]{3,2,1,0:T(8,128)S(1)} %get-tuple-element.37), channel_id=1, source_target_pairs={{1,2},{3,4},{5,6},{7,8},{9,10},{11,12},{13,14},{15,16},{17,18},{19... | collective-permute-start | bytes 983048 | tf_op jit(solution)/shard_map/ppermute | solution.py:691
  8.8 3.4 %collective-permute-done.first = f32[5,16,8,128]{3,2,1,0:T(8,128)S(1)} collective-permute-done((f32[5,16,8,128]{3,2,1,0:T(8,128)S(1)}, f32[5,16,8,128]{3,2,1,0:T(8,128)S(1)}, u32[]{:S(2)}, u32[]{:S(2)}) %collective-permute-start) | collective-permute-done | bytes 327712 | tf_op jit(solution)/shard_map/ppermute | solution.py:691
  12.2 3.7 %collective-permute-done.1.second = f32[5,16,8,128]{3,2,1,0:T(8,128)S(1)} collective-permute-done((f32[5,16,8,128]{3,2,1,0:T(8,128)S(1)}, f32[5,16,8,128]{3,2,1,0:T(8,128)S(1)}, u32[]{:S(2)}, u32[]{:S(2)}) %collective-permute-start.1) | collective-permute-done | bytes 327712 | tf_op jit(solution)/shard_map/ppermute | solution.py:691
  15.9 0.7 join0.1
  16.7 1.7 %collective-permute-start.3 = (f32[36,32,128]{2,1,0:T(8,128)S(1)}, f32[36,32,128]{2,1,0:T(8,128)S(1)}, u32[]{:S(2)}, u32[]{:S(2)}) collective-permute-start(f32[36,32,128]{2,1,0:T(8,128)S(1)} %get-tuple-element.40), channel_id=1, source_target_pairs={{0,32},{64,96},{128,160},{192,224},{32,0},{96,64},{160,128},{224,1... | collective-permute-start | bytes 1769480 | tf_op jit(solution)/shard_map/ppermute | solution.py:691
  18.3 3.1 %collective-permute-start.2 = (f32[36,32,128]{2,1,0:T(8,128)S(1)}, f32[36,32,128]{2,1,0:T(8,128)S(1)}, u32[]{:S(2)}, u32[]{:S(2)}) collective-permute-start(f32[36,32,128]{2,1,0:T(8,128)S(1)} %get-tuple-element.38), channel_id=1, source_target_pairs={{32,64},{96,128},{160,192},{64,32},{128,96},{192,160},{33,65},{97,... | collective-permute-start | bytes 1769480 | tf_op jit(solution)/shard_map/ppermute | solution.py:691
  21.4 0.0 collective-permute-done.3.near
  21.4 6.7 %inner0.1 = (f32[5,32,32,128]{3,2,1,0:T(8,128)S(1)}, f32[7,32,32,128]{3,2,1,0:T(8,128)S(1)}, f32[3,32,32,128]{3,2,1,0:T(8,128)S(1)}, f32[3,32,32,128]{3,2,1,0:T(...) custom-call(s32[4]{0:T(128)S(1)} %pad_add_fusion.place, ...), custom_call_target="tpu_custom_call", output_to_operand_aliasing={{0}: (1, {})} | custom-call | tf_op jit(solution)/shard_map/inner0/pallas_call | solution.py:206
  28.2 1.3 %collective-permute-done.2.far = f32[36,32,128]{2,1,0:T(8,128)S(1)} collective-permute-done((f32[36,32,128]{2,1,0:T(8,128)S(1)}, f32[36,32,128]{2,1,0:T(8,128)S(1)}, u32[]{:S(2)}, u32[]{:S(2)}) %collective-permute-start.2) | collective-permute-done | bytes 589856 | tf_op jit(solution)/shard_map/ppermute | solution.py:691
  29.5 3.7 %outer0.1 = (f32[5,32,32,128]{3,2,1,0:T(8,128)S(1)}, f32[7,32,32,128]{3,2,1,0:T(8,128)S(1)}, f32[3,32,32,128]{3,2,1,0:T(8,128)S(1)}, f32[3,32,32,128]{3,2,1,0:T(...) custom-call(s32[4]{0:T(128)S(1)} %pad_add_fusion.place, ...), custom_call_target="tpu_custom_call", output_to_operand_aliasing={{0}: (2, {}), {1}: (3, {}), {2}: (4, {}), {3}: (5, {}), {4}... | custom-call | tf_op jit(solution)/shard_map/outer0/pallas_call | solution.py:206
  33.2 0.1 collective-permute-start.4
  33.3 5.5 %collective-permute-start.5 = (f32[5,8,8,128]{3,2,1,0:T(8,128)S(1)}, f32[5,8,8,128]{3,2,1,0:T(8,128)S(1)}, u32[]{:S(2)}, u32[]{:S(2)}) collective-permute-start(f32[5,8,8,128]{3,2,1,0:T(8,128)S(1)} %get-tuple-element.51), channel_id=1, source_target_pairs={{1,2},{3,4},{5,6},{7,8},{9,10},{11,12},{13,14},{15,16},{17,18},{19... | collective-permute-start | bytes 491528 | tf_op jit(solution)/shard_map/ppermute | solution.py:691
  38.8 0.7 trim0.1
  39.6 0.0 collective-permute-done.4.first
  39.6 1.9 %collective-permute-done.5.second = f32[5,8,8,128]{3,2,1,0:T(8,128)S(1)} collective-permute-done((f32[5,8,8,128]{3,2,1,0:T(8,128)S(1)}, f32[5,8,8,128]{3,2,1,0:T(8,128)S(1)}, u32[]{:S(2)}, u32[]{:S(2)}) %collective-permute-start.5) | collective-permute-done | bytes 163872 | tf_op jit(solution)/shard_map/ppermute | solution.py:691
  41.5 0.8 cut1.1
  42.3 0.1 collective-permute-start.6
  42.4 5.5 %collective-permute-start.7 = (f32[5,4,32,128]{3,2,1,0:T(8,128)S(1)}, f32[5,4,32,128]{3,2,1,0:T(8,128)S(1)}, u32[]{:S(2)}, u32[]{:S(2)}) collective-permute-start(f32[5,4,32,128]{3,2,1,0:T(8,128)S(1)} %get-tuple-element.57), channel_id=1, source_target_pairs={{32,64},{96,128},{160,192},{64,32},{128,96},{192,160},{33,65},{97,... | collective-permute-start | bytes 983048 | tf_op jit(solution)/shard_map/ppermute | solution.py:691
  47.9 0.0 collective-permute-done.6.near
  47.9 4.7 %collective-permute-done.7.far = f32[5,4,32,128]{3,2,1,0:T(8,128)S(1)} collective-permute-done((f32[5,4,32,128]{3,2,1,0:T(8,128)S(1)}, f32[5,4,32,128]{3,2,1,0:T(8,128)S(1)}, u32[]{:S(2)}, u32[]{:S(2)}) %collective-permute-start.7) | collective-permute-done | bytes 327712 | tf_op jit(solution)/shard_map/ppermute | solution.py:691
  52.7 6.2 %down1.1 = (f32[5,16,32,128]{3,2,1,0:T(8,128)S(1)}, f32[3,16,32,128]{3,2,1,0:T(8,128)S(1)}, f32[5,16,128]{2,1,0:T(8,128)S(1)}, f32[7,16,32,128]{3,2,1,0:T(8,128)S(1)}) custom-call(s32[4]{0:T(128)S(1)} %pad_add_fusion.place, f32[5,8,32,128]{3,2,1,0:T(8,128)S(1)} %get-tuple-element.55.centre, f32[5,4,32,128]{3,2,1,0:T(8,128)S(1)} %collective-permute-done.6.near, ...), custom_call_target="tpu_custom_call" | custom-call | tf_op jit(solution)/shard_map/down1/pallas_call | solution.py:206
  58.9 20.9 %all_to_all.10.parts = f32[32,5,4,128]{3,2,1,0:T(4,128)S(1)} all-to-all(f32[32,5,4,128]{3,2,1,0:T(4,128)S(1)} %broadcast_in_dim.4), channel_id=1, replica_groups=mesh['grp'=8,'brick'=32] {'brick'}, dimensions={0} | all-to-all | bytes 655360 | tf_op jit(solution)/shard_map/all_to_all | solution.py:759
  79.8 0.6 column.1
  80.5 13.7 %all_to_all.11.mine = f32[4,5,48,128]{3,2,1,0:T(8,128)S(1)} all-to-all(f32[4,5,48,128]{3,2,1,0:T(8,128)S(1)} %broadcast_in_dim.5), channel_id=1, replica_groups={{0,64,128,192},{32,96,160,224},{1,65,129,193},{33,97,161,225},{2,66,130..., dimensions={0} | all-to-all | bytes 983040 | tf_op jit(solution)/shard_map/all_to_all | solution.py:761
  94.2 3.2 %collective-permute-start.8 = (f32[4,5,48,128]{3,2,1,0:T(8,128)S(1)}, f32[4,5,48,128]{3,2,1,0:T(8,128)S(1)}, u32[]{:S(2)}, u32[]{:S(2)}) collective-permute-start(f32[4,5,48,128]{3,2,1,0:T(8,128)S(1)} %all_to_all.11.mine), channel_id=1, source_target_pairs={{0,32},{64,96},{128,160},{192,224},{32,0},{96,64},{160,128},{224,1... | collective-permute-start | bytes 1474568 | tf_op jit(solution)/shard_map/ppermute | solution.py:691
  97.4 0.7 trim1.1
  98.1 0.8 collective-permute-done.8.other
  98.9 18.4 %climb.1 = f32[3,16,16,128]{3,2,1,0:T(8,128)} custom-call(s32[4]{0:T(128)S(1)} %pad_add_fusion.place, f32[4,5,48,128]{3,2,1,0:T(8,128)S(1)} %all_to_all.11.mine, f32[4,5,48,128]{3,2,1,0:T(8,128)S(1)} %collective-permute-done.8.other, f32[3,12,24,128]{3,2,1,0:T(8,128)S(1)} %get-tuple-element.62.data1, f32[3,12,24,128]{3,2,1,0:T(8,128)S(1)} %get-tuple-element.63.saved1, ...), custom_call_target="tpu_custom_call" | custom-call | tf_op jit(solution)/shard_map/climb/pallas_call | solution.py:206
  (3 shorter events, 0.1 us)
Async XLA Ops:
  0.1 1.0 copy-start
  1.1 0.9 copy-start.1
  2.0 0.9 copy-start.2
  3.6 8.7 %collective-permute-start = (f32[5,16,8,128]{3,2,1,0:T(8,128)S(1)}, f32[5,16,8,128]{3,2,1,0:T(8,128)S(1)}, u32[]{:S(2)}, u32[]{:S(2)}) collective-permute-start(f32[5,16,8,128]{3,2,1,0:T(8,128)S(1)} %get-tuple-element.36), channel_id=1, source_target_pairs={{0,1},{2,3},{4,5},{6,7},{8,9},{10,11},{12,13},{14,15},{16,17},{18,... | collective-permute-start | bytes 983048 | tf_op jit(solution)/shard_map/ppermute | solution.py:691
  3.7 12.2 %collective-permute-start.1 = (f32[5,16,8,128]{3,2,1,0:T(8,128)S(1)}, f32[5,16,8,128]{3,2,1,0:T(8,128)S(1)}, u32[]{:S(2)}, u32[]{:S(2)}) collective-permute-start(f32[5,16,8,128]{3,2,1,0:T(8,128)S(1)} %get-tuple-element.37), channel_id=1, source_target_pairs={{1,2},{3,4},{5,6},{7,8},{9,10},{11,12},{13,14},{15,16},{17,18},{19... | collective-permute-start | bytes 983048 | tf_op jit(solution)/shard_map/ppermute | solution.py:691
  16.7 4.8 %collective-permute-start.3 = (f32[36,32,128]{2,1,0:T(8,128)S(1)}, f32[36,32,128]{2,1,0:T(8,128)S(1)}, u32[]{:S(2)}, u32[]{:S(2)}) collective-permute-start(f32[36,32,128]{2,1,0:T(8,128)S(1)} %get-tuple-element.40), channel_id=1, source_target_pairs={{0,32},{64,96},{128,160},{192,224},{32,0},{96,64},{160,128},{224,1... | collective-permute-start | bytes 1769480 | tf_op jit(solution)/shard_map/ppermute | solution.py:691
  18.3 11.2 %collective-permute-start.2 = (f32[36,32,128]{2,1,0:T(8,128)S(1)}, f32[36,32,128]{2,1,0:T(8,128)S(1)}, u32[]{:S(2)}, u32[]{:S(2)}) collective-permute-start(f32[36,32,128]{2,1,0:T(8,128)S(1)} %get-tuple-element.38), channel_id=1, source_target_pairs={{32,64},{96,128},{160,192},{64,32},{128,96},{192,160},{33,65},{97,... | collective-permute-start | bytes 1769480 | tf_op jit(solution)/shard_map/ppermute | solution.py:691
  33.2 6.3 %collective-permute-start.4 = (f32[5,8,8,128]{3,2,1,0:T(8,128)S(1)}, f32[5,8,8,128]{3,2,1,0:T(8,128)S(1)}, u32[]{:S(2)}, u32[]{:S(2)}) collective-permute-start(f32[5,8,8,128]{3,2,1,0:T(8,128)S(1)} %get-tuple-element.50), channel_id=1, source_target_pairs={{0,1},{2,3},{4,5},{6,7},{8,9},{10,11},{12,13},{14,15},{16,17},{18,... | collective-permute-start | bytes 491528 | tf_op jit(solution)/shard_map/ppermute | solution.py:691
  33.3 8.2 %collective-permute-start.5 = (f32[5,8,8,128]{3,2,1,0:T(8,128)S(1)}, f32[5,8,8,128]{3,2,1,0:T(8,128)S(1)}, u32[]{:S(2)}, u32[]{:S(2)}) collective-permute-start(f32[5,8,8,128]{3,2,1,0:T(8,128)S(1)} %get-tuple-element.51), channel_id=1, source_target_pairs={{1,2},{3,4},{5,6},{7,8},{9,10},{11,12},{13,14},{15,16},{17,18},{19... | collective-permute-start | bytes 491528 | tf_op jit(solution)/shard_map/ppermute | solution.py:691
  42.3 5.6 %collective-permute-start.6 = (f32[5,4,32,128]{3,2,1,0:T(8,128)S(1)}, f32[5,4,32,128]{3,2,1,0:T(8,128)S(1)}, u32[]{:S(2)}, u32[]{:S(2)}) collective-permute-start(f32[5,4,32,128]{3,2,1,0:T(8,128)S(1)} %get-tuple-element.56), channel_id=1, source_target_pairs={{0,32},{64,96},{128,160},{192,224},{32,0},{96,64},{160,128},{224,1... | collective-permute-start | bytes 983048 | tf_op jit(solution)/shard_map/ppermute | solution.py:691
  42.4 10.3 %collective-permute-start.7 = (f32[5,4,32,128]{3,2,1,0:T(8,128)S(1)}, f32[5,4,32,128]{3,2,1,0:T(8,128)S(1)}, u32[]{:S(2)}, u32[]{:S(2)}) collective-permute-start(f32[5,4,32,128]{3,2,1,0:T(8,128)S(1)} %get-tuple-element.57), channel_id=1, source_target_pairs={{32,64},{96,128},{160,192},{64,32},{128,96},{192,160},{33,65},{97,... | collective-permute-start | bytes 983048 | tf_op jit(solution)/shard_map/ppermute | solution.py:691
  94.2 4.7 %collective-permute-start.8 = (f32[4,5,48,128]{3,2,1,0:T(8,128)S(1)}, f32[4,5,48,128]{3,2,1,0:T(8,128)S(1)}, u32[]{:S(2)}, u32[]{:S(2)}) collective-permute-start(f32[4,5,48,128]{3,2,1,0:T(8,128)S(1)} %all_to_all.11.mine), channel_id=1, source_target_pairs={{0,32},{64,96},{128,160},{192,224},{32,0},{96,64},{160,128},{224,1... | collective-permute-start | bytes 1474568 | tf_op jit(solution)/shard_map/ppermute | solution.py:691

commit v7 on v6

--- a/solution.py
+++ b/solution.py
@@ -84,10 +84,11 @@
     )
 
 
-def setup(level, stiff, react, coef, inside, lo, hi):
+def setup(level, data, coef, inside, state, direction, lo, hi):
     kx, ky, kym, kz, kzm, diag, inv = coef
     half = 0.5 * level.scale
     front, back = level.lanes()
+    stiff = lambda i: data[3, i]
     kx[lo - 1] = half * (stiff(lo - 1) + stiff(lo))
 
     def body(i, _):
@@ -98,26 +99,18 @@
         ym = behind_y(yp)
         zp = half * (centre + jnp.where(back, 0.0, ahead_z(centre)))
         zm = half * (centre + jnp.where(front, 0.0, behind_z(centre)))
-        total = ((xp + xm) + (yp + ym)) + (zp + zm) + react(i)
+        total = ((xp + xm) + (yp + ym)) + (zp + zm) + data[4, i]
         kx[i] = xp
         ky[i] = yp
         kym[i] = ym
         kz[i] = jnp.where(back, 0.0, zp)
         kzm[i] = jnp.where(front, 0.0, zm)
         diag[i] = total
-        inv[i] = jnp.where(inside(i), 1.0 / (total + 2.0 * BETA * level.scale), 0.0)
-        return 0
-
-    lax.fori_loop(lo, hi, body, 0, unroll=8 if hi - lo == 8 else 7 if hi - lo == 14 else 4)
-
-
-def begin(level, src, coef, state, direction, lo, hi):
-    inv = coef[6]
-
-    def body(i, _):
-        scaled = inv[i] * (1.0 / THETA)
+        inverse = jnp.where(inside(i), 1.0 / (total + 2.0 * BETA * level.scale), 0.0)
+        inv[i] = inverse
+        scaled = inverse * (1.0 / THETA)
         for c in range(3):
-            value = scaled * src[c, i]
+            value = scaled * data[c, i]
             state[c, i] = value
             direction[c, i] = value
         return 0
@@ -316,8 +309,7 @@
 def fine_pass(place, refs, pair, ranges, known):
     data, kept, s0, d0, t0, resid, wide, saved = refs
     coef = [kept.at[j] for j in range(7)]
-    setup(FINE, lambda i: data[3, i], lambda i: data[4, i], coef, fine_inside(place), *ranges[0])
-    begin(FINE, data, coef, s0, d0, *ranges[0])
+    setup(FINE, data, coef, fine_inside(place), s0, d0, *ranges[0])
     step(FINE, 1, data, coef, s0, t0, d0, *ranges[1])
     step(FINE, 2, data, coef, t0, s0, d0, *ranges[2])
     step(FINE, 3, data, coef, s0, t0, d0, *ranges[3])
@@ -472,8 +464,7 @@
         place[0],
         lambda even: middle_join(centre, *((far, near) if even else (near, far)), data),
     )
-    setup(MIDDLE, lambda i: data[3, i], lambda i: data[4, i], coef, middle_inside(place), 1, 15)
-    begin(MIDDLE, data, coef, s1, d1, 1, 15)
+    setup(MIDDLE, data, coef, middle_inside(place), s1, d1, 1, 15)
     step(MIDDLE, 1, data, coef, s1, t1, d1, 1, 15)
     step(MIDDLE, 2, data, coef, t1, s1, d1, 1, 15)
     step(MIDDLE, 3, data, coef, s1, saved, d1, 1, 15)
@@ -565,8 +556,7 @@
             ghosts(COARSE, data2, (q,))
 
     by_parity(place[0], act)
-    setup(COARSE, lambda i: data2[3, i], lambda i: data2[4, i], coef2, coarse_inside(place), 1, 9)
-    begin(COARSE, data2, coef2, s2, d2, 1, 9)
+    setup(COARSE, data2, coef2, coarse_inside(place), s2, d2, 1, 9)
     step(COARSE, 1, data2, coef2, s2, t2, d2, 1, 9)
     step(COARSE, 2, data2, coef2, t2, s2, d2, 1, 9)
     step(COARSE, 3, data2, coef2, s2, keep2, d2, 1, 9)
@@ -590,8 +580,7 @@
         for i in range(2):
             data3[q, i + 1] = shrunk[q, i]
         ghosts(LAST, data3, (q,))
-    setup(LAST, lambda i: data3[3, i], lambda i: data3[4, i], coef3, last_inside(place), 1, 3)
-    begin(LAST, data3, coef3, s3, d3, 1, 3)
+    setup(LAST, data3, coef3, last_inside(place), s3, d3, 1, 3)
     step(LAST, 1, data3, coef3, s3, t3, d3, 1, 3)
     step(LAST, 2, data3, coef3, t3, s3, d3, 1, 3)
     step(LAST, 3, data3, coef3, s3, t3, d3, 1, 3)

time: 118 us -> 118 us (level)
  no operation moved by 1% of the time
where the time goes in v7:
time: 118 us; the launch traced here: 117 us
  Pallas kernels  39 us (33%)
  blocking collectives  34.9 us (30%)
  starting transfers between devices  24.4 us (21%)
  waiting for transfers between devices  15.9 us (13%)
  local copies, waits for them, and re-layouts  2.89 us (2%)
    pallas_call x9, Pallas kernels, call(): pl.pallas_call(kernel, out_shape=[jax.ShapeDtypeStruct(s, F32) for s in o...  38.3 us
    ppermute x9, starting transfers between devices, swap(): return lax.ppermute(value, axis, ends + [(b, a) for a, b in ends])  24.4 us
    all_to_all x1, blocking collectives, on_device(): lax.all_to_all(jnp.broadcast_to(block[None], (bricks, 5, 4, 128)), 'brick...  21.1 us
    ppermute x9, waiting for transfers between devices, swap(): return lax.ppermute(value, axis, ends + [(b, a) for a, b in ends])  15.9 us
    all_to_all x1, blocking collectives, on_device(): lax.all_to_all(jnp.broadcast_to(column[None], (count // 2, 5, 48, 128)),...  13.8 us
    unnamed x6, local copies, waits for them, and re-layouts  2.8 us
  transfers between devices with their start and end apart: 9, of which 6 were waited for; matrix products, arithmetic and copies ran while one was open for 0% of the time, Pallas kernels for 7%

profile of v7, /device:TPU:33, one launch (start us, length us, event | category | flops | bytes accessed | tf_op | source)
XLA Modules:
  0.0 117.3 jit_solution(1822588984932850446)
XLA Ops:
  0.0 0.1 pad_add_fusion.place
  0.1 0.0 copy-start
  0.1 1.0 copy-done
  1.1 0.0 copy-start.1
  1.1 0.9 copy-done.1
  2.0 0.0 copy-start.2
  2.0 0.9 copy-done.2
  2.9 0.7 cut0.1
  3.6 0.1 collective-permute-start
  3.7 5.2 %collective-permute-start.1 = (f32[5,16,8,128]{3,2,1,0:T(8,128)S(1)}, f32[5,16,8,128]{3,2,1,0:T(8,128)S(1)}, u32[]{:S(2)}, u32[]{:S(2)}) collective-permute-start(f32[5,16,8,128]{3,2,1,0:T(8,128)S(1)} %get-tuple-element.37), channel_id=1, source_target_pairs={{1,2},{3,4},{5,6},{7,8},{9,10},{11,12},{13,14},{15,16},{17,18},{19... | collective-permute-start | bytes 983048 | tf_op jit(solution)/shard_map/ppermute | solution.py:680
  8.8 3.4 %collective-permute-done.first = f32[5,16,8,128]{3,2,1,0:T(8,128)S(1)} collective-permute-done((f32[5,16,8,128]{3,2,1,0:T(8,128)S(1)}, f32[5,16,8,128]{3,2,1,0:T(8,128)S(1)}, u32[]{:S(2)}, u32[]{:S(2)}) %collective-permute-start) | collective-permute-done | bytes 327712 | tf_op jit(solution)/shard_map/ppermute | solution.py:680
  12.2 3.7 %collective-permute-done.1.second = f32[5,16,8,128]{3,2,1,0:T(8,128)S(1)} collective-permute-done((f32[5,16,8,128]{3,2,1,0:T(8,128)S(1)}, f32[5,16,8,128]{3,2,1,0:T(8,128)S(1)}, u32[]{:S(2)}, u32[]{:S(2)}) %collective-permute-start.1) | collective-permute-done | bytes 327712 | tf_op jit(solution)/shard_map/ppermute | solution.py:680
  15.9 0.7 join0.1
  16.7 1.7 %collective-permute-start.3 = (f32[36,32,128]{2,1,0:T(8,128)S(1)}, f32[36,32,128]{2,1,0:T(8,128)S(1)}, u32[]{:S(2)}, u32[]{:S(2)}) collective-permute-start(f32[36,32,128]{2,1,0:T(8,128)S(1)} %get-tuple-element.40), channel_id=1, source_target_pairs={{0,32},{64,96},{128,160},{192,224},{32,0},{96,64},{160,128},{224,1... | collective-permute-start | bytes 1769480 | tf_op jit(solution)/shard_map/ppermute | solution.py:680
  18.3 3.1 %collective-permute-start.2 = (f32[36,32,128]{2,1,0:T(8,128)S(1)}, f32[36,32,128]{2,1,0:T(8,128)S(1)}, u32[]{:S(2)}, u32[]{:S(2)}) collective-permute-start(f32[36,32,128]{2,1,0:T(8,128)S(1)} %get-tuple-element.38), channel_id=1, source_target_pairs={{32,64},{96,128},{160,192},{64,32},{128,96},{192,160},{33,65},{97,... | collective-permute-start | bytes 1769480 | tf_op jit(solution)/shard_map/ppermute | solution.py:680
  21.4 0.0 collective-permute-done.3.near
  21.4 6.7 %inner0.1 = (f32[5,32,32,128]{3,2,1,0:T(8,128)S(1)}, f32[7,32,32,128]{3,2,1,0:T(8,128)S(1)}, f32[3,32,32,128]{3,2,1,0:T(8,128)S(1)}, f32[3,32,32,128]{3,2,1,0:T(...) custom-call(s32[4]{0:T(128)S(1)} %pad_add_fusion.place, ...), custom_call_target="tpu_custom_call", output_to_operand_aliasing={{0}: (1, {})} | custom-call | tf_op jit(solution)/shard_map/inner0/pallas_call | solution.py:199
  28.1 1.4 %collective-permute-done.2.far = f32[36,32,128]{2,1,0:T(8,128)S(1)} collective-permute-done((f32[36,32,128]{2,1,0:T(8,128)S(1)}, f32[36,32,128]{2,1,0:T(8,128)S(1)}, u32[]{:S(2)}, u32[]{:S(2)}) %collective-permute-start.2) | collective-permute-done | bytes 589856 | tf_op jit(solution)/shard_map/ppermute | solution.py:680
  29.5 3.7 %outer0.1 = (f32[5,32,32,128]{3,2,1,0:T(8,128)S(1)}, f32[7,32,32,128]{3,2,1,0:T(8,128)S(1)}, f32[3,32,32,128]{3,2,1,0:T(8,128)S(1)}, f32[3,32,32,128]{3,2,1,0:T(...) custom-call(s32[4]{0:T(128)S(1)} %pad_add_fusion.place, ...), custom_call_target="tpu_custom_call", output_to_operand_aliasing={{0}: (2, {}), {1}: (3, {}), {2}: (4, {}), {3}: (5, {}), {4}... | custom-call | tf_op jit(solution)/shard_map/outer0/pallas_call | solution.py:199
  33.2 0.1 collective-permute-start.4
  33.3 5.5 %collective-permute-start.5 = (f32[5,8,8,128]{3,2,1,0:T(8,128)S(1)}, f32[5,8,8,128]{3,2,1,0:T(8,128)S(1)}, u32[]{:S(2)}, u32[]{:S(2)}) collective-permute-start(f32[5,8,8,128]{3,2,1,0:T(8,128)S(1)} %get-tuple-element.51), channel_id=1, source_target_pairs={{1,2},{3,4},{5,6},{7,8},{9,10},{11,12},{13,14},{15,16},{17,18},{19... | collective-permute-start | bytes 491528 | tf_op jit(solution)/shard_map/ppermute | solution.py:680
  38.8 0.7 trim0.1
  39.6 0.0 collective-permute-done.4.first
  39.6 1.9 %collective-permute-done.5.second = f32[5,8,8,128]{3,2,1,0:T(8,128)S(1)} collective-permute-done((f32[5,8,8,128]{3,2,1,0:T(8,128)S(1)}, f32[5,8,8,128]{3,2,1,0:T(8,128)S(1)}, u32[]{:S(2)}, u32[]{:S(2)}) %collective-permute-start.5) | collective-permute-done | bytes 163872 | tf_op jit(solution)/shard_map/ppermute | solution.py:680
  41.5 0.8 cut1.1
  42.3 0.1 collective-permute-start.6
  42.4 5.5 %collective-permute-start.7 = (f32[5,4,32,128]{3,2,1,0:T(8,128)S(1)}, f32[5,4,32,128]{3,2,1,0:T(8,128)S(1)}, u32[]{:S(2)}, u32[]{:S(2)}) collective-permute-start(f32[5,4,32,128]{3,2,1,0:T(8,128)S(1)} %get-tuple-element.57), channel_id=1, source_target_pairs={{32,64},{96,128},{160,192},{64,32},{128,96},{192,160},{33,65},{97,... | collective-permute-start | bytes 983048 | tf_op jit(solution)/shard_map/ppermute | solution.py:680
  47.9 0.0 collective-permute-done.6.near
  47.9 4.7 %collective-permute-done.7.far = f32[5,4,32,128]{3,2,1,0:T(8,128)S(1)} collective-permute-done((f32[5,4,32,128]{3,2,1,0:T(8,128)S(1)}, f32[5,4,32,128]{3,2,1,0:T(8,128)S(1)}, u32[]{:S(2)}, u32[]{:S(2)}) %collective-permute-start.7) | collective-permute-done | bytes 327712 | tf_op jit(solution)/shard_map/ppermute | solution.py:680
  52.7 6.0 %down1.1 = (f32[5,16,32,128]{3,2,1,0:T(8,128)S(1)}, f32[3,16,32,128]{3,2,1,0:T(8,128)S(1)}, f32[5,16,128]{2,1,0:T(8,128)S(1)}, f32[7,16,32,128]{3,2,1,0:T(8,128)S(1)}) custom-call(s32[4]{0:T(128)S(1)} %pad_add_fusion.place, f32[5,8,32,128]{3,2,1,0:T(8,128)S(1)} %get-tuple-element.55.centre, f32[5,4,32,128]{3,2,1,0:T(8,128)S(1)} %collective-permute-done.6.near, ...), custom_call_target="tpu_custom_call" | custom-call | tf_op jit(solution)/shard_map/down1/pallas_call | solution.py:199
  58.7 21.1 %all_to_all.10.parts = f32[32,5,4,128]{3,2,1,0:T(4,128)S(1)} all-to-all(f32[32,5,4,128]{3,2,1,0:T(4,128)S(1)} %broadcast_in_dim.4), channel_id=1, replica_groups=mesh['grp'=8,'brick'=32] {'brick'}, dimensions={0} | all-to-all | bytes 655360 | tf_op jit(solution)/shard_map/all_to_all | solution.py:748
  79.8 0.6 column.1
  80.4 13.8 %all_to_all.11.mine = f32[4,5,48,128]{3,2,1,0:T(8,128)S(1)} all-to-all(f32[4,5,48,128]{3,2,1,0:T(8,128)S(1)} %broadcast_in_dim.5), channel_id=1, replica_groups={{0,64,128,192},{32,96,160,224},{1,65,129,193},{33,97,161,225},{2,66,130..., dimensions={0} | all-to-all | bytes 983040 | tf_op jit(solution)/shard_map/all_to_all | solution.py:750
  94.2 3.2 %collective-permute-start.8 = (f32[4,5,48,128]{3,2,1,0:T(8,128)S(1)}, f32[4,5,48,128]{3,2,1,0:T(8,128)S(1)}, u32[]{:S(2)}, u32[]{:S(2)}) collective-permute-start(f32[4,5,48,128]{3,2,1,0:T(8,128)S(1)} %all_to_all.11.mine), channel_id=1, source_target_pairs={{0,32},{64,96},{128,160},{192,224},{32,0},{96,64},{160,128},{224,1... | collective-permute-start | bytes 1474568 | tf_op jit(solution)/shard_map/ppermute | solution.py:680
  97.4 0.7 trim1.1
  98.1 0.8 collective-permute-done.8.other
  98.9 18.5 %climb.1 = f32[3,16,16,128]{3,2,1,0:T(8,128)} custom-call(s32[4]{0:T(128)S(1)} %pad_add_fusion.place, f32[4,5,48,128]{3,2,1,0:T(8,128)S(1)} %all_to_all.11.mine, f32[4,5,48,128]{3,2,1,0:T(8,128)S(1)} %collective-permute-done.8.other, f32[3,12,24,128]{3,2,1,0:T(8,128)S(1)} %get-tuple-element.62.data1, f32[3,12,24,128]{3,2,1,0:T(8,128)S(1)} %get-tuple-element.63.saved1, ...), custom_call_target="tpu_custom_call" | custom-call | tf_op jit(solution)/shard_map/climb/pallas_call | solution.py:199
  (3 shorter events, 0.1 us)
Async XLA Ops:
  0.1 1.0 copy-start
  1.1 0.9 copy-start.1
  2.0 0.9 copy-start.2
  3.6 8.7 %collective-permute-start = (f32[5,16,8,128]{3,2,1,0:T(8,128)S(1)}, f32[5,16,8,128]{3,2,1,0:T(8,128)S(1)}, u32[]{:S(2)}, u32[]{:S(2)}) collective-permute-start(f32[5,16,8,128]{3,2,1,0:T(8,128)S(1)} %get-tuple-element.36), channel_id=1, source_target_pairs={{0,1},{2,3},{4,5},{6,7},{8,9},{10,11},{12,13},{14,15},{16,17},{18,... | collective-permute-start | bytes 983048 | tf_op jit(solution)/shard_map/ppermute | solution.py:680
  3.7 12.2 %collective-permute-start.1 = (f32[5,16,8,128]{3,2,1,0:T(8,128)S(1)}, f32[5,16,8,128]{3,2,1,0:T(8,128)S(1)}, u32[]{:S(2)}, u32[]{:S(2)}) collective-permute-start(f32[5,16,8,128]{3,2,1,0:T(8,128)S(1)} %get-tuple-element.37), channel_id=1, source_target_pairs={{1,2},{3,4},{5,6},{7,8},{9,10},{11,12},{13,14},{15,16},{17,18},{19... | collective-permute-start | bytes 983048 | tf_op jit(solution)/shard_map/ppermute | solution.py:680
  16.7 4.8 %collective-permute-start.3 = (f32[36,32,128]{2,1,0:T(8,128)S(1)}, f32[36,32,128]{2,1,0:T(8,128)S(1)}, u32[]{:S(2)}, u32[]{:S(2)}) collective-permute-start(f32[36,32,128]{2,1,0:T(8,128)S(1)} %get-tuple-element.40), channel_id=1, source_target_pairs={{0,32},{64,96},{128,160},{192,224},{32,0},{96,64},{160,128},{224,1... | collective-permute-start | bytes 1769480 | tf_op jit(solution)/shard_map/ppermute | solution.py:680
  18.3 11.2 %collective-permute-start.2 = (f32[36,32,128]{2,1,0:T(8,128)S(1)}, f32[36,32,128]{2,1,0:T(8,128)S(1)}, u32[]{:S(2)}, u32[]{:S(2)}) collective-permute-start(f32[36,32,128]{2,1,0:T(8,128)S(1)} %get-tuple-element.38), channel_id=1, source_target_pairs={{32,64},{96,128},{160,192},{64,32},{128,96},{192,160},{33,65},{97,... | collective-permute-start | bytes 1769480 | tf_op jit(solution)/shard_map/ppermute | solution.py:680
  33.2 6.3 %collective-permute-start.4 = (f32[5,8,8,128]{3,2,1,0:T(8,128)S(1)}, f32[5,8,8,128]{3,2,1,0:T(8,128)S(1)}, u32[]{:S(2)}, u32[]{:S(2)}) collective-permute-start(f32[5,8,8,128]{3,2,1,0:T(8,128)S(1)} %get-tuple-element.50), channel_id=1, source_target_pairs={{0,1},{2,3},{4,5},{6,7},{8,9},{10,11},{12,13},{14,15},{16,17},{18,... | collective-permute-start | bytes 491528 | tf_op jit(solution)/shard_map/ppermute | solution.py:680
  33.3 8.2 %collective-permute-start.5 = (f32[5,8,8,128]{3,2,1,0:T(8,128)S(1)}, f32[5,8,8,128]{3,2,1,0:T(8,128)S(1)}, u32[]{:S(2)}, u32[]{:S(2)}) collective-permute-start(f32[5,8,8,128]{3,2,1,0:T(8,128)S(1)} %get-tuple-element.51), channel_id=1, source_target_pairs={{1,2},{3,4},{5,6},{7,8},{9,10},{11,12},{13,14},{15,16},{17,18},{19... | collective-permute-start | bytes 491528 | tf_op jit(solution)/shard_map/ppermute | solution.py:680
  42.3 5.6 %collective-permute-start.6 = (f32[5,4,32,128]{3,2,1,0:T(8,128)S(1)}, f32[5,4,32,128]{3,2,1,0:T(8,128)S(1)}, u32[]{:S(2)}, u32[]{:S(2)}) collective-permute-start(f32[5,4,32,128]{3,2,1,0:T(8,128)S(1)} %get-tuple-element.56), channel_id=1, source_target_pairs={{0,32},{64,96},{128,160},{192,224},{32,0},{96,64},{160,128},{224,1... | collective-permute-start | bytes 983048 | tf_op jit(solution)/shard_map/ppermute | solution.py:680
  42.4 10.3 %collective-permute-start.7 = (f32[5,4,32,128]{3,2,1,0:T(8,128)S(1)}, f32[5,4,32,128]{3,2,1,0:T(8,128)S(1)}, u32[]{:S(2)}, u32[]{:S(2)}) collective-permute-start(f32[5,4,32,128]{3,2,1,0:T(8,128)S(1)} %get-tuple-element.57), channel_id=1, source_target_pairs={{32,64},{96,128},{160,192},{64,32},{128,96},{192,160},{33,65},{97,... | collective-permute-start | bytes 983048 | tf_op jit(solution)/shard_map/ppermute | solution.py:680
  94.2 4.6 %collective-permute-start.8 = (f32[4,5,48,128]{3,2,1,0:T(8,128)S(1)}, f32[4,5,48,128]{3,2,1,0:T(8,128)S(1)}, u32[]{:S(2)}, u32[]{:S(2)}) collective-permute-start(f32[4,5,48,128]{3,2,1,0:T(8,128)S(1)} %all_to_all.11.mine), channel_id=1, source_target_pairs={{0,32},{64,96},{128,160},{192,224},{32,0},{96,64},{160,128},{224,1... | collective-permute-start | bytes 1474568 | tf_op jit(solution)/shard_map/ppermute | solution.py:680
